TPU v7x, 512 devices: a whole 4x8x8 slice. The times are simulated.
512 devices in a mesh: seq: 64 (over z, x, core), dp: 8 (over y).
Axes of the slice: x: 4, y: 8, z: 8, core: 2. Of those that a mesh axis runs over, the one named last changes fastest.
Arguments:
- tokens: bfloat16 [8, 16384, 256], P('dp', 'seq'), may hold values from -6 to 6
- occupancy: int32 [8, 16384], P('dp', 'seq'), may hold values 0 or 1
- counts: int32 [8, 64], P('dp', 'seq'), may hold values from 64 to 256, as said below
- queries: bfloat16 [512, 1024], replicated, may hold values from -6 to 6
- saved_lse: float32 [8, 512, 8], P('dp', 'seq'), as said below
- grad_out: bfloat16 [8, 512, 1024], P('dp', 'seq'), may hold values from -6 to 6
- attn_out: bfloat16 [8, 512, 1024], P('dp', 'seq'), may hold values from -6 to 6
- w_key: bfloat16 [256, 1024], replicated, may hold values from -0.375 to 0.375
- w_value: bfloat16 [256, 1024], replicated, may hold values from -0.375 to 0.375
Outputs:
- grad_tokens: bfloat16 [8, 16384, 256], P('dp', 'seq')
- grad_queries: float32 [512, 1024], P('seq')
- grad_w_key: float32 [256, 1024], replicated
- grad_w_value: float32 [256, 1024], replicated
Inputs may be any that keep to these rules, and one draw needn't show every extreme that they name: `counts`: each shard's count lies between 64 and 256; in every draw some shard is full. `saved_lse`: values lie near the logarithm of a window's number of occupied tokens.
All inputs are finite; a program needn't handle non-finite values. No bound on the sum of `occupancy` on one device may be relied on, other than what follows from the above.
Results may differ from a plain program's by a relative error of at most 0.0082.
The roundings to bfloat16 on the way count: a program that leaves them out, or rounds other values in their place, can miss the bound.
Values may be sent and summed in bfloat16 or wider, within the bound.
No kernel may reach another device: no remote copies, remote signals or barrier semaphores. Data moves between devices by JAX's collectives and lax.ppermute only.
A program may use at most 64 MiB of HBM per device.

v0:
```python
import math

import jax
import jax.numpy as jnp
from jax import lax
from jax.sharding import PartitionSpec as P


def layer_norm(tokens_f32):
    center = tokens_f32 - jnp.mean(tokens_f32, axis=-1, keepdims=True)
    inverse = lax.rsqrt(jnp.mean(center * center, axis=-1, keepdims=True) + 1e-05)
    return (center * inverse, inverse)


def split_heads(matrix, heads):
    return matrix.reshape(matrix.shape[0], heads, -1).transpose(1, 0, 2)


def join_heads(stacked):
    return stacked.transpose(1, 0, 2).reshape(stacked.shape[1], -1)


def head_sums(grad_rows, out_rows, heads):
    product = grad_rows.astype(jnp.float32) * out_rows.astype(jnp.float32)
    return jnp.sum(product.reshape(product.shape[0], heads, -1), axis=-1)


def head_backward(live_keys, scale_factor):

    def one_head(carry, items):
        query_head, key_head, value_head, grad_head, lse_head, delta_head = items
        scores = (
            lax.dot_general(
                query_head, key_head, (((1,), (1,)), ((), ())), preferred_element_type=jnp.float32
            )
            * scale_factor
        )
        probs = live_keys[None, :] * jnp.exp(scores - lse_head[:, None])
        probs_low = probs.astype(jnp.bfloat16)
        grad_value = lax.dot_general(
            probs_low, grad_head, (((0,), (0,)), ((), ())), preferred_element_type=jnp.float32
        ).astype(jnp.bfloat16)
        grad_probs = lax.dot_general(
            grad_head, value_head, (((1,), (1,)), ((), ())), preferred_element_type=jnp.float32
        )
        grad_scores = (scale_factor * probs * (grad_probs - delta_head[:, None])).astype(
            jnp.bfloat16
        )
        grad_query = jnp.dot(grad_scores, key_head, preferred_element_type=jnp.float32)
        grad_key = lax.dot_general(
            grad_scores, query_head, (((0,), (0,)), ((), ())), preferred_element_type=jnp.float32
        ).astype(jnp.bfloat16)
        return (carry, (grad_query, grad_key, grad_value))

    return one_head


def window_backward(
    tokens_window, live_keys, queries, lse_rows, delta_rows, grad_rows, w_key, w_value
):
    heads = lse_rows.shape[1]
    scale_factor = 1.0 / math.sqrt(queries.shape[1] // heads)
    normal_f32, inverse = layer_norm(tokens_window.astype(jnp.float32))
    normal_low = normal_f32.astype(jnp.bfloat16)
    key_rows = jnp.dot(normal_low, w_key, preferred_element_type=jnp.float32).astype(jnp.bfloat16)
    value_rows = jnp.dot(normal_low, w_value, preferred_element_type=jnp.float32).astype(
        jnp.bfloat16
    )
    items = (
        split_heads(queries, heads),
        split_heads(key_rows, heads),
        split_heads(value_rows, heads),
        split_heads(grad_rows, heads),
        lse_rows.T,
        delta_rows.T,
    )
    _, stacked = lax.scan(head_backward(live_keys, scale_factor), jnp.zeros((), jnp.float32), items)
    grad_query = join_heads(stacked[0])
    grad_keys = join_heads(stacked[1])
    grad_values = join_heads(stacked[2])
    grad_wkey = lax.dot_general(
        normal_low, grad_keys, (((0,), (0,)), ((), ())), preferred_element_type=jnp.float32
    )
    grad_wvalue = lax.dot_general(
        normal_low, grad_values, (((0,), (0,)), ((), ())), preferred_element_type=jnp.float32
    )
    grad_normal = lax.dot_general(
        grad_keys, w_key, (((1,), (1,)), ((), ())), preferred_element_type=jnp.float32
    )
    grad_normal = grad_normal + lax.dot_general(
        grad_values, w_value, (((1,), (1,)), ((), ())), preferred_element_type=jnp.float32
    )
    grad_input = inverse * (
        grad_normal
        - jnp.mean(grad_normal, axis=-1, keepdims=True)
        - normal_f32 * jnp.mean(grad_normal * normal_f32, axis=-1, keepdims=True)
    )
    return (grad_input.astype(jnp.bfloat16), grad_query, grad_wkey, grad_wvalue)


def body(tokens, occupancy, counts, queries, saved_lse, grad_out, attn_out, w_key, w_value):
    heads = saved_lse.shape[2]
    shard_tokens = tokens.shape[1]
    positions = jnp.arange(shard_tokens, dtype=jnp.int32)
    live_keys = jnp.where(positions < counts[0, 0], occupancy[0], 0).astype(jnp.float32)
    grad_all, out_all = (
        lax.all_gather(grad_out, "seq", axis=1, tiled=True),
        lax.all_gather(attn_out, "seq", axis=1, tiled=True),
    )
    lse_all = lax.all_gather(saved_lse, "seq", axis=1, tiled=True)
    delta_rows = head_sums(grad_all[0], out_all[0], heads)
    grad_input, grad_query, grad_wkey, grad_wvalue = window_backward(
        tokens[0], live_keys, queries, lse_all[0], delta_rows, grad_all[0], w_key, w_value
    )
    window_share = lax.psum_scatter(grad_query, "seq", scatter_dimension=0, tiled=True)
    query_share = lax.psum(window_share, "dp")
    key_total, value_total = lax.psum((grad_wkey, grad_wvalue), ("seq", "dp"))
    return (grad_input[None], query_share, key_total, value_total)


def solution(mesh):
    placed = (
        P("dp", "seq", None),
        P("dp", "seq"),
        P("dp", "seq"),
        P(),
        P("dp", "seq", None),
        P("dp", "seq", None),
        P("dp", "seq", None),
        P(),
        P(),
    )
    return jax.shard_map(
        body,
        mesh=mesh,
        in_specs=placed,
        out_specs=(P("dp", "seq", None), P("seq", None), P(), P()),
        check_vma=False,
    )
```

profile of v0, /device:TPU:1, one launch (start us, length us, event | category | flops | bytes accessed | tf_op | source)
XLA Modules:
  0.0 725.5 jit_solution(11828682885021193913)
XLA Ops:
  7.2 0.7 all-gather.3.cloned.1.call-update
  8.0 0.7 all-gather.5.cloned.1.call-update
  8.8 1.0 copy.32
  9.8 1.5 copy.33
  11.3 51.6 %all_gather.9 = f32[1,512,8]{2,0,1:T(1,128)S(1)} all-gather(f32[1,8,8]{2,0,1:T(1,128)S(1)} %bitcast.157), channel_id=1, replica_groups=mesh['seq'=64,'dp'=8] {'seq'}, dimensions={1}, use_global_device_ids=true | all-gather | bytes 16640 | tf_op jit(solution)/shard_map/all_gather | solution.py:110
  63.8 0.3 fusion.29
  64.2 0.3 fusion.30
  64.5 1.2 bitcast_bitcast_fusion
  65.8 34.0 %all-gather.3.cloned.1.call-done = bf16[1,512,1024]{2,1,0:T(8,128)(2,1)} async-done(((bf16[1,8,1024]{2,1,0:T(8,128)(2,1)}), bf16[1,512,1024]{2,1,0:T(8,128)(2,1)}) %all-gather.3.cloned.1.call-update) | async-done | bytes 1048592 | tf_op jit(solution)/shard_map/all_gather | solution.py:107
  99.8 1.5 copy.36
  101.3 81.6 %all-gather.5.cloned.1.call-done = bf16[1,512,1024]{2,1,0:T(8,128)(2,1)} async-done(((bf16[1,8,1024]{2,1,0:T(8,128)(2,1)}), bf16[1,512,1024]{2,1,0:T(8,128)(2,1)}) %all-gather.5.cloned.1.call-update) | async-done | bytes 1048592 | tf_op jit(solution)/shard_map/all_gather | solution.py:108
  182.9 2.3 copy.38
  185.2 1.5 fusion.28
  186.7 43.9 %while.14 = (s32[]{:T(128)}, f32[8,512,128]{2,1,0:T(8,128)}, bf16[8,256,128]{1,2,0:T(8,128)(2,1)}, bf16[8,256,128]{1,2,0:T(8,128)(2,1)}, f32[256]{0:T(256)S(1)},...) while((s32[]{:T(128)}, f32[8,512,128]{2,1,0:T(8,128)}, ...), condition=%wide.region_4.5_spmd, body=%wide.region_3.4_spmd.sunk | while | flops 168886272 | bytes 4014725 | solution.py:77
  186.8 1.1 fusion.91
  187.9 1.1 fusion.92
  189.0 1.8 fusion.93
  191.5 0.7 constant_dynamic-update-slice_fusion.3
  192.2 1.1 fusion.91
  193.4 1.1 fusion.92
  194.5 1.8 fusion.93
  197.0 0.7 constant_dynamic-update-slice_fusion.3
  197.7 1.1 fusion.91
  198.9 1.1 fusion.92
  200.0 1.8 fusion.93
  202.5 0.7 constant_dynamic-update-slice_fusion.3
  203.2 1.1 fusion.91
  204.3 1.1 fusion.92
  205.4 1.8 fusion.93
  207.2 0.3 fusion.95
  207.6 0.3 fusion.94
  208.0 0.7 constant_dynamic-update-slice_fusion.3
  208.7 1.1 fusion.91
  209.8 1.1 fusion.92
  210.9 1.8 fusion.93
  213.5 0.7 constant_dynamic-update-slice_fusion.3
  214.2 1.1 fusion.91
  215.3 1.1 fusion.92
  216.4 1.8 fusion.93
  218.6 0.3 fusion.94
  219.0 0.7 constant_dynamic-update-slice_fusion.3
  219.6 1.1 fusion.91
  220.8 1.1 fusion.92
  221.9 1.8 fusion.93
  223.7 0.3 fusion.95
  224.1 0.3 fusion.94
  224.5 0.7 constant_dynamic-update-slice_fusion.3
  225.1 1.1 fusion.91
  226.3 1.1 fusion.92
  227.4 1.8 fusion.93
  229.9 0.7 constant_dynamic-update-slice_fusion.3
  230.6 3.2 copy_bitcast_fusion
  233.9 1.4 dynamic-slice
  235.9 0.3 fusion.54
  236.2 1.3 fusion.48
  237.5 1.3 fusion.46
  238.8 0.3 fusion.53
  239.3 0.8 copy.45
  240.0 190.3 %all-reduce.5.cloned.1.call-done = f32[512,1024]{1,0:T(8,128)} async-done(((f32[512,1024]{1,0:T(8,128)}), f32[512,1024]{1,0:T(8,128)}) %all-reduce.5.cloned.1.call-update) | async-done | bytes 2097168
  430.4 0.8 constant_dynamic-slice_fusion.2
  431.1 23.6 %psum.21 = f32[8,1024]{1,0:T(8,128)} all-reduce(f32[8,1024]{1,0:T(8,128)S(1)} %constant_dynamic-slice_fusion.2), channel_id=1, replica_groups=mesh['seq'=64,'dp'=8] {'dp'}, use_global_device_ids=true, to_apply=%region_8.9 | all-reduce | flops 8192 | bytes 65536 | tf_op jit(solution)/shard_map/psum | solution.py:116
  454.7 260.9 %all-reduce.7.cloned.1.call-done = (f32[256,1024]{1,0:T(8,128)}, f32[256,1024]{1,0:T(8,128)}) async-done(((f32[256,1024]{1,0:T(8,128)}, f32[256,1024]{1,0:T(8,128)}), (f32[256,1024]{1,0:T(8,128)}, f32[256,1024]{1,0:T(8,128)})) %all-reduce.7.cloned.1.call-update) | async-done | bytes 2097168 | tf_op jit(solution)/shard_map/psum | solution.py:117
  715.6 2.4 copy.83
  718.0 1.0 copy.84
  (77 shorter events, 5.3 us)
Async XLA Ops:
  7.2 57.0 %copy-start = (bf16[256,1024]{1,0:T(8,128)(2,1)S(1)}, bf16[256,1024]{1,0:T(8,128)(2,1)}, u32[]{:S(2)}) copy-start(bf16[256,1024]{1,0:T(8,128)(2,1)} %param.19) | copy-start | bytes 1572868
  7.2 4.1 copy-start.6
  7.2 56.7 %copy-start.1 = (bf16[256,1024]{1,0:T(8,128)(2,1)S(1)}, bf16[256,1024]{1,0:T(8,128)(2,1)}, u32[]{:S(2)}) copy-start(bf16[256,1024]{1,0:T(8,128)(2,1)} %param.18) | copy-start | bytes 1572868
  7.2 92.6 %all-gather.3.cloned.1.call-start = ((), (), s32[]{:S(2)}) async-start(), calls=%async_computation | async-start | bytes 1064960 | tf_op jit(solution)/shard_map/all_gather | solution.py:107
  7.9 175.0 %all-gather.5.cloned.1.call-start = ((), (), s32[]{:S(2)}) async-start(), calls=%async_computation.1 | async-start | bytes 1064960 | tf_op jit(solution)/shard_map/all_gather | solution.py:108
  8.7 421.7 %all-reduce.5.cloned.1.call-start = ((), (), s32[]{:S(2)}) async-start(), calls=%async_computation.2 | async-start | bytes 4194304
  11.3 53.2 %copy-start.7 = (s32[1,256]{1,0:T(1,128)S(1)}, s32[1,256]{1,0:T(1,128)}, u32[]{:S(2)}) copy-start(s32[1,256]{1,0:T(1,128)} %param.12) | copy-start | bytes 3076
  233.8 2.1 copy-start.2
  233.8 2.1 copy-start.3
  233.8 3.7 copy-start.4
  233.8 481.8 %all-reduce.7.cloned.1.call-start = ((), (), s32[]{:S(2)}) async-start(), calls=%async_computation.3 | async-start | bytes 4194304 | tf_op jit(solution)/shard_map/psum | solution.py:117
  715.6 2.4 copy-start.5
Sparse Core Ops, SparseCore 0:
  11.4 88.3 all-gather.2
  103.2 79.7 all-gather.4
  233.9 196.3 all-reduce.4
  435.9 279.7 all-reduce.6
where the time goes:
time: 727 us; the launch traced here: 726 us
  waiting for transfers between devices  568 us (78%)
  blocking collectives  75.2 us (10%)
  matrix products  40.1 us (6%)
  local copies, waits for them, and re-layouts  24.3 us (3%)
  between operations  15.3 us (2%)
    psum x1, waiting for transfers between devices, body(): key_total, value_total = lax.psum((grad_wkey, grad_wvalue), ('seq', 'dp'))  261 us
    unnamed x5, waiting for transfers between devices  192 us
    all_gather x1, waiting for transfers between devices, body(): lax.all_gather(attn_out, 'seq', axis=1, tiled=True)  81.6 us
    all_gather x1, blocking collectives, body(): lse_all = lax.all_gather(saved_lse, 'seq', axis=1, tiled=True)  51.6 us
    all_gather x1, waiting for transfers between devices, body(): lax.all_gather(grad_out, 'seq', axis=1, tiled=True)  34 us
    psum x1, blocking collectives, body(): query_share = lax.psum(window_share, 'dp')  23.6 us
  transfers between devices with their start and end apart: 4, of which 4 were waited for; matrix products, arithmetic and copies ran while one was open for 2% of the time, Pallas kernels for 0%

commit v1 on v0

v1 whole, which is shorter than its diff:
```python
import math

import jax
import jax.numpy as jnp
from jax import lax
from jax.experimental import pallas as pl
from jax.experimental.pallas import tpu as pltpu
from jax.sharding import Mesh
from jax.sharding import PartitionSpec as P

HEAD = 128
EPS = 1e-05
LOG2E = math.log2(math.e)
PAD = 16
F32, BF16 = jnp.float32, jnp.bfloat16
VMEM = pl.BlockSpec(memory_space=pltpu.VMEM)
SMEM = pl.BlockSpec(memory_space=pltpu.SMEM)


def params(mib):
    return pltpu.CompilerParams(vmem_limit_bytes=mib * 1024 * 1024)


def mm(left, right, left_dim, right_dim):
    return lax.dot_general(
        left, right, (((left_dim,), (right_dim,)), ((), ())), preferred_element_type=F32
    )


def layer_norm(tokens):
    center = tokens - jnp.mean(tokens, axis=-1, keepdims=True)
    inverse = lax.rsqrt(jnp.mean(center * center, axis=-1, keepdims=True) + EPS)
    return center * inverse, inverse


def live_rows(occupancy, count, width):
    shard = occupancy.shape[1]
    place = lax.broadcasted_iota(jnp.int32, (1, shard), 1)
    live = jnp.where(place < count, occupancy, 0).astype(F32)
    return jnp.broadcast_to(live, (width, shard)).T


def three_parts(column):
    parts = []
    for _ in range(3):
        part = column.astype(BF16).astype(F32)
        parts.append(part)
        column = column - part
    return parts


def pack_kernel(counts, tokens, occupancy, grad, out, lse, sent):
    heads, (shard, width) = sent.shape[0], tokens.shape
    live = live_rows(occupancy[...], counts[0, 0], width)
    masked = jnp.where(live > 0.0, tokens[...].astype(F32), 0.0).astype(BF16)
    rows = grad.shape[0]
    lane = lax.broadcasted_iota(jnp.int32, (rows, HEAD), 1)
    for head in range(heads):
        sent[head, :shard, :] = masked
        cols = slice(head * HEAD, (head + 1) * HEAD)
        grad_f32 = grad[:, cols].astype(F32)
        delta = jnp.sum(grad_f32 * out[:, cols].astype(F32), axis=1, keepdims=True)
        extra = jnp.zeros((rows, HEAD), F32)
        for at, part in enumerate(three_parts(lse[:, head : head + 1]) + three_parts(delta)):
            extra = jnp.where(lane == at, part, extra)
        both = jnp.concatenate([grad_f32, extra], axis=1)
        both = jnp.concatenate([both, jnp.zeros((PAD - rows, 2 * HEAD), F32)], axis=0)
        sent[head, shard:, :] = both.astype(BF16)


def main_kernel(head, got, rows, query, w_key, w_value, back, parts, query_sum, weight_sum):
    del head
    blocks, shard = back.shape[0], back.shape[1]
    groups, part_rows = parts.shape[0], parts.shape[1]
    scale = 1.0 / math.sqrt(HEAD)
    grad = rows[:, :HEAD]
    extra = rows[:, HEAD:].astype(F32).T
    lse = (extra[0:1] + extra[1:2] + extra[2:3]) * LOG2E
    delta = extra[3:4] + extra[4:5] + extra[5:6]
    queries = query[...]
    weights = jnp.concatenate([w_key[...], w_value[...]], axis=1)
    for block in range(blocks):
        normal = layer_norm(got[block, :shard, :].astype(F32))[0].astype(BF16)
        both = jnp.dot(normal, weights, preferred_element_type=F32).astype(BF16)
        keys, values = both[:, :HEAD], both[:, HEAD:]
        probs = jnp.exp2(mm(keys, queries, 1, 1) * (scale * LOG2E) - lse)
        grad_values = jnp.dot(probs.astype(BF16), grad, preferred_element_type=F32)
        grad_probs = mm(values, grad, 1, 1)
        grad_scores = (scale * probs * (grad_probs - delta)).astype(BF16)
        grad_keys = jnp.dot(grad_scores, queries, preferred_element_type=F32)
        grad_both = jnp.concatenate([grad_keys, grad_values], axis=1).astype(BF16)
        back[block] = grad_both
        query_part = mm(keys, grad_scores, 0, 0)
        weight_part = mm(normal, grad_both, 0, 0)
        if block == 0:
            query_sum[...] = query_part
            weight_sum[...] = weight_part
        else:
            query_sum[...] += query_part
            weight_sum[...] += weight_part
    turned = query_sum[...].T.astype(BF16)
    totals = weight_sum[...].astype(BF16)
    each = weight_sum.shape[0] // groups
    half = part_rows - each
    for group in range(groups):
        parts[group, :each, :] = totals[group * each : (group + 1) * each, :]
        start = group * 2 * half
        parts[group, each:, :HEAD] = turned[start : start + half]
        parts[group, each:, HEAD:] = turned[start + half : start + 2 * half]


def add_up(got):
    total = got[0].astype(F32)
    for at in range(1, got.shape[0]):
        total = total + got[at].astype(F32)
    return total


def spread_kernel(got, sent):
    total = add_up(got).astype(BF16)
    for at in range(sent.shape[0]):
        sent[at] = total


def total_kernel(got, sent, query_rows):
    total = add_up(got)
    each = sent.shape[1]
    low = total[:each].astype(BF16)
    for at in range(sent.shape[0]):
        sent[at] = low
    query_rows[: got.shape[1] - each, :] = total[each:, :HEAD]
    query_rows[got.shape[1] - each :, :] = total[each:, HEAD:]


def gather_kernel(back, weights, query_rows, sent):
    blocks, shard = back.shape[0], back.shape[1]
    depth = weights.shape[0]
    rows = query_rows.shape[0] // blocks
    for block in range(blocks):
        sent[block, :shard, :] = back[block]
        sent[block, shard : shard + depth, :] = weights[...]
        piece = query_rows[block * rows : (block + 1) * rows, :]
        high = piece.astype(BF16).astype(F32)
        both = jnp.concatenate([high, piece - high], axis=1)
        both = jnp.concatenate([both, jnp.zeros((PAD - rows, 2 * HEAD), F32)], axis=0)
        sent[block, shard + depth :, :] = both.astype(BF16)


def finish_kernel(
    counts, got, tokens, occupancy, w_key, w_value, grad_tokens, query_rows, key_total, value_total
):
    heads, (shard, width) = got.shape[0], tokens.shape
    depth = key_total.shape[0]
    rows = query_rows.shape[0]
    normal, inverse = layer_norm(tokens[...].astype(F32))
    grad_normal = jnp.zeros((shard, width), F32)
    for head in range(heads):
        cols = slice(head * HEAD, (head + 1) * HEAD)
        weights = jnp.concatenate([w_key[:, cols], w_value[:, cols]], axis=1)
        grad_normal += mm(got[head, :shard, :], weights, 1, 1)
        both = got[head, shard : shard + depth, :].astype(F32)
        key_total[:, cols] = both[:, :HEAD]
        value_total[:, cols] = both[:, HEAD:]
        piece = got[head, shard + depth :, :].astype(F32)
        query_rows[:, cols] = (piece[:, :HEAD] + piece[:, HEAD:])[:rows]
    live = live_rows(occupancy[...], counts[0, 0], width)
    grad_normal = jnp.where(live > 0.0, grad_normal, 0.0)
    grad_input = inverse * (
        grad_normal
        - jnp.mean(grad_normal, axis=-1, keepdims=True)
        - normal * jnp.mean(grad_normal * normal, axis=-1, keepdims=True)
    )
    grad_tokens[...] = grad_input.astype(BF16)


def swap(array, axis):
    return lax.all_to_all(array, axis, 0, 0, tiled=True)


def shape(dims, dtype=BF16):
    return jax.ShapeDtypeStruct(dims, dtype)


def body(tokens, occupancy, counts, queries, saved_lse, grad_out, attn_out, w_key, w_value):
    tokens, grad, out, lse = tokens[0], grad_out[0], attn_out[0], saved_lse[0]
    heads, (shard, width) = lse.shape[1], tokens.shape
    latents, rows = queries.shape[0], grad.shape[0]
    groups = latents // (rows * heads)
    windows = lax.axis_size("y")
    sent = pl.pallas_call(
        pack_kernel,
        out_shape=shape((heads, shard + PAD, width)),
        in_specs=[SMEM] + [VMEM] * 5,
        out_specs=VMEM,
        compiler_params=params(16),
    )(counts, tokens, occupancy, grad, out, lse)
    got = swap(sent, "g")
    mine = got[:, shard : shard + rows, :].reshape(1, rows * heads, width)
    all_rows = swap(jnp.broadcast_to(mine, (groups, rows * heads, width)), "z")

    each, half = width // groups, rows * heads // 2
    head = lax.axis_index("g").reshape(1).astype(jnp.int32)
    whole3 = lambda at, head: (0, 0, 0)
    whole2 = lambda at, head: (0, 0)
    column = lambda at, head: (0, head[0])
    back, parts = pl.pallas_call(
        main_kernel,
        out_shape=(shape((heads, shard, width)), shape((groups, each + half, width))),
        grid_spec=pltpu.PrefetchScalarGridSpec(
            num_scalar_prefetch=1,
            grid=(1,),
            in_specs=[
                pl.BlockSpec(got.shape, whole3),
                pl.BlockSpec((latents, width), whole2),
                pl.BlockSpec((latents, HEAD), column),
                pl.BlockSpec((width, HEAD), column),
                pl.BlockSpec((width, HEAD), column),
            ],
            out_specs=[
                pl.BlockSpec((heads, shard, width), whole3),
                pl.BlockSpec((groups, each + half, width), whole3),
            ],
            scratch_shapes=[pltpu.VMEM((HEAD, latents), F32), pltpu.VMEM((width, width), F32)],
        ),
        compiler_params=params(40),
    )(head, got, all_rows.reshape(latents, width), queries, w_key, w_value)

    parts = swap(parts, "z")
    parts = pl.pallas_call(
        spread_kernel,
        out_shape=shape((windows, each + half, width)),
        in_specs=[VMEM],
        out_specs=VMEM,
        compiler_params=params(8),
    )(parts)
    parts = swap(parts, "y")
    weights, query_part = pl.pallas_call(
        total_kernel,
        out_shape=(shape((groups, each, width)), shape((2 * half, HEAD), F32)),
        in_specs=[VMEM],
        out_specs=(VMEM, VMEM),
        compiler_params=params(8),
    )(parts)
    weights = swap(weights, "z").reshape(width, width)
    sent = pl.pallas_call(
        gather_kernel,
        out_shape=shape((heads, shard + width + PAD, width)),
        in_specs=[VMEM] * 3,
        out_specs=VMEM,
        compiler_params=params(16),
    )(back, weights, query_part)
    got = swap(sent, "g")
    grad_tokens, query_rows, key_total, value_total = pl.pallas_call(
        finish_kernel,
        out_shape=(
            shape((shard, width)),
            shape((rows, heads * HEAD), F32),
            shape((width, heads * HEAD), F32),
            shape((width, heads * HEAD), F32),
        ),
        in_specs=[SMEM] + [VMEM] * 5,
        out_specs=(VMEM,) * 4,
        compiler_params=params(24),
    )(counts, got, tokens, occupancy, w_key, w_value)
    return grad_tokens[None], query_rows, key_total, value_total


def solution(mesh):
    seq, dp = mesh.shape["seq"], mesh.shape["dp"]
    split = Mesh(mesh.devices.reshape(seq // 8, 8, dp), ("z", "g", "y"))
    both = ("z", "g")
    rows = P("y", both, None)
    return jax.shard_map(
        body,
        mesh=split,
        in_specs=(rows, P("y", both), P("y", both), P(), rows, rows, rows, P(), P()),
        out_specs=(rows, P(both, None), P(), P()),
        check_vma=False,
    )
```

time: 727 us -> 131 us (0.18)
  waiting for transfers between devices: 568 us -> 10.2 us
  matrix products: 40.1 us -> 0 us
  blocking collectives: 75.2 us -> 99.9 us
  local copies, waits for them, and re-layouts: 24.3 us -> 4.45 us
  between operations: 15.3 us -> 1.35 us
  Pallas kernels: 0 us -> 8.42 us
    psum x1 -> x0, waiting for transfers between devices: 261 us -> none  [body(): key_total, value_total = lax.psum((grad_wkey, grad_wvalue), ('seq', 'dp'))]
    unnamed x5 -> x0, waiting for transfers between devices: 192 us -> none
    all_gather x2 -> x0, waiting for transfers between devices: 116 us -> none  [the longest x1 81.6 us: body(): lax.all_gather(attn_out, 'seq', axis=1, tiled=True)]
    all_to_all x0 -> x5, blocking collectives: none -> 99.9 us  [swap(): return lax.all_to_all(array, axis, 0, 0, tiled=True)]
    all_gather x1 -> x0, blocking collectives: 51.6 us -> none  [body(): lse_all = lax.all_gather(saved_lse, 'seq', axis=1, tiled=True)]
    dot_general x46 -> x0, matrix products: 40.1 us -> none  [the longest x8 14.2 us: one_head(): jnp.dot(grad_scores, key_head, preferred_element_type=jnp.float32)]
    psum x1 -> x0, blocking collectives: 23.6 us -> none  [body(): query_share = lax.psum(window_share, 'dp')]
    all_to_all x0 -> x1, waiting for transfers between devices: none -> 10.2 us  [swap(): return lax.all_to_all(array, axis, 0, 0, tiled=True)]
  transfers between devices with their start and end apart: 4 -> 1, of which waited for: 4 -> 1; matrix products, arithmetic and copies ran while one was open for 2% -> 0% of each run, Pallas kernels for 0% -> 0%
where the time goes in v1:
time: 131 us
  blocking collectives  99.9 us (76%)
  waiting for transfers between devices  10.2 us (8%)
  Pallas kernels  8.42 us (6%)
  starting transfers between devices  6.37 us (5%)
  local copies, waits for them, and re-layouts  4.45 us (3%)
  between operations  1.35 us (1%)
    all_to_all x5, blocking collectives, swap(): return lax.all_to_all(array, axis, 0, 0, tiled=True)  99.9 us
    all_to_all x1, waiting for transfers between devices, swap(): return lax.all_to_all(array, axis, 0, 0, tiled=True)  10.2 us
    all_to_all x1, starting transfers between devices, swap(): return lax.all_to_all(array, axis, 0, 0, tiled=True)  6.37 us
    pallas_call x1, Pallas kernels, body(): pl.pallas_call(main_kernel, out_shape=(shape((heads, shard, width)), shap...  5.98 us
    unnamed x20, local copies, waits for them, and re-layouts  3.73 us
  transfers between devices with their start and end apart: 1, of which 1 were waited for; matrix products, arithmetic and copies ran while one was open for 0% of the time, Pallas kernels for 0%

profile of v1, /device:TPU:1, one launch (start us, length us, event | category | flops | bytes accessed | tf_op | source)
XLA Modules:
  0.0 130.6 jit_solution(17517349035036197338)
XLA Ops:
  1.3 0.0 copy-start.3
  1.3 0.9 copy-done.3
  2.2 0.0 copy-start.5
  2.2 0.7 copy-done.5
  2.9 0.0 copy-start.6
  2.9 0.7 copy-done.6
  3.6 0.0 copy-start.7
  3.6 0.7 copy-done.7
  4.3 0.0 copy-start.8
  4.3 0.7 copy-done.8
  5.0 0.3 shard_map.120
  5.3 0.0 copy-start
  5.3 0.0 copy-start.1
  5.3 0.0 copy-start.2
  5.3 25.5 %all_to_all.30.got = bf16[8,272,256]{2,1,0:T(8,128)(2,1)S(1)} all-to-all(bf16[8,272,256]{2,1,0:T(8,128)(2,1)S(1)} %shard_map.120), channel_id=1, replica_groups=mesh['z'=8,'g'=8,'y'=8] {'g'}, dimensions={0} | all-to-all | bytes 2228224 | tf_op jit(solution)/shard_map/all_to_all | solution.py:177
  30.8 0.7 broadcast_in_dim.11
  31.5 6.4 %all-to-all-start.1 = ((bf16[8,64,256]{2,1,0:T(8,128)(2,1)}), bf16[8,64,256]{2,1,0:T(8,128)(2,1)S(1)}, u32[]{:S(2)}, u32[]{:S(2)}) async-start(bf16[8,64,256]{2,1,0:T(8,128)(2,1)} %broadcast_in_dim.11), calls=%async_computation.1 | async-start | bytes 524288 | tf_op jit(solution)/shard_map/all_to_all | solution.py:177
  37.8 10.2 %all-to-all-done.1 = bf16[8,64,256]{2,1,0:T(8,128)(2,1)S(1)} async-done(((bf16[8,64,256]{2,1,0:T(8,128)(2,1)}), bf16[8,64,256]{2,1,0:T(8,128)(2,1)S(1)}, u32[]{:S(2)}, u32[]{:S(2)}) %all-to-all-start.1) | async-done | bytes 262176 | tf_op jit(solution)/shard_map/all_to_all | solution.py:177
  48.0 0.0 copy-done
  48.0 0.0 copy-done.1
  48.0 0.0 copy-done.2
  48.0 6.0 %shard_map.121 = (bf16[8,256,256]{2,1,0:T(8,128)(2,1)S(1)}, bf16[8,64,256]{2,1,0:T(8,128)(2,1)S(1)}) custom-call(s32[1]{0:T(128)} %bitcast.head, bf16[8,272,256]{2,1,0:T(8,128)(2,1)S(1)} %all_to_all.30.got, bf16[512,256]{1,0:T(8,128)(2,1)S(1)} %bitcast.10, bf16[512,1024]{1,0:T(8,128)(2,1)S(1)} %copy-done.2, bf16[256,1024]{1,0:T(8,128)(2,1)S(1)} %copy-done, ...), custom_call_target="tpu_custom_call" | custom-call | tf_op jit(solution)/shard_map/pallas_call | solution.py:206
  54.0 12.1 %all_to_all.31.got = bf16[8,64,256]{2,1,0:T(8,128)(2,1)S(1)} all-to-all(bf16[8,64,256]{2,1,0:T(8,128)(2,1)S(1)} %get-tuple-element.13), channel_id=1, replica_groups=mesh['z'=8,'g'=8,'y'=8] {'z'}, dimensions={0} | all-to-all | bytes 524288 | tf_op jit(solution)/shard_map/all_to_all | solution.py:177
  66.1 16.1 %all_to_all.32.got = bf16[8,64,256]{2,1,0:T(8,128)(2,1)S(1)} all-to-all(bf16[8,64,256]{2,1,0:T(8,128)(2,1)S(1)} %shard_map.122), channel_id=1, replica_groups=mesh['z'=8,'g'=8,'y'=8] {'y'}, dimensions={0} | all-to-all | bytes 524288 | tf_op jit(solution)/shard_map/all_to_all | solution.py:177
  82.3 10.3 %all_to_all.33 = bf16[8,32,256]{2,1,0:T(8,128)(2,1)S(1)} all-to-all(bf16[8,32,256]{2,1,0:T(8,128)(2,1)S(1)} %get-tuple-element.14), channel_id=1, replica_groups=mesh['z'=8,'g'=8,'y'=8] {'z'}, dimensions={0} | all-to-all | bytes 262144 | tf_op jit(solution)/shard_map/all_to_all | solution.py:177
  92.6 0.1 shard_map.124
  92.7 0.0 copy-start.4
  92.7 0.0 copy-start.9
  92.7 35.9 %all_to_all.34.got = bf16[8,528,256]{2,1,0:T(8,128)(2,1)S(1)} all-to-all(bf16[8,528,256]{2,1,0:T(8,128)(2,1)S(1)} %shard_map.124), channel_id=1, replica_groups=mesh['z'=8,'g'=8,'y'=8] {'g'}, dimensions={0} | all-to-all | bytes 4325376 | tf_op jit(solution)/shard_map/all_to_all | solution.py:177
  128.7 0.0 copy-done.4
  128.7 0.0 copy-done.9
  128.7 2.0 %shard_map.125 = (bf16[256,256]{1,0:T(8,128)(2,1)}, f32[8,1024]{1,0:T(8,128)}, f32[256,1024]{1,0:T(8,128)}, f32[256,1024]{1,0:T(8,128)}) custom-call(s32[1,1]{1,0:T(1,128)S(6)} %copy.13.counts, bf16[8,528,256]{2,1,0:T(8,128)(2,1)S(1)} %all_to_all.34.got, bf16[256,256]{1,0:T(8,128)(2,1)S(1)} %bitcast.13, s32[1,256]{1,0:T(1,128)S(1)} %copy-done.9, ...), custom_call_target="tpu_custom_call" | custom-call | tf_op jit(solution)/shard_map/pallas_call | solution.py:253
  (3 shorter events, 0.1 us)
Async XLA Ops:
  1.3 0.9 copy-start.3
  2.2 0.7 copy-start.5
  2.9 0.7 copy-start.6
  3.6 0.7 copy-start.7
  4.3 0.7 copy-start.8
  5.3 42.8 %copy-start = (bf16[256,1024]{1,0:T(8,128)(2,1)S(1)}, bf16[256,1024]{1,0:T(8,128)(2,1)}, u32[]{:S(2)}) copy-start(bf16[256,1024]{1,0:T(8,128)(2,1)} %w_key.3) | copy-start | bytes 1572868
  5.3 42.8 %copy-start.1 = (bf16[256,1024]{1,0:T(8,128)(2,1)S(1)}, bf16[256,1024]{1,0:T(8,128)(2,1)}, u32[]{:S(2)}) copy-start(bf16[256,1024]{1,0:T(8,128)(2,1)} %w_value.3) | copy-start | bytes 1572868
  5.3 42.8 %copy-start.2 = (bf16[512,1024]{1,0:T(8,128)(2,1)S(1)}, bf16[512,1024]{1,0:T(8,128)(2,1)}, u32[]{:S(2)}) copy-start(bf16[512,1024]{1,0:T(8,128)(2,1)} %query.1) | copy-start | bytes 3145732
  31.5 16.6 %all-to-all-start.1 = ((bf16[8,64,256]{2,1,0:T(8,128)(2,1)}), bf16[8,64,256]{2,1,0:T(8,128)(2,1)S(1)}, u32[]{:S(2)}, u32[]{:S(2)}) async-start(bf16[8,64,256]{2,1,0:T(8,128)(2,1)} %broadcast_in_dim.11), calls=%async_computation.1 | async-start | bytes 524288 | tf_op jit(solution)/shard_map/all_to_all | solution.py:177
  92.7 36.0 %copy-start.4 = (bf16[1,256,256]{2,1,0:T(8,128)(2,1)S(1)}, bf16[1,256,256]{2,1,0:T(8,128)(2,1)}, u32[]{:S(2)}) copy-start(bf16[1,256,256]{2,1,0:T(8,128)(2,1)} %param.9) | copy-start | bytes 393220
  92.7 35.9 %copy-start.9 = (s32[1,256]{1,0:T(1,128)S(1)}, s32[1,256]{1,0:T(1,128)}, u32[]{:S(2)}) copy-start(s32[1,256]{1,0:T(1,128)} %occupancy.3) | copy-start | bytes 3076

commit v2 on v1

v2 whole, which is shorter than its diff:
```python
import math

import jax
import jax.numpy as jnp
from jax import lax
from jax.experimental import pallas as pl
from jax.experimental.pallas import tpu as pltpu
from jax.sharding import Mesh
from jax.sharding import PartitionSpec as P

HEAD = 128
EPS = 1e-05
LOG2E = math.log2(math.e)
F32, BF16 = jnp.float32, jnp.bfloat16
VMEM = pl.BlockSpec(memory_space=pltpu.VMEM)
SMEM = pl.BlockSpec(memory_space=pltpu.SMEM)


def params(mib):
    return pltpu.CompilerParams(vmem_limit_bytes=mib * 1024 * 1024)


def mm(left, right, left_dim, right_dim):
    return lax.dot_general(
        left, right, (((left_dim,), (right_dim,)), ((), ())), preferred_element_type=F32
    )


def layer_norm(tokens):
    center = tokens - jnp.mean(tokens, axis=-1, keepdims=True)
    inverse = lax.rsqrt(jnp.mean(center * center, axis=-1, keepdims=True) + EPS)
    return center * inverse, inverse


def live_rows(occupancy, count, width):
    shard = occupancy.shape[1]
    place = lax.broadcasted_iota(jnp.int32, (1, shard), 1)
    live = jnp.where(place < count, occupancy, 0).astype(F32)
    return jnp.broadcast_to(live, (width, shard)).T


def three_parts(column):
    parts = []
    for _ in range(3):
        part = column.astype(BF16).astype(F32)
        parts.append(part)
        column = column - part
    return parts


def pack_kernel(*refs):
    sources, sent, (counts, tokens, occupancy, grad, out, lse), done = (
        refs[:6],
        refs[6],
        refs[7:13],
        refs[13],
    )
    copies = [
        pltpu.make_async_copy(source, target, done.at[at])
        for at, (source, target) in enumerate(zip(sources, refs[7:13]))
    ]
    for copy in copies:
        copy.start()
    for copy in copies:
        copy.wait()
    chips, (shard, width) = sent.shape[0], tokens.shape
    live = live_rows(occupancy[...], counts[0, 0], width)
    masked = jnp.where(live > 0.0, tokens[...].astype(F32), 0.0).astype(BF16)
    rows = grad.shape[0]
    lane = lax.broadcasted_iota(jnp.int32, (rows, HEAD), 1)
    for chip in range(chips):
        sent[chip, :shard, :] = masked
        extras, grads = [], []
        for head in (2 * chip, 2 * chip + 1):
            cols = slice(head * HEAD, (head + 1) * HEAD)
            grad_f32 = grad[:, cols].astype(F32)
            delta = jnp.sum(grad_f32 * out[:, cols].astype(F32), axis=1, keepdims=True)
            extra = jnp.zeros((rows, HEAD), F32)
            for at, part in enumerate(three_parts(lse[:, head : head + 1]) + three_parts(delta)):
                extra = jnp.where(lane == at, part, extra)
            extras.append(extra)
            grads.append(grad_f32)
        both = jnp.concatenate(
            [jnp.concatenate(grads, axis=1), jnp.concatenate(extras, axis=1)], axis=0
        )
        sent[chip, shard:, :] = both.astype(BF16)


def turn_kernel(got, sent):
    chips, width = got.shape[0], got.shape[2]
    shard = got.shape[1] - sent.shape[1] // chips * 2
    pieces = [got[chip, shard:, :].astype(F32) for chip in range(chips)]
    rows = sent.shape[1] // chips
    grads = jnp.concatenate([piece[:rows] for piece in pieces], axis=0)
    extras = jnp.concatenate([piece[rows:] for piece in pieces], axis=0)
    for core in range(2):
        cols = slice(core * HEAD, (core + 1) * HEAD)
        both = jnp.concatenate([grads[:, cols], extras[:, cols]], axis=1).astype(BF16)
        for group in range(sent.shape[0] // 2):
            sent[2 * group + core] = both


def latent_order(got, chips):
    rows = got.shape[1] // chips
    blocks = [got[at].astype(F32) for at in range(got.shape[0])]
    return jnp.concatenate(
        [
            blocks[2 * group + core][chip * rows : (chip + 1) * rows]
            for group in range(got.shape[0] // 2)
            for chip in range(chips)
            for core in range(2)
        ],
        axis=0,
    )


def main_kernel(
    head, mine, other, got, query, w_key, w_value, keep, give, parts, query_sum, weight_sum
):
    del head
    chips, shard = keep.shape[0], keep.shape[1]
    groups, part_rows = parts.shape[0], parts.shape[1]
    scale = 1.0 / math.sqrt(HEAD)
    rows = latent_order(got, chips)
    grad = rows[:, :HEAD].astype(BF16)
    extra = rows[:, HEAD:].T
    lse = (extra[0:1] + extra[1:2] + extra[2:3]) * LOG2E
    delta = extra[3:4] + extra[4:5] + extra[5:6]
    queries = query[...]
    weights = jnp.concatenate([w_key[...], w_value[...]], axis=1)
    for block in range(2 * chips):
        source, target = (mine, keep) if block < chips else (other, give)
        chip = block % chips
        normal = layer_norm(source[chip, :shard, :].astype(F32))[0].astype(BF16)
        both = jnp.dot(normal, weights, preferred_element_type=F32).astype(BF16)
        keys, values = both[:, :HEAD], both[:, HEAD:]
        probs = jnp.exp2(mm(keys, queries, 1, 1) * (scale * LOG2E) - lse)
        grad_values = jnp.dot(probs.astype(BF16), grad, preferred_element_type=F32)
        grad_probs = mm(values, grad, 1, 1)
        grad_scores = (scale * probs * (grad_probs - delta)).astype(BF16)
        grad_keys = jnp.dot(grad_scores, queries, preferred_element_type=F32)
        grad_both = jnp.concatenate([grad_keys, grad_values], axis=1).astype(BF16)
        target[chip] = grad_both
        query_part = mm(keys, grad_scores, 0, 0)
        weight_part = mm(normal, grad_both, 0, 0)
        if block == 0:
            query_sum[...] = query_part
            weight_sum[...] = weight_part
        else:
            query_sum[...] += query_part
            weight_sum[...] += weight_part
    turned = query_sum[...].T.astype(BF16)
    totals = weight_sum[...].astype(BF16)
    each = weight_sum.shape[0] // groups
    half = part_rows - each
    for group in range(groups):
        parts[group, :each, :] = totals[group * each : (group + 1) * each, :]
        start = group * 2 * half
        parts[group, each:, :HEAD] = turned[start : start + half]
        parts[group, each:, HEAD:] = turned[start + half : start + 2 * half]


def add_up(got):
    total = got[0].astype(F32)
    for at in range(1, got.shape[0]):
        total = total + got[at].astype(F32)
    return total


def spread_kernel(got, sent):
    total = add_up(got).astype(BF16)
    for at in range(sent.shape[0]):
        sent[at] = total


def total_kernel(got, sent, query_rows):
    total = add_up(got)
    each = sent.shape[1]
    low = total[:each].astype(BF16)
    for at in range(sent.shape[0]):
        sent[at] = low
    query_rows[: got.shape[1] - each, :] = total[each:, :HEAD]
    query_rows[got.shape[1] - each :, :] = total[each:, HEAD:]


def gather_kernel(
    heads, keep, theirs, weights, query_rows, my_key, my_value, their_key, their_value, sent
):
    del heads
    chips, shard = keep.shape[0], keep.shape[1]
    depth = weights.shape[0]
    rows = query_rows.shape[0] // chips
    mine = jnp.concatenate([my_key[...], my_value[...]], axis=1)
    other = jnp.concatenate([their_key[...], their_value[...]], axis=1)
    for chip in range(chips):
        grad_normal = mm(keep[chip], mine, 1, 1) + mm(theirs[chip], other, 1, 1)
        sent[chip, :shard, :] = grad_normal.astype(BF16)
        sent[chip, shard : shard + depth, :] = weights[...]
        piece = query_rows[chip * rows : (chip + 1) * rows, :]
        high = piece.astype(BF16).astype(F32)
        sent[chip, shard + depth :, :] = jnp.concatenate([high, piece - high], axis=1).astype(BF16)


def tokens_kernel(counts, got, tokens, occupancy, grad_tokens):
    chips, (shard, width) = got.shape[0], tokens.shape
    normal, inverse = layer_norm(tokens[...].astype(F32))
    grad_normal = got[0, :shard, :].astype(F32)
    for chip in range(1, chips):
        grad_normal += got[chip, :shard, :].astype(F32)
    live = live_rows(occupancy[...], counts[0, 0], width)
    grad_normal = jnp.where(live > 0.0, grad_normal, 0.0)
    grad_input = inverse * (
        grad_normal
        - jnp.mean(grad_normal, axis=-1, keepdims=True)
        - normal * jnp.mean(grad_normal * normal, axis=-1, keepdims=True)
    )
    grad_tokens[...] = grad_input.astype(BF16)


def finish_kernel(core, got, other, query_rows, key_total, value_total):
    chips, depth, rows = got.shape[0], key_total.shape[0], query_rows.shape[0]
    shard = got.shape[1] - depth - 2 * rows

    def write(low, high):
        for chip in range(chips):
            for at, source in ((2 * chip, low), (2 * chip + 1, high)):
                cols = slice(at * HEAD, (at + 1) * HEAD)
                both = source[chip, shard : shard + depth, :].astype(F32)
                key_total[:, cols] = both[:, :HEAD]
                value_total[:, cols] = both[:, HEAD:]
                piece = source[chip, shard + depth :, :].astype(F32)
                both_rows = piece[:, :HEAD] + piece[:, HEAD:]
                query_rows[:, cols] = jnp.where(core[0] == 0, both_rows[:rows], both_rows[rows:])

    @pl.when(core[0] == 0)
    def _():
        write(got, other)

    @pl.when(core[0] != 0)
    def _():
        write(other, got)


def swap(array, axis):
    return lax.all_to_all(array, axis, 0, 0, tiled=True)


def shape(dims, dtype=BF16):
    return jax.ShapeDtypeStruct(dims, dtype)


def sibling(array):
    return lax.ppermute(array, "c", ((0, 1), (1, 0)))


def full(dims):
    return pl.BlockSpec(dims, lambda *_: (0,) * len(dims))


def column(dims, at):
    return pl.BlockSpec(dims, lambda step, heads: (0, heads[at]))


def body(tokens, occupancy, counts, queries, saved_lse, grad_out, attn_out, w_key, w_value):
    tokens, grad, out, lse = tokens[0], grad_out[0], attn_out[0], saved_lse[0]
    shard, width = tokens.shape
    latents, rows = queries.shape[0], grad.shape[0]
    chips, groups, windows = lax.axis_size("x"), lax.axis_size("z"), lax.axis_size("y")
    heads = lse.shape[1]
    core = lax.axis_index("c").astype(jnp.int32)
    head = 2 * lax.axis_index("x").astype(jnp.int32) + core
    head_pair = jnp.stack([head, head + 1 - 2 * core])
    core = core.reshape(1)
    tokens, head_pair, core = lax.optimization_barrier((tokens, head_pair, core))
    sent = pl.pallas_call(
        pack_kernel,
        out_shape=shape((chips, shard + 2 * rows, width)),
        in_specs=[pl.BlockSpec(memory_space=pltpu.HBM)] * 6,
        out_specs=VMEM,
        scratch_shapes=[pltpu.SMEM(counts.shape, counts.dtype)]
        + [pltpu.VMEM(ref.shape, ref.dtype) for ref in (tokens, occupancy, grad, out, lse)]
        + [pltpu.SemaphoreType.DMA((6,))],
        compiler_params=params(60),
    )(counts, tokens, occupancy, grad, out, lse)
    got = swap(sent, "x")
    other = sibling(got)
    grads = pl.pallas_call(
        turn_kernel,
        out_shape=shape((2 * groups, rows * chips, width)),
        in_specs=[VMEM],
        out_specs=VMEM,
        compiler_params=params(8),
    )(got)
    grads = swap(grads, ("z", "c"))

    each, half = width // groups, rows * heads // 2
    back = (chips, shard, width)
    part = (groups, each + half, width)
    keep, give, parts = pl.pallas_call(
        main_kernel,
        out_shape=(shape(back), shape(back), shape(part)),
        grid_spec=pltpu.PrefetchScalarGridSpec(
            num_scalar_prefetch=1,
            grid=(1,),
            in_specs=[
                full(got.shape),
                full(other.shape),
                full(grads.shape),
                column((latents, HEAD), 0),
                column((width, HEAD), 0),
                column((width, HEAD), 0),
            ],
            out_specs=[full(back), full(back), full(part)],
            scratch_shapes=[pltpu.VMEM((HEAD, latents), F32), pltpu.VMEM((width, width), F32)],
        ),
        compiler_params=params(40),
    )(head_pair, got, other, grads, queries, w_key, w_value)

    theirs, parts = lax.optimization_barrier((sibling(give), swap(parts, "z")))
    parts = pl.pallas_call(
        spread_kernel,
        out_shape=shape((windows, each + half, width)),
        in_specs=[VMEM],
        out_specs=VMEM,
        compiler_params=params(8),
    )(parts)
    parts = swap(parts, "y")
    weights, query_part = pl.pallas_call(
        total_kernel,
        out_shape=(shape((groups, each, width)), shape((2 * half, HEAD), F32)),
        in_specs=[VMEM],
        out_specs=(VMEM, VMEM),
        compiler_params=params(8),
    )(parts)
    weights = swap(weights, "z").reshape(width, width)
    last = (chips, shard + width + 2 * rows, width)
    sent = pl.pallas_call(
        gather_kernel,
        out_shape=shape(last),
        grid_spec=pltpu.PrefetchScalarGridSpec(
            num_scalar_prefetch=1,
            grid=(1,),
            in_specs=[full(back), full(back), full(weights.shape), full(query_part.shape)]
            + [column((width, HEAD), at) for at in (0, 0, 1, 1)],
            out_specs=full(last),
        ),
        compiler_params=params(20),
    )(head_pair, keep, theirs, weights, query_part, w_key, w_value, w_key, w_value)
    got = swap(sent, "x")
    other = sibling(got)
    grad_tokens = pl.pallas_call(
        tokens_kernel,
        out_shape=shape((shard, width)),
        in_specs=[SMEM] + [VMEM] * 3,
        out_specs=VMEM,
        compiler_params=params(16),
        cost_estimate=pl.CostEstimate(flops=2000000, bytes_accessed=1000000, transcendentals=256),
    )(counts, got, tokens, occupancy)
    query_rows, key_total, value_total = pl.pallas_call(
        finish_kernel,
        out_shape=(
            shape((rows, heads * HEAD), F32),
            shape((width, heads * HEAD), F32),
            shape((width, heads * HEAD), F32),
        ),
        in_specs=[SMEM] + [VMEM] * 2,
        out_specs=(VMEM,) * 3,
        compiler_params=params(16),
    )(core, got, other)
    return grad_tokens[None], query_rows, key_total, value_total


def solution(mesh):
    seq, dp = mesh.shape["seq"], mesh.shape["dp"]
    split = Mesh(mesh.devices.reshape(seq // 8, 4, 2, dp), ("z", "x", "c", "y"))
    both = ("z", "x", "c")
    rows = P("y", both, None)
    return jax.shard_map(
        body,
        mesh=split,
        in_specs=(rows, P("y", both), P("y", both), P(), rows, rows, rows, P(), P()),
        out_specs=(rows, P(both, None), P(), P()),
        check_vma=False,
    )
```

time: 131 us -> 120 us (0.916)
  blocking collectives: 99.9 us -> 86.9 us
  starting transfers between devices: 6.37 us -> 17.2 us
  waiting for transfers between devices: 10.2 us -> 1.28 us
  local copies, waits for them, and re-layouts: 4.45 us -> 0.03 us
  Pallas kernels: 8.42 us -> 12.3 us
    ppermute x0 -> x3, starting transfers between devices: none -> 17.2 us  [sibling(): return lax.ppermute(array, 'c', ((0, 1), (1, 0)))]
    all_to_all x5 -> x6, blocking collectives: 99.9 us -> 86.9 us  [swap(): return lax.all_to_all(array, axis, 0, 0, tiled=True)]
    all_to_all x1 -> x0, waiting for transfers between devices: 10.2 us -> none  [swap(): return lax.all_to_all(array, axis, 0, 0, tiled=True)]
    all_to_all x1 -> x0, starting transfers between devices: 6.37 us -> none  [swap(): return lax.all_to_all(array, axis, 0, 0, tiled=True)]
    pallas_call x4 -> x6, Pallas kernels: 8.35 us -> 12.2 us  [the longest x1 6.52 us: body(): pl.pallas_call(main_kernel, out_shape=(shape(back), shape(back), shape(pa...]
    unnamed x20 -> x10, local copies, waits for them, and re-layouts: 3.73 us -> 0.03 us
  transfers between devices with their start and end apart: 1 -> 3, of which waited for: 1 -> 1; matrix products, arithmetic and copies ran while one was open for 0% -> 0% of each run, Pallas kernels for 0% -> 1%
where the time goes in v2:
time: 120 us; the launch traced here: 119 us
  blocking collectives  86.9 us (72%)
  starting transfers between devices  17.2 us (14%)
  Pallas kernels  12.3 us (10%)
  between operations  1.42 us (1%)
  waiting for transfers between devices  1.28 us (1%)
    all_to_all x6, blocking collectives, swap(): return lax.all_to_all(array, axis, 0, 0, tiled=True)  86.9 us
    ppermute x3, starting transfers between devices, sibling(): return lax.ppermute(array, 'c', ((0, 1), (1, 0)))  17.2 us
    pallas_call x1, Pallas kernels, body(): pl.pallas_call(main_kernel, out_shape=(shape(back), shape(back), shape(pa...  6.52 us
  transfers between devices with their start and end apart: 3, of which 1 were waited for; matrix products, arithmetic and copies ran while one was open for 0% of the time, Pallas kernels for 1%

profile of v2, /device:TPU:1, one launch (start us, length us, event | category | flops | bytes accessed | tf_op | source)
XLA Modules:
  0.0 119.2 jit_solution(18252044126792319653)
XLA Ops:
  0.6 0.1 pad_add_fusion.head.heads
  1.4 2.0 %shard_map.120 = bf16[4,272,256]{2,1,0:T(8,128)(2,1)} custom-call(s32[1,1]{1,0:T(1,128)S(6)} %copy.13.refs_0_.counts, bf16[256,256]{1,0:T(8,128)(2,1)} %bitcast.10, s32[1,256]{1,0:T(1,128)} %occupancy.1, bf16[8,1024]{1,0:T(8,128)(2,1)} %bitcast.13, bf16[8,1024]{1,0:T(8,128)(2,1)} %bitcast.14, f32[8,8]{1,0:T(8,128)} %bitcast.15), custom_call_target="tpu_custom_call" | custom-call | tf_op jit(solution)/shard_map/pallas_call | solution.py:275
  3.4 0.0 copy-start
  3.4 0.0 copy-start.1
  3.4 0.0 copy-start.2
  3.5 12.1 %all_to_all.30.got.mine = bf16[4,272,256]{2,1,0:T(8,128)(2,1)S(1)} all-to-all(bf16[4,272,256]{2,1,0:T(8,128)(2,1)} %shard_map.120), channel_id=1, replica_groups=mesh['z'=8,'x'=4,'c'=2,'y'=8] {'x'}, dimensions={0} | all-to-all | bytes 1114112 | tf_op jit(solution)/shard_map/all_to_all | solution.py:245
  15.5 8.5 %collective-permute-start = (bf16[4,272,256]{2,1,0:T(8,128)(2,1)S(1)}, bf16[4,272,256]{2,1,0:T(8,128)(2,1)S(1)}, u32[]{:S(2)}, u32[]{:S(2)}) collective-permute-start(bf16[4,272,256]{2,1,0:T(8,128)(2,1)S(1)} %all_to_all.30.got.mine), channel_id=1, source_target_pairs={{0,8},{8,0},{1,9},{9,1},{2,10},{10,2},{3,11},{11,3},{4,12},{12,4},... | collective-permute-start | bytes 1671176 | tf_op jit(solution)/shard_map/ppermute | solution.py:253
  24.1 19.0 %all_to_all.31.got = bf16[16,32,256]{2,1,0:T(8,128)(2,1)S(1)} all-to-all(bf16[16,32,256]{2,1,0:T(8,128)(2,1)S(1)} %shard_map.121), channel_id=1, replica_groups=mesh['z'=8,'x'=4,'c'=2,'y'=8] {'z','c'}, dimensions={0} | all-to-all | bytes 524288 | tf_op jit(solution)/shard_map/all_to_all | solution.py:245
  43.1 0.0 collective-permute-done.other
  43.1 0.0 copy-done
  43.1 0.0 copy-done.1
  43.1 0.0 copy-done.2
  43.1 6.5 %shard_map.122 = (bf16[4,256,256]{2,1,0:T(8,128)(2,1)S(1)}, bf16[4,256,256]{2,1,0:T(8,128)(2,1)S(1)}, bf16[8,64,256]{2,1,0:T(8,128)(2,1)S(1)}) custom-call(s32[2]{0:T(128)S(1)} %pad_add_fusion.head.heads, bf16[4,272,256]{2,1,0:T(8,128)(2,1)S(1)} %all_to_all.30.got.mine, bf16[4,272,256]{2,1,0:T(8,128)(2,1)S(1)} %collective-permute-done.other, ...), custom_call_target="tpu_custom_call" | custom-call | tf_op jit(solution)/shard_map/pallas_call | solution.py:299
  49.6 1.9 %collective-permute-start.1 = (bf16[4,256,256]{2,1,0:T(8,128)(2,1)S(1)}, bf16[4,256,256]{2,1,0:T(8,128)(2,1)S(1)}, u32[]{:S(2)}, u32[]{:S(2)}) collective-permute-start(bf16[4,256,256]{2,1,0:T(8,128)(2,1)S(1)} %get-tuple-element.20), channel_id=1, source_target_pairs={{0,8},{8,0},{1,9},{9,1},{2,10},{10,2},{3,11},{11,3},{4,12},{12,4},... | collective-permute-start | bytes 1572872 | tf_op jit(solution)/shard_map/ppermute | solution.py:253
  51.6 14.6 %all_to_all.32.got = bf16[8,64,256]{2,1,0:T(8,128)(2,1)S(1)} all-to-all(bf16[8,64,256]{2,1,0:T(8,128)(2,1)S(1)} %get-tuple-element.21), channel_id=1, replica_groups=mesh['z'=8,'x'=4,'c'=2,'y'=8] {'z'}, dimensions={0} | all-to-all | bytes 524288 | tf_op jit(solution)/shard_map/all_to_all | solution.py:245
  66.2 0.0 collective-permute-done.1.theirs
  66.3 16.7 %all_to_all.33.got = bf16[8,64,256]{2,1,0:T(8,128)(2,1)S(1)} all-to-all(bf16[8,64,256]{2,1,0:T(8,128)(2,1)S(1)} %shard_map.123), channel_id=1, replica_groups=mesh['z'=8,'x'=4,'c'=2,'y'=8] {'y'}, dimensions={0} | all-to-all | bytes 524288 | tf_op jit(solution)/shard_map/all_to_all | solution.py:245
  83.0 10.3 %all_to_all.34 = bf16[8,32,256]{2,1,0:T(8,128)(2,1)S(1)} all-to-all(bf16[8,32,256]{2,1,0:T(8,128)(2,1)S(1)} %get-tuple-element.24), channel_id=1, replica_groups=mesh['z'=8,'x'=4,'c'=2,'y'=8] {'z'}, dimensions={0} | all-to-all | bytes 262144 | tf_op jit(solution)/shard_map/all_to_all | solution.py:245
  93.3 1.0 shard_map.125
  94.3 0.0 copy-start.3
  94.4 0.0 copy-start.4
  94.4 14.1 %all_to_all.35.got = bf16[4,528,256]{2,1,0:T(8,128)(2,1)S(1)} all-to-all(bf16[4,528,256]{2,1,0:T(8,128)(2,1)S(1)} %shard_map.125), channel_id=1, replica_groups=mesh['z'=8,'x'=4,'c'=2,'y'=8] {'x'}, dimensions={0} | all-to-all | bytes 2162688 | tf_op jit(solution)/shard_map/all_to_all | solution.py:245
  108.5 6.8 %collective-permute-start.2 = (bf16[4,528,256]{2,1,0:T(8,128)(2,1)S(1)}, bf16[4,528,256]{2,1,0:T(8,128)(2,1)S(1)}, u32[]{:S(2)}, u32[]{:S(2)}) collective-permute-start(bf16[4,528,256]{2,1,0:T(8,128)(2,1)S(1)} %all_to_all.35.got), channel_id=1, source_target_pairs={{0,8},{8,0},{1,9},{9,1},{2,10},{10,2},{3,11},{11,3},{4,12},{12,4},... | collective-permute-start | bytes 3244040 | tf_op jit(solution)/shard_map/ppermute | solution.py:253
  115.3 0.0 copy-done.3
  115.3 0.0 copy-done.4
  115.3 1.0 shard_map.126
  116.3 1.3 %collective-permute-done.2.other = bf16[4,528,256]{2,1,0:T(8,128)(2,1)S(1)} collective-permute-done((bf16[4,528,256]{2,1,0:T(8,128)(2,1)S(1)}, bf16[4,528,256]{2,1,0:T(8,128)(2,1)S(1)}, u32[]{:S(2)}, u32[]{:S(2)}) %collective-permute-start.2) | collective-permute-done | bytes 1081376 | tf_op jit(solution)/shard_map/ppermute | solution.py:253
  117.6 1.6 %shard_map.127 = (f32[8,1024]{1,0:T(8,128)}, f32[256,1024]{1,0:T(8,128)}, f32[256,1024]{1,0:T(8,128)}) custom-call(s32[1]{0:T(128)} %bitcast.3.core, bf16[4,528,256]{2,1,0:T(8,128)(2,1)S(1)} %all_to_all.35.got, bf16[4,528,256]{2,1,0:T(8,128)(2,1)S(1)} %collective-permute-done.2.other), custom_call_target="tpu_custom_call" | custom-call | tf_op jit(solution)/shard_map/pallas_call | solution.py:359
  (3 shorter events, 0.1 us)
Async XLA Ops:
  3.4 39.7 %copy-start = (bf16[256,1024]{1,0:T(8,128)(2,1)S(1)}, bf16[256,1024]{1,0:T(8,128)(2,1)}, u32[]{:S(2)}) copy-start(bf16[256,1024]{1,0:T(8,128)(2,1)} %their_key.1) | copy-start | bytes 1572868
  3.4 39.7 %copy-start.1 = (bf16[256,1024]{1,0:T(8,128)(2,1)S(1)}, bf16[256,1024]{1,0:T(8,128)(2,1)}, u32[]{:S(2)}) copy-start(bf16[256,1024]{1,0:T(8,128)(2,1)} %their_value.1) | copy-start | bytes 1572868
  3.4 39.7 %copy-start.2 = (bf16[512,1024]{1,0:T(8,128)(2,1)S(1)}, bf16[512,1024]{1,0:T(8,128)(2,1)}, u32[]{:S(2)}) copy-start(bf16[512,1024]{1,0:T(8,128)(2,1)} %query.1) | copy-start | bytes 3145732
  15.5 27.6 %collective-permute-start = (bf16[4,272,256]{2,1,0:T(8,128)(2,1)S(1)}, bf16[4,272,256]{2,1,0:T(8,128)(2,1)S(1)}, u32[]{:S(2)}, u32[]{:S(2)}) collective-permute-start(bf16[4,272,256]{2,1,0:T(8,128)(2,1)S(1)} %all_to_all.30.got.mine), channel_id=1, source_target_pairs={{0,8},{8,0},{1,9},{9,1},{2,10},{10,2},{3,11},{11,3},{4,12},{12,4},... | collective-permute-start | bytes 1671176 | tf_op jit(solution)/shard_map/ppermute | solution.py:253
  49.6 16.6 %collective-permute-start.1 = (bf16[4,256,256]{2,1,0:T(8,128)(2,1)S(1)}, bf16[4,256,256]{2,1,0:T(8,128)(2,1)S(1)}, u32[]{:S(2)}, u32[]{:S(2)}) collective-permute-start(bf16[4,256,256]{2,1,0:T(8,128)(2,1)S(1)} %get-tuple-element.20), channel_id=1, source_target_pairs={{0,8},{8,0},{1,9},{9,1},{2,10},{10,2},{3,11},{11,3},{4,12},{12,4},... | collective-permute-start | bytes 1572872 | tf_op jit(solution)/shard_map/ppermute | solution.py:253
  94.3 21.0 %copy-start.3 = (bf16[1,256,256]{2,1,0:T(8,128)(2,1)S(1)}, bf16[1,256,256]{2,1,0:T(8,128)(2,1)}, u32[]{:S(2)}) copy-start(bf16[1,256,256]{2,1,0:T(8,128)(2,1)} %param.9) | copy-start | bytes 393220
  94.4 20.9 %copy-start.4 = (s32[1,256]{1,0:T(1,128)S(1)}, s32[1,256]{1,0:T(1,128)}, u32[]{:S(2)}) copy-start(s32[1,256]{1,0:T(1,128)} %occupancy.1) | copy-start | bytes 3076
  108.5 9.1 %collective-permute-start.2 = (bf16[4,528,256]{2,1,0:T(8,128)(2,1)S(1)}, bf16[4,528,256]{2,1,0:T(8,128)(2,1)S(1)}, u32[]{:S(2)}, u32[]{:S(2)}) collective-permute-start(bf16[4,528,256]{2,1,0:T(8,128)(2,1)S(1)} %all_to_all.35.got), channel_id=1, source_target_pairs={{0,8},{8,0},{1,9},{9,1},{2,10},{10,2},{3,11},{11,3},{4,12},{12,4},... | collective-permute-start | bytes 3244040 | tf_op jit(solution)/shard_map/ppermute | solution.py:253

commit v3 on v2

--- a/solution.py
+++ b/solution.py
@@ -9,6 +9,7 @@
 from jax.sharding import PartitionSpec as P
 
 HEAD = 128
+ROWS = 8
 EPS = 1e-05
 LOG2E = math.log2(math.e)
 F32, BF16 = jnp.float32, jnp.bfloat16
@@ -119,7 +120,6 @@
 ):
     del head
     chips, shard = keep.shape[0], keep.shape[1]
-    groups, part_rows = parts.shape[0], parts.shape[1]
     scale = 1.0 / math.sqrt(HEAD)
     rows = latent_order(got, chips)
     grad = rows[:, :HEAD].astype(BF16)
@@ -149,15 +149,14 @@
         else:
             query_sum[...] += query_part
             weight_sum[...] += weight_part
-    turned = query_sum[...].T.astype(BF16)
-    totals = weight_sum[...].astype(BF16)
-    each = weight_sum.shape[0] // groups
-    half = part_rows - each
-    for group in range(groups):
-        parts[group, :each, :] = totals[group * each : (group + 1) * each, :]
-        start = group * 2 * half
-        parts[group, each:, :HEAD] = turned[start : start + half]
-        parts[group, each:, HEAD:] = turned[start + half : start + 2 * half]
+    turned = query_sum[...].T
+    totals = weight_sum[...]
+    halves = parts.shape[0] // 2
+    for at in range(parts.shape[0]):
+        start = at % halves * ROWS
+        cols = slice(at // halves * HEAD, (at // halves + 1) * HEAD)
+        piece = [totals[start : start + ROWS, cols], turned[at * ROWS : (at + 1) * ROWS]]
+        parts[at] = jnp.concatenate(piece, axis=1).astype(BF16)
 
 
 def add_up(got):
@@ -173,32 +172,25 @@
         sent[at] = total
 
 
-def total_kernel(got, sent, query_rows):
-    total = add_up(got)
-    each = sent.shape[1]
-    low = total[:each].astype(BF16)
-    for at in range(sent.shape[0]):
-        sent[at] = low
-    query_rows[: got.shape[1] - each, :] = total[each:, :HEAD]
-    query_rows[got.shape[1] - each :, :] = total[each:, HEAD:]
-
-
 def gather_kernel(
-    heads, keep, theirs, weights, query_rows, my_key, my_value, their_key, their_value, sent
+    places, keep, theirs, got, my_key, my_value, their_key, their_value, sent
 ):
-    del heads
     chips, shard = keep.shape[0], keep.shape[1]
-    depth = weights.shape[0]
-    rows = query_rows.shape[0] // chips
+    halves = got.shape[0] // 2
+    depth = halves * ROWS
     mine = jnp.concatenate([my_key[...], my_value[...]], axis=1)
     other = jnp.concatenate([their_key[...], their_value[...]], axis=1)
+    pieces = [got[at].astype(F32)[:, :HEAD] for at in range(2 * halves)]
+    weights = jnp.concatenate(
+        [jnp.concatenate(pieces[:halves], axis=0), jnp.concatenate(pieces[halves:], axis=0)], axis=1
+    ).astype(BF16)
     for chip in range(chips):
         grad_normal = mm(keep[chip], mine, 1, 1) + mm(theirs[chip], other, 1, 1)
         sent[chip, :shard, :] = grad_normal.astype(BF16)
-        sent[chip, shard : shard + depth, :] = weights[...]
-        piece = query_rows[chip * rows : (chip + 1) * rows, :]
-        high = piece.astype(BF16).astype(F32)
-        sent[chip, shard + depth :, :] = jnp.concatenate([high, piece - high], axis=1).astype(BF16)
+        sent[chip, shard : shard + depth, :] = weights
+        first = places[2] * 2 * chips + 2 * chip
+        rows = [got[first + core].astype(F32) for core in range(2)]
+        sent[chip, shard + depth :, :] = jnp.concatenate(rows, axis=0).astype(BF16)
 
 
 def tokens_kernel(counts, got, tokens, occupancy, grad_tokens):
@@ -229,7 +221,7 @@
                 key_total[:, cols] = both[:, :HEAD]
                 value_total[:, cols] = both[:, HEAD:]
                 piece = source[chip, shard + depth :, :].astype(F32)
-                both_rows = piece[:, :HEAD] + piece[:, HEAD:]
+                both_rows = piece[:, HEAD:]
                 query_rows[:, cols] = jnp.where(core[0] == 0, both_rows[:rows], both_rows[rows:])
 
     @pl.when(core[0] == 0)
@@ -269,7 +261,7 @@
     heads = lse.shape[1]
     core = lax.axis_index("c").astype(jnp.int32)
     head = 2 * lax.axis_index("x").astype(jnp.int32) + core
-    head_pair = jnp.stack([head, head + 1 - 2 * core])
+    head_pair = jnp.stack([head, head + 1 - 2 * core, lax.axis_index("z").astype(jnp.int32)])
     core = core.reshape(1)
     tokens, head_pair, core = lax.optimization_barrier((tokens, head_pair, core))
     sent = pl.pallas_call(
@@ -293,9 +285,8 @@
     )(got)
     grads = swap(grads, ("z", "c"))
 
-    each, half = width // groups, rows * heads // 2
     back = (chips, shard, width)
-    part = (groups, each + half, width)
+    part = (groups * windows, ROWS, width)
     keep, give, parts = pl.pallas_call(
         main_kernel,
         out_shape=(shape(back), shape(back), shape(part)),
@@ -316,23 +307,15 @@
         compiler_params=params(40),
     )(head_pair, got, other, grads, queries, w_key, w_value)
 
-    theirs, parts = lax.optimization_barrier((sibling(give), swap(parts, "z")))
+    theirs, parts = lax.optimization_barrier((sibling(give), swap(parts, ("z", "y"))))
     parts = pl.pallas_call(
         spread_kernel,
-        out_shape=shape((windows, each + half, width)),
+        out_shape=shape(part),
         in_specs=[VMEM],
         out_specs=VMEM,
         compiler_params=params(8),
     )(parts)
-    parts = swap(parts, "y")
-    weights, query_part = pl.pallas_call(
-        total_kernel,
-        out_shape=(shape((groups, each, width)), shape((2 * half, HEAD), F32)),
-        in_specs=[VMEM],
-        out_specs=(VMEM, VMEM),
-        compiler_params=params(8),
-    )(parts)
-    weights = swap(weights, "z").reshape(width, width)
+    parts = swap(parts, ("z", "y"))
     last = (chips, shard + width + 2 * rows, width)
     sent = pl.pallas_call(
         gather_kernel,
@@ -340,12 +323,12 @@
         grid_spec=pltpu.PrefetchScalarGridSpec(
             num_scalar_prefetch=1,
             grid=(1,),
-            in_specs=[full(back), full(back), full(weights.shape), full(query_part.shape)]
+            in_specs=[full(back), full(back), full(part)]
             + [column((width, HEAD), at) for at in (0, 0, 1, 1)],
             out_specs=full(last),
         ),
         compiler_params=params(20),
-    )(head_pair, keep, theirs, weights, query_part, w_key, w_value, w_key, w_value)
+    )(head_pair, keep, theirs, parts, w_key, w_value, w_key, w_value)
     got = swap(sent, "x")
     other = sibling(got)
     grad_tokens = pl.pallas_call(

time: 120 us -> 117 us (0.975)
  blocking collectives: 86.9 us -> 85.3 us
    all_to_all x6 -> x5, blocking collectives: 86.9 us -> 85.3 us  [swap(): return lax.all_to_all(array, axis, 0, 0, tiled=True)]
where the time goes in v3:
time: 117 us
  blocking collectives  85.3 us (73%)
  starting transfers between devices  16.7 us (14%)
  Pallas kernels  12.3 us (11%)
  between operations  1.43 us (1%)
  waiting for transfers between devices  1.28 us (1%)
    all_to_all x5, blocking collectives, swap(): return lax.all_to_all(array, axis, 0, 0, tiled=True)  85.3 us
    ppermute x3, starting transfers between devices, sibling(): return lax.ppermute(array, 'c', ((0, 1), (1, 0)))  16.7 us
    pallas_call x1, Pallas kernels, body(): pl.pallas_call(main_kernel, out_shape=(shape(back), shape(back), shape(pa...  6.51 us
  transfers between devices with their start and end apart: 3, of which 1 were waited for; matrix products, arithmetic and copies ran while one was open for 0% of the time, Pallas kernels for 1%

profile of v3, /device:TPU:1, one launch (start us, length us, event | category | flops | bytes accessed | tf_op | source)
XLA Modules:
  0.0 117.1 jit_solution(11560377975549097330)
XLA Ops:
  0.6 0.1 pad_add_fusion.head.places
  1.4 2.0 %shard_map.120 = bf16[4,272,256]{2,1,0:T(8,128)(2,1)} custom-call(s32[1,1]{1,0:T(1,128)S(6)} %copy.13.refs_0_.counts, bf16[256,256]{1,0:T(8,128)(2,1)} %bitcast.9, s32[1,256]{1,0:T(1,128)} %occupancy.1, bf16[8,1024]{1,0:T(8,128)(2,1)} %bitcast.12, bf16[8,1024]{1,0:T(8,128)(2,1)} %bitcast.13, f32[8,8]{1,0:T(8,128)} %bitcast.14), custom_call_target="tpu_custom_call" | custom-call | tf_op jit(solution)/shard_map/pallas_call | solution.py:267
  3.4 0.0 copy-start
  3.4 0.0 copy-start.1
  3.4 0.0 copy-start.2
  3.5 12.1 %all_to_all.25.got.mine = bf16[4,272,256]{2,1,0:T(8,128)(2,1)S(1)} all-to-all(bf16[4,272,256]{2,1,0:T(8,128)(2,1)} %shard_map.120), channel_id=1, replica_groups=mesh['z'=8,'x'=4,'c'=2,'y'=8] {'x'}, dimensions={0} | all-to-all | bytes 1114112 | tf_op jit(solution)/shard_map/all_to_all | solution.py:237
  15.6 8.5 %collective-permute-start = (bf16[4,272,256]{2,1,0:T(8,128)(2,1)S(1)}, bf16[4,272,256]{2,1,0:T(8,128)(2,1)S(1)}, u32[]{:S(2)}, u32[]{:S(2)}) collective-permute-start(bf16[4,272,256]{2,1,0:T(8,128)(2,1)S(1)} %all_to_all.25.got.mine), channel_id=1, source_target_pairs={{0,8},{8,0},{1,9},{9,1},{2,10},{10,2},{3,11},{11,3},{4,12},{12,4},... | collective-permute-start | bytes 1671176 | tf_op jit(solution)/shard_map/ppermute | solution.py:245
  24.1 19.0 %all_to_all.26.got = bf16[16,32,256]{2,1,0:T(8,128)(2,1)S(1)} all-to-all(bf16[16,32,256]{2,1,0:T(8,128)(2,1)S(1)} %shard_map.121), channel_id=1, replica_groups=mesh['z'=8,'x'=4,'c'=2,'y'=8] {'z','c'}, dimensions={0} | all-to-all | bytes 524288 | tf_op jit(solution)/shard_map/all_to_all | solution.py:237
  43.1 0.0 collective-permute-done.other
  43.1 0.0 copy-done
  43.1 0.0 copy-done.1
  43.1 0.0 copy-done.2
  43.1 6.5 %shard_map.122 = (bf16[4,256,256]{2,1,0:T(8,128)(2,1)S(1)}, bf16[4,256,256]{2,1,0:T(8,128)(2,1)S(1)}, bf16[64,8,256]{2,1,0:T(8,128)(2,1)S(1)}) custom-call(s32[3]{0:T(128)S(1)} %pad_add_fusion.head.places, bf16[4,272,256]{2,1,0:T(8,128)(2,1)S(1)} %all_to_all.25.got.mine, bf16[4,272,256]{2,1,0:T(8,128)(2,1)S(1)} %collective-permute-done.other, ...), custom_call_target="tpu_custom_call" | custom-call | tf_op jit(solution)/shard_map/pallas_call | solution.py:290
  49.6 1.9 %collective-permute-start.1 = (bf16[4,256,256]{2,1,0:T(8,128)(2,1)S(1)}, bf16[4,256,256]{2,1,0:T(8,128)(2,1)S(1)}, u32[]{:S(2)}, u32[]{:S(2)}) collective-permute-start(bf16[4,256,256]{2,1,0:T(8,128)(2,1)S(1)} %get-tuple-element.18), channel_id=1, source_target_pairs={{0,8},{8,0},{1,9},{9,1},{2,10},{10,2},{3,11},{11,3},{4,12},{12,4},... | collective-permute-start | bytes 1572872 | tf_op jit(solution)/shard_map/ppermute | solution.py:245
  51.6 22.2 %all_to_all.27.got = bf16[64,8,256]{2,1,0:T(8,128)(2,1)S(1)} all-to-all(bf16[64,8,256]{2,1,0:T(8,128)(2,1)S(1)} %get-tuple-element.19), channel_id=1, replica_groups=mesh['z'=8,'x'=4,'c'=2,'y'=8] {'z','y'}, dimensions={0} | all-to-all | bytes 524288 | tf_op jit(solution)/shard_map/all_to_all | solution.py:237
  73.8 0.0 collective-permute-done.1.theirs
  73.8 0.1 shard_map.123
  73.9 17.4 %all_to_all.28.got = bf16[64,8,256]{2,1,0:T(8,128)(2,1)S(1)} all-to-all(bf16[64,8,256]{2,1,0:T(8,128)(2,1)S(1)} %shard_map.123), channel_id=1, replica_groups=mesh['z'=8,'x'=4,'c'=2,'y'=8] {'z','y'}, dimensions={0} | all-to-all | bytes 524288 | tf_op jit(solution)/shard_map/all_to_all | solution.py:237
  91.2 1.1 shard_map.124
  92.3 0.0 copy-start.3
  92.3 0.0 copy-start.4
  92.3 14.6 %all_to_all.29.got = bf16[4,528,256]{2,1,0:T(8,128)(2,1)S(1)} all-to-all(bf16[4,528,256]{2,1,0:T(8,128)(2,1)S(1)} %shard_map.124), channel_id=1, replica_groups=mesh['z'=8,'x'=4,'c'=2,'y'=8] {'x'}, dimensions={0} | all-to-all | bytes 2162688 | tf_op jit(solution)/shard_map/all_to_all | solution.py:237
  106.9 6.2 %collective-permute-start.2 = (bf16[4,528,256]{2,1,0:T(8,128)(2,1)S(1)}, bf16[4,528,256]{2,1,0:T(8,128)(2,1)S(1)}, u32[]{:S(2)}, u32[]{:S(2)}) collective-permute-start(bf16[4,528,256]{2,1,0:T(8,128)(2,1)S(1)} %all_to_all.29.got), channel_id=1, source_target_pairs={{0,8},{8,0},{1,9},{9,1},{2,10},{10,2},{3,11},{11,3},{4,12},{12,4},... | collective-permute-start | bytes 3244040 | tf_op jit(solution)/shard_map/ppermute | solution.py:245
  113.2 0.0 copy-done.3
  113.2 0.0 copy-done.4
  113.2 1.0 shard_map.125
  114.2 1.3 %collective-permute-done.2.other = bf16[4,528,256]{2,1,0:T(8,128)(2,1)S(1)} collective-permute-done((bf16[4,528,256]{2,1,0:T(8,128)(2,1)S(1)}, bf16[4,528,256]{2,1,0:T(8,128)(2,1)S(1)}, u32[]{:S(2)}, u32[]{:S(2)}) %collective-permute-start.2) | collective-permute-done | bytes 1081376 | tf_op jit(solution)/shard_map/ppermute | solution.py:245
  115.5 1.6 %shard_map.126 = (f32[8,1024]{1,0:T(8,128)}, f32[256,1024]{1,0:T(8,128)}, f32[256,1024]{1,0:T(8,128)}) custom-call(s32[1]{0:T(128)} %bitcast.4.core, bf16[4,528,256]{2,1,0:T(8,128)(2,1)S(1)} %all_to_all.29.got, bf16[4,528,256]{2,1,0:T(8,128)(2,1)S(1)} %collective-permute-done.2.other), custom_call_target="tpu_custom_call" | custom-call | tf_op jit(solution)/shard_map/pallas_call | solution.py:342
  (1 shorter events, 0.0 us)
Async XLA Ops:
  3.4 39.7 %copy-start = (bf16[256,1024]{1,0:T(8,128)(2,1)S(1)}, bf16[256,1024]{1,0:T(8,128)(2,1)}, u32[]{:S(2)}) copy-start(bf16[256,1024]{1,0:T(8,128)(2,1)} %their_key.1) | copy-start | bytes 1572868
  3.4 39.7 %copy-start.1 = (bf16[256,1024]{1,0:T(8,128)(2,1)S(1)}, bf16[256,1024]{1,0:T(8,128)(2,1)}, u32[]{:S(2)}) copy-start(bf16[256,1024]{1,0:T(8,128)(2,1)} %their_value.1) | copy-start | bytes 1572868
  3.4 39.7 %copy-start.2 = (bf16[512,1024]{1,0:T(8,128)(2,1)S(1)}, bf16[512,1024]{1,0:T(8,128)(2,1)}, u32[]{:S(2)}) copy-start(bf16[512,1024]{1,0:T(8,128)(2,1)} %query.1) | copy-start | bytes 3145732
  15.6 27.6 %collective-permute-start = (bf16[4,272,256]{2,1,0:T(8,128)(2,1)S(1)}, bf16[4,272,256]{2,1,0:T(8,128)(2,1)S(1)}, u32[]{:S(2)}, u32[]{:S(2)}) collective-permute-start(bf16[4,272,256]{2,1,0:T(8,128)(2,1)S(1)} %all_to_all.25.got.mine), channel_id=1, source_target_pairs={{0,8},{8,0},{1,9},{9,1},{2,10},{10,2},{3,11},{11,3},{4,12},{12,4},... | collective-permute-start | bytes 1671176 | tf_op jit(solution)/shard_map/ppermute | solution.py:245
  49.6 24.2 %collective-permute-start.1 = (bf16[4,256,256]{2,1,0:T(8,128)(2,1)S(1)}, bf16[4,256,256]{2,1,0:T(8,128)(2,1)S(1)}, u32[]{:S(2)}, u32[]{:S(2)}) collective-permute-start(bf16[4,256,256]{2,1,0:T(8,128)(2,1)S(1)} %get-tuple-element.18), channel_id=1, source_target_pairs={{0,8},{8,0},{1,9},{9,1},{2,10},{10,2},{3,11},{11,3},{4,12},{12,4},... | collective-permute-start | bytes 1572872 | tf_op jit(solution)/shard_map/ppermute | solution.py:245
  92.3 20.9 %copy-start.3 = (bf16[1,256,256]{2,1,0:T(8,128)(2,1)S(1)}, bf16[1,256,256]{2,1,0:T(8,128)(2,1)}, u32[]{:S(2)}) copy-start(bf16[1,256,256]{2,1,0:T(8,128)(2,1)} %param.9) | copy-start | bytes 393220
  92.3 20.9 %copy-start.4 = (s32[1,256]{1,0:T(1,128)S(1)}, s32[1,256]{1,0:T(1,128)}, u32[]{:S(2)}) copy-start(s32[1,256]{1,0:T(1,128)} %occupancy.1) | copy-start | bytes 3076
  106.9 8.6 %collective-permute-start.2 = (bf16[4,528,256]{2,1,0:T(8,128)(2,1)S(1)}, bf16[4,528,256]{2,1,0:T(8,128)(2,1)S(1)}, u32[]{:S(2)}, u32[]{:S(2)}) collective-permute-start(bf16[4,528,256]{2,1,0:T(8,128)(2,1)S(1)} %all_to_all.29.got), channel_id=1, source_target_pairs={{0,8},{8,0},{1,9},{9,1},{2,10},{10,2},{3,11},{11,3},{4,12},{12,4},... | collective-permute-start | bytes 3244040 | tf_op jit(solution)/shard_map/ppermute | solution.py:245

commit v4 on v3

--- a/solution.py
+++ b/solution.py
@@ -10,6 +10,7 @@
 
 HEAD = 128
 ROWS = 8
+BLOCK = 512
 EPS = 1e-05
 LOG2E = math.log2(math.e)
 F32, BF16 = jnp.float32, jnp.bfloat16
@@ -115,8 +116,16 @@
     )
 
 
+def share_kernel(head, keep, give, w_key, w_value, kept, given):
+    del head
+    weights = jnp.concatenate([w_key[...], w_value[...]], axis=1)
+    for chip in range(keep.shape[0]):
+        kept[chip] = mm(keep[chip], weights, 1, 1)
+        given[chip] = mm(give[chip], weights, 1, 1).astype(BF16)
+
+
 def main_kernel(
-    head, mine, other, got, query, w_key, w_value, keep, give, parts, query_sum, weight_sum
+    head, mine, other, got, query, w_key, w_value, keep, give, parts, query_sum, normals, grads
 ):
     del head
     chips, shard = keep.shape[0], keep.shape[1]
@@ -128,10 +137,13 @@
     delta = extra[3:4] + extra[4:5] + extra[5:6]
     queries = query[...]
     weights = jnp.concatenate([w_key[...], w_value[...]], axis=1)
-    for block in range(2 * chips):
-        source, target = (mine, keep) if block < chips else (other, give)
-        chip = block % chips
-        normal = layer_norm(source[chip, :shard, :].astype(F32))[0].astype(BF16)
+    per = BLOCK // shard
+    for block in range(2 * chips // per):
+        first = block * per
+        source, target = (mine, keep) if first < chips else (other, give)
+        spots = [(first + at) % chips for at in range(per)]
+        tokens = jnp.concatenate([source[spot, :shard, :] for spot in spots], axis=0)
+        normal = layer_norm(tokens.astype(F32))[0].astype(BF16)
         both = jnp.dot(normal, weights, preferred_element_type=F32).astype(BF16)
         keys, values = both[:, :HEAD], both[:, HEAD:]
         probs = jnp.exp2(mm(keys, queries, 1, 1) * (scale * LOG2E) - lse)
@@ -140,17 +152,17 @@
         grad_scores = (scale * probs * (grad_probs - delta)).astype(BF16)
         grad_keys = jnp.dot(grad_scores, queries, preferred_element_type=F32)
         grad_both = jnp.concatenate([grad_keys, grad_values], axis=1).astype(BF16)
-        target[chip] = grad_both
+        for at, spot in enumerate(spots):
+            target[spot] = grad_both[at * shard : (at + 1) * shard]
         query_part = mm(keys, grad_scores, 0, 0)
-        weight_part = mm(normal, grad_both, 0, 0)
         if block == 0:
             query_sum[...] = query_part
-            weight_sum[...] = weight_part
         else:
             query_sum[...] += query_part
-            weight_sum[...] += weight_part
+        normals[block * BLOCK : (block + 1) * BLOCK, :] = normal
+        grads[block * BLOCK : (block + 1) * BLOCK, :] = grad_both
     turned = query_sum[...].T
-    totals = weight_sum[...]
+    totals = mm(normals[...], grads[...], 0, 0)
     halves = parts.shape[0] // 2
     for at in range(parts.shape[0]):
         start = at % halves * ROWS
@@ -172,23 +184,18 @@
         sent[at] = total
 
 
-def gather_kernel(
-    places, keep, theirs, got, my_key, my_value, their_key, their_value, sent
-):
-    chips, shard = keep.shape[0], keep.shape[1]
+def gather_kernel(group, kept, theirs, got, sent):
+    chips, shard = kept.shape[0], kept.shape[1]
     halves = got.shape[0] // 2
     depth = halves * ROWS
-    mine = jnp.concatenate([my_key[...], my_value[...]], axis=1)
-    other = jnp.concatenate([their_key[...], their_value[...]], axis=1)
     pieces = [got[at].astype(F32)[:, :HEAD] for at in range(2 * halves)]
     weights = jnp.concatenate(
         [jnp.concatenate(pieces[:halves], axis=0), jnp.concatenate(pieces[halves:], axis=0)], axis=1
     ).astype(BF16)
     for chip in range(chips):
-        grad_normal = mm(keep[chip], mine, 1, 1) + mm(theirs[chip], other, 1, 1)
-        sent[chip, :shard, :] = grad_normal.astype(BF16)
+        sent[chip, :shard, :] = (kept[chip] + theirs[chip].astype(F32)).astype(BF16)
         sent[chip, shard : shard + depth, :] = weights
-        first = places[2] * 2 * chips + 2 * chip
+        first = group[0] * 2 * chips + 2 * chip
         rows = [got[first + core].astype(F32) for core in range(2)]
         sent[chip, shard + depth :, :] = jnp.concatenate(rows, axis=0).astype(BF16)
 
@@ -260,10 +267,9 @@
     chips, groups, windows = lax.axis_size("x"), lax.axis_size("z"), lax.axis_size("y")
     heads = lse.shape[1]
     core = lax.axis_index("c").astype(jnp.int32)
-    head = 2 * lax.axis_index("x").astype(jnp.int32) + core
-    head_pair = jnp.stack([head, head + 1 - 2 * core, lax.axis_index("z").astype(jnp.int32)])
-    core = core.reshape(1)
-    tokens, head_pair, core = lax.optimization_barrier((tokens, head_pair, core))
+    head = (2 * lax.axis_index("x").astype(jnp.int32) + core).reshape(1)
+    core, group = core.reshape(1), lax.axis_index("z").astype(jnp.int32).reshape(1)
+    tokens, head, core, group = lax.optimization_barrier((tokens, head, core, group))
     sent = pl.pallas_call(
         pack_kernel,
         out_shape=shape((chips, shard + 2 * rows, width)),
@@ -302,12 +308,26 @@
                 column((width, HEAD), 0),
             ],
             out_specs=[full(back), full(back), full(part)],
-            scratch_shapes=[pltpu.VMEM((HEAD, latents), F32), pltpu.VMEM((width, width), F32)],
+            scratch_shapes=[pltpu.VMEM((HEAD, latents), F32)]
+            + [pltpu.VMEM((2 * chips * shard, width), BF16)] * 2,
         ),
         compiler_params=params(40),
-    )(head_pair, got, other, grads, queries, w_key, w_value)
-
-    theirs, parts = lax.optimization_barrier((sibling(give), swap(parts, ("z", "y"))))
+    )(head, got, other, grads, queries, w_key, w_value)
+
+    kept, given = pl.pallas_call(
+        share_kernel,
+        out_shape=(shape(back, F32), shape(back)),
+        grid_spec=pltpu.PrefetchScalarGridSpec(
+            num_scalar_prefetch=1,
+            grid=(1,),
+            in_specs=[full(back)] * 2 + [column((width, HEAD), 0)] * 2,
+            out_specs=[full(back)] * 2,
+        ),
+        compiler_params=params(20),
+        cost_estimate=pl.CostEstimate(flops=270000000, bytes_accessed=3000000, transcendentals=0),
+    )(head, keep, give, w_key, w_value)
+    theirs = sibling(given)
+    parts = swap(parts, ("z", "y"))
     parts = pl.pallas_call(
         spread_kernel,
         out_shape=shape(part),
@@ -320,15 +340,10 @@
     sent = pl.pallas_call(
         gather_kernel,
         out_shape=shape(last),
-        grid_spec=pltpu.PrefetchScalarGridSpec(
-            num_scalar_prefetch=1,
-            grid=(1,),
-            in_specs=[full(back), full(back), full(part)]
-            + [column((width, HEAD), at) for at in (0, 0, 1, 1)],
-            out_specs=full(last),
-        ),
-        compiler_params=params(20),
-    )(head_pair, keep, theirs, parts, w_key, w_value, w_key, w_value)
+        in_specs=[SMEM] + [VMEM] * 3,
+        out_specs=VMEM,
+        compiler_params=params(16),
+    )(group, kept, theirs, parts)
     got = swap(sent, "x")
     other = sibling(got)
     grad_tokens = pl.pallas_call(

time: 117 us -> 113 us (0.966)
  blocking collectives: 85.3 us -> 45.6 us
  waiting for transfers between devices: 1.28 us -> 22.9 us
  starting transfers between devices: 16.7 us -> 31.5 us
    all_to_all x5 -> x3, blocking collectives: 85.3 us -> 45.6 us  [swap(): return lax.all_to_all(array, axis, 0, 0, tiled=True)]
    all_to_all x0 -> x2, waiting for transfers between devices: none -> 21.6 us  [swap(): return lax.all_to_all(array, axis, 0, 0, tiled=True)]
    all_to_all x0 -> x2, starting transfers between devices: none -> 14.1 us  [swap(): return lax.all_to_all(array, axis, 0, 0, tiled=True)]
    pallas_call x1, Pallas kernels: 6.51 us -> 4.6 us  [body(): pl.pallas_call(main_kernel, out_shape=(shape(back), shape(back), shape(pa...]
  transfers between devices with their start and end apart: 3 -> 5, of which waited for: 1 -> 3; matrix products, arithmetic and copies ran while one was open for 0% -> 0% of each run, Pallas kernels for 1% -> 3%
where the time goes in v4:
time: 113 us
  blocking collectives  45.6 us (40%)
  starting transfers between devices  31.5 us (28%)
  waiting for transfers between devices  22.9 us (20%)
  Pallas kernels  11.5 us (10%)
  between operations  1.43 us (1%)
    all_to_all x3, blocking collectives, swap(): return lax.all_to_all(array, axis, 0, 0, tiled=True)  45.6 us
    all_to_all x2, waiting for transfers between devices, swap(): return lax.all_to_all(array, axis, 0, 0, tiled=True)  21.6 us
    ppermute x3, starting transfers between devices, sibling(): return lax.ppermute(array, 'c', ((0, 1), (1, 0)))  17.4 us
    all_to_all x2, starting transfers between devices, swap(): return lax.all_to_all(array, axis, 0, 0, tiled=True)  14.1 us
    pallas_call x1, Pallas kernels, body(): pl.pallas_call(main_kernel, out_shape=(shape(back), shape(back), shape(pa...  4.6 us
  transfers between devices with their start and end apart: 5, of which 3 were waited for; matrix products, arithmetic and copies ran while one was open for 0% of the time, Pallas kernels for 3%

profile of v4, /device:TPU:1, one launch (start us, length us, event | category | flops | bytes accessed | tf_op | source)
XLA Modules:
  0.0 112.9 jit_solution(17286054358617216840)
XLA Ops:
  1.3 2.0 %shard_map.120 = bf16[4,272,256]{2,1,0:T(8,128)(2,1)} custom-call(s32[1,1]{1,0:T(1,128)S(6)} %copy.13.refs_0_.counts, bf16[256,256]{1,0:T(8,128)(2,1)} %bitcast.8, s32[1,256]{1,0:T(1,128)} %occupancy.1, bf16[8,1024]{1,0:T(8,128)(2,1)} %bitcast.11, bf16[8,1024]{1,0:T(8,128)(2,1)} %bitcast.12, f32[8,8]{1,0:T(8,128)} %bitcast.13), custom_call_target="tpu_custom_call" | custom-call | tf_op jit(solution)/shard_map/pallas_call | solution.py:273
  3.3 0.0 copy-start
  3.3 0.0 copy-start.1
  3.4 0.0 copy-start.2
  3.4 12.1 %all_to_all.25.got.mine = bf16[4,272,256]{2,1,0:T(8,128)(2,1)S(1)} all-to-all(bf16[4,272,256]{2,1,0:T(8,128)(2,1)} %shard_map.120), channel_id=1, replica_groups=mesh['z'=8,'x'=4,'c'=2,'y'=8] {'x'}, dimensions={0} | all-to-all | bytes 1114112 | tf_op jit(solution)/shard_map/all_to_all | solution.py:244
  15.5 8.5 %collective-permute-start = (bf16[4,272,256]{2,1,0:T(8,128)(2,1)S(1)}, bf16[4,272,256]{2,1,0:T(8,128)(2,1)S(1)}, u32[]{:S(2)}, u32[]{:S(2)}) collective-permute-start(bf16[4,272,256]{2,1,0:T(8,128)(2,1)S(1)} %all_to_all.25.got.mine), channel_id=1, source_target_pairs={{0,8},{8,0},{1,9},{9,1},{2,10},{10,2},{3,11},{11,3},{4,12},{12,4},... | collective-permute-start | bytes 1671176 | tf_op jit(solution)/shard_map/ppermute | solution.py:252
  24.0 19.0 %all_to_all.26.got = bf16[16,32,256]{2,1,0:T(8,128)(2,1)S(1)} all-to-all(bf16[16,32,256]{2,1,0:T(8,128)(2,1)S(1)} %shard_map.121), channel_id=1, replica_groups=mesh['z'=8,'x'=4,'c'=2,'y'=8] {'z','c'}, dimensions={0} | all-to-all | bytes 524288 | tf_op jit(solution)/shard_map/all_to_all | solution.py:244
  43.0 0.0 collective-permute-done.other
  43.0 0.0 copy-done
  43.0 0.0 copy-done.1
  43.0 0.0 copy-done.2
  43.0 4.6 %shard_map.122 = (bf16[4,256,256]{2,1,0:T(8,128)(2,1)S(1)}, bf16[4,256,256]{2,1,0:T(8,128)(2,1)S(1)}, bf16[64,8,256]{2,1,0:T(8,128)(2,1)}) custom-call(s32[1]{0:T(128)} %bitcast.1.head, bf16[4,272,256]{2,1,0:T(8,128)(2,1)S(1)} %all_to_all.25.got.mine, bf16[4,272,256]{2,1,0:T(8,128)(2,1)S(1)} %collective-permute-done.other, ...), custom_call_target="tpu_custom_call" | custom-call | tf_op jit(solution)/shard_map/pallas_call | solution.py:296
  47.6 8.5 %all-to-all-start.2 = ((bf16[64,8,256]{2,1,0:T(8,128)(2,1)}), bf16[64,8,256]{2,1,0:T(8,128)(2,1)S(1)}, u32[]{:S(2)}, u32[]{:S(2)}) async-start(bf16[64,8,256]{2,1,0:T(8,128)(2,1)} %get-tuple-element.23), calls=%async_computation.2 | async-start | bytes 524288 | tf_op jit(solution)/shard_map/all_to_all | solution.py:244
  56.1 1.3 %shard_map.123 = (f32[4,256,256]{2,1,0:T(8,128)S(1)}, bf16[4,256,256]{2,1,0:T(8,128)(2,1)}) custom-call(s32[1]{0:T(128)} %bitcast.1.head, bf16[4,256,256]{2,1,0:T(8,128)(2,1)S(1)} %get-tuple-element.19.keep, bf16[4,256,256]{2,1,0:T(8,128)(2,1)S(1)} %get-tuple-element.20.give, bf16[256,1024]{1,0:T(8,128)(2,1)S(1)} %copy-done, bf16[256,1024]{1,0:T(8,128)(2,1)S(1)} %copy-done.1), custom_call_target="tpu_custom_call" | custom-call | flops 270000000 | bytes 3000000 | tf_op jit(solution)/shard_map/pallas_call | solution.py:317
  57.4 2.6 %collective-permute-start.1 = (bf16[4,256,256]{2,1,0:T(8,128)(2,1)}, bf16[4,256,256]{2,1,0:T(8,128)(2,1)S(1)}, u32[]{:S(2)}, u32[]{:S(2)}) collective-permute-start(bf16[4,256,256]{2,1,0:T(8,128)(2,1)} %get-tuple-element.22), channel_id=1, source_target_pairs={{0,8},{8,0},{1,9},{9,1},{2,10},{10,2},{3,11},{11,3},{4,12},{12,4},... | collective-permute-start | bytes 1572872 | tf_op jit(solution)/shard_map/ppermute | solution.py:252
  60.0 9.1 %all-to-all-done.2.got = bf16[64,8,256]{2,1,0:T(8,128)(2,1)S(1)} async-done(((bf16[64,8,256]{2,1,0:T(8,128)(2,1)}), bf16[64,8,256]{2,1,0:T(8,128)(2,1)S(1)}, u32[]{:S(2)}, u32[]{:S(2)}) %all-to-all-start.2) | async-done | bytes 262176 | tf_op jit(solution)/shard_map/all_to_all | solution.py:244
  69.1 0.8 shard_map.124
  69.9 5.6 %all-to-all-start.3 = ((bf16[64,8,256]{2,1,0:T(8,128)(2,1)}), bf16[64,8,256]{2,1,0:T(8,128)(2,1)S(1)}, u32[]{:S(2)}, u32[]{:S(2)}) async-start(bf16[64,8,256]{2,1,0:T(8,128)(2,1)} %shard_map.124), calls=%async_computation.3 | async-start | bytes 524288 | tf_op jit(solution)/shard_map/all_to_all | solution.py:244
  75.5 0.0 collective-permute-done.1.theirs
  75.5 12.5 %all-to-all-done.3.got = bf16[64,8,256]{2,1,0:T(8,128)(2,1)S(1)} async-done(((bf16[64,8,256]{2,1,0:T(8,128)(2,1)}), bf16[64,8,256]{2,1,0:T(8,128)(2,1)S(1)}, u32[]{:S(2)}, u32[]{:S(2)}) %all-to-all-start.3) | async-done | bytes 262176 | tf_op jit(solution)/shard_map/all_to_all | solution.py:244
  88.0 0.1 shard_map.125
  88.1 0.0 copy-start.3
  88.2 0.0 copy-start.4
  88.2 14.5 %all_to_all.27.got = bf16[4,528,256]{2,1,0:T(8,128)(2,1)S(1)} all-to-all(bf16[4,528,256]{2,1,0:T(8,128)(2,1)S(1)} %shard_map.125), channel_id=1, replica_groups=mesh['z'=8,'x'=4,'c'=2,'y'=8] {'x'}, dimensions={0} | all-to-all | bytes 2162688 | tf_op jit(solution)/shard_map/all_to_all | solution.py:244
  102.7 6.3 %collective-permute-start.2 = (bf16[4,528,256]{2,1,0:T(8,128)(2,1)S(1)}, bf16[4,528,256]{2,1,0:T(8,128)(2,1)S(1)}, u32[]{:S(2)}, u32[]{:S(2)}) collective-permute-start(bf16[4,528,256]{2,1,0:T(8,128)(2,1)S(1)} %all_to_all.27.got), channel_id=1, source_target_pairs={{0,8},{8,0},{1,9},{9,1},{2,10},{10,2},{3,11},{11,3},{4,12},{12,4},... | collective-permute-start | bytes 3244040 | tf_op jit(solution)/shard_map/ppermute | solution.py:252
  109.0 0.0 copy-done.3
  109.0 0.0 copy-done.4
  109.0 1.0 shard_map.126
  110.0 1.3 %collective-permute-done.2.other = bf16[4,528,256]{2,1,0:T(8,128)(2,1)S(1)} collective-permute-done((bf16[4,528,256]{2,1,0:T(8,128)(2,1)S(1)}, bf16[4,528,256]{2,1,0:T(8,128)(2,1)S(1)}, u32[]{:S(2)}, u32[]{:S(2)}) %collective-permute-start.2) | collective-permute-done | bytes 1081376 | tf_op jit(solution)/shard_map/ppermute | solution.py:252
  111.3 1.6 %shard_map.127 = (f32[8,1024]{1,0:T(8,128)}, f32[256,1024]{1,0:T(8,128)}, f32[256,1024]{1,0:T(8,128)}) custom-call(s32[1]{0:T(128)} %bitcast.2.core, bf16[4,528,256]{2,1,0:T(8,128)(2,1)S(1)} %all_to_all.27.got, bf16[4,528,256]{2,1,0:T(8,128)(2,1)S(1)} %collective-permute-done.2.other), custom_call_target="tpu_custom_call" | custom-call | tf_op jit(solution)/shard_map/pallas_call | solution.py:357
  (1 shorter events, 0.0 us)
Async XLA Ops:
  3.3 39.7 %copy-start = (bf16[256,1024]{1,0:T(8,128)(2,1)S(1)}, bf16[256,1024]{1,0:T(8,128)(2,1)}, u32[]{:S(2)}) copy-start(bf16[256,1024]{1,0:T(8,128)(2,1)} %w_key.3) | copy-start | bytes 1572868
  3.3 39.7 %copy-start.1 = (bf16[256,1024]{1,0:T(8,128)(2,1)S(1)}, bf16[256,1024]{1,0:T(8,128)(2,1)}, u32[]{:S(2)}) copy-start(bf16[256,1024]{1,0:T(8,128)(2,1)} %w_value.3) | copy-start | bytes 1572868
  3.4 39.7 %copy-start.2 = (bf16[512,1024]{1,0:T(8,128)(2,1)S(1)}, bf16[512,1024]{1,0:T(8,128)(2,1)}, u32[]{:S(2)}) copy-start(bf16[512,1024]{1,0:T(8,128)(2,1)} %query.1) | copy-start | bytes 3145732
  15.5 27.6 %collective-permute-start = (bf16[4,272,256]{2,1,0:T(8,128)(2,1)S(1)}, bf16[4,272,256]{2,1,0:T(8,128)(2,1)S(1)}, u32[]{:S(2)}, u32[]{:S(2)}) collective-permute-start(bf16[4,272,256]{2,1,0:T(8,128)(2,1)S(1)} %all_to_all.25.got.mine), channel_id=1, source_target_pairs={{0,8},{8,0},{1,9},{9,1},{2,10},{10,2},{3,11},{11,3},{4,12},{12,4},... | collective-permute-start | bytes 1671176 | tf_op jit(solution)/shard_map/ppermute | solution.py:252
  47.6 21.5 %all-to-all-start.2 = ((bf16[64,8,256]{2,1,0:T(8,128)(2,1)}), bf16[64,8,256]{2,1,0:T(8,128)(2,1)S(1)}, u32[]{:S(2)}, u32[]{:S(2)}) async-start(bf16[64,8,256]{2,1,0:T(8,128)(2,1)} %get-tuple-element.23), calls=%async_computation.2 | async-start | bytes 524288 | tf_op jit(solution)/shard_map/all_to_all | solution.py:244
  57.4 18.1 %collective-permute-start.1 = (bf16[4,256,256]{2,1,0:T(8,128)(2,1)}, bf16[4,256,256]{2,1,0:T(8,128)(2,1)S(1)}, u32[]{:S(2)}, u32[]{:S(2)}) collective-permute-start(bf16[4,256,256]{2,1,0:T(8,128)(2,1)} %get-tuple-element.22), channel_id=1, source_target_pairs={{0,8},{8,0},{1,9},{9,1},{2,10},{10,2},{3,11},{11,3},{4,12},{12,4},... | collective-permute-start | bytes 1572872 | tf_op jit(solution)/shard_map/ppermute | solution.py:252
  69.9 18.1 %all-to-all-start.3 = ((bf16[64,8,256]{2,1,0:T(8,128)(2,1)}), bf16[64,8,256]{2,1,0:T(8,128)(2,1)S(1)}, u32[]{:S(2)}, u32[]{:S(2)}) async-start(bf16[64,8,256]{2,1,0:T(8,128)(2,1)} %shard_map.124), calls=%async_computation.3 | async-start | bytes 524288 | tf_op jit(solution)/shard_map/all_to_all | solution.py:244
  88.1 20.9 %copy-start.3 = (bf16[1,256,256]{2,1,0:T(8,128)(2,1)S(1)}, bf16[1,256,256]{2,1,0:T(8,128)(2,1)}, u32[]{:S(2)}) copy-start(bf16[1,256,256]{2,1,0:T(8,128)(2,1)} %param.9) | copy-start | bytes 393220
  88.2 20.9 %copy-start.4 = (s32[1,256]{1,0:T(1,128)S(1)}, s32[1,256]{1,0:T(1,128)}, u32[]{:S(2)}) copy-start(s32[1,256]{1,0:T(1,128)} %occupancy.1) | copy-start | bytes 3076
  102.7 8.6 %collective-permute-start.2 = (bf16[4,528,256]{2,1,0:T(8,128)(2,1)S(1)}, bf16[4,528,256]{2,1,0:T(8,128)(2,1)S(1)}, u32[]{:S(2)}, u32[]{:S(2)}) collective-permute-start(bf16[4,528,256]{2,1,0:T(8,128)(2,1)S(1)} %all_to_all.27.got), channel_id=1, source_target_pairs={{0,8},{8,0},{1,9},{9,1},{2,10},{10,2},{3,11},{11,3},{4,12},{12,4},... | collective-permute-start | bytes 3244040 | tf_op jit(solution)/shard_map/ppermute | solution.py:252

commit v5 on v4

--- a/solution.py
+++ b/solution.py
@@ -15,6 +15,7 @@
 LOG2E = math.log2(math.e)
 F32, BF16 = jnp.float32, jnp.bfloat16
 VMEM = pl.BlockSpec(memory_space=pltpu.VMEM)
+HBM = pl.BlockSpec(memory_space=pltpu.HBM)
 SMEM = pl.BlockSpec(memory_space=pltpu.SMEM)
 
 
@@ -119,30 +120,23 @@
 def share_kernel(head, keep, give, w_key, w_value, kept, given):
     del head
     weights = jnp.concatenate([w_key[...], w_value[...]], axis=1)
-    for chip in range(keep.shape[0]):
-        kept[chip] = mm(keep[chip], weights, 1, 1)
-        given[chip] = mm(give[chip], weights, 1, 1).astype(BF16)
-
-
-def main_kernel(
-    head, mine, other, got, query, w_key, w_value, keep, give, parts, query_sum, normals, grads
-):
-    del head
-    chips, shard = keep.shape[0], keep.shape[1]
+    shard = kept.shape[1]
+    for chip in range(kept.shape[0]):
+        rows = slice(chip * shard, (chip + 1) * shard)
+        kept[chip] = mm(keep[rows, :], weights, 1, 1)
+        given[chip] = mm(give[rows, :], weights, 1, 1).astype(BF16)
+
+
+def attend(source, grad, lse, delta, queries, weights, target, query_sum, normals, grads, done):
+    chips = source.shape[0]
+    shard = target.shape[0] // chips
     scale = 1.0 / math.sqrt(HEAD)
-    rows = latent_order(got, chips)
-    grad = rows[:, :HEAD].astype(BF16)
-    extra = rows[:, HEAD:].T
-    lse = (extra[0:1] + extra[1:2] + extra[2:3]) * LOG2E
-    delta = extra[3:4] + extra[4:5] + extra[5:6]
-    queries = query[...]
-    weights = jnp.concatenate([w_key[...], w_value[...]], axis=1)
     per = BLOCK // shard
-    for block in range(2 * chips // per):
+    copies = []
+    for block in range(chips // per):
         first = block * per
-        source, target = (mine, keep) if first < chips else (other, give)
-        spots = [(first + at) % chips for at in range(per)]
-        tokens = jnp.concatenate([source[spot, :shard, :] for spot in spots], axis=0)
+        rows = pl.ds(block * BLOCK, BLOCK)
+        tokens = jnp.concatenate([source[first + at, :shard, :] for at in range(per)], axis=0)
         normal = layer_norm(tokens.astype(F32))[0].astype(BF16)
         both = jnp.dot(normal, weights, preferred_element_type=F32).astype(BF16)
         keys, values = both[:, :HEAD], both[:, HEAD:]
@@ -152,17 +146,66 @@
         grad_scores = (scale * probs * (grad_probs - delta)).astype(BF16)
         grad_keys = jnp.dot(grad_scores, queries, preferred_element_type=F32)
         grad_both = jnp.concatenate([grad_keys, grad_values], axis=1).astype(BF16)
-        for at, spot in enumerate(spots):
-            target[spot] = grad_both[at * shard : (at + 1) * shard]
-        query_part = mm(keys, grad_scores, 0, 0)
-        if block == 0:
-            query_sum[...] = query_part
-        else:
-            query_sum[...] += query_part
-        normals[block * BLOCK : (block + 1) * BLOCK, :] = normal
-        grads[block * BLOCK : (block + 1) * BLOCK, :] = grad_both
-    turned = query_sum[...].T
-    totals = mm(normals[...], grads[...], 0, 0)
+        query_sum[...] += mm(keys, grad_scores, 0, 0)
+        normals[rows, :] = normal
+        grads[rows, :] = grad_both
+        copy = pltpu.make_async_copy(grads.at[rows], target.at[rows], done.at[block])
+        copy.start()
+        copies.append(copy)
+    total = mm(normals[...], grads[...], 0, 0)
+    for copy in copies:
+        copy.wait()
+    return total
+
+
+def first_kernel(
+    head, mine, got, query, w_key, w_value, keep, grad_rows, lines, query_sum, weight_sum, *scratch
+):
+    del head
+    rows = latent_order(got, got.shape[1] // ROWS)
+    grad = rows[:, :HEAD].astype(BF16)
+    extra = rows[:, HEAD:].T
+    lse = (extra[0:1] + extra[1:2] + extra[2:3]) * LOG2E
+    delta = extra[3:4] + extra[4:5] + extra[5:6]
+    grad_rows[...] = grad
+    lines[...] = jnp.concatenate([lse, delta, jnp.zeros((ROWS - 2, rows.shape[0]), F32)], axis=0)
+    weights = jnp.concatenate([w_key[...], w_value[...]], axis=1)
+    query_sum[...] = jnp.zeros_like(query_sum)
+    weight_sum[...] = attend(
+        mine, grad, lse, delta, query[...], weights, keep, query_sum, *scratch
+    )
+
+
+def second_kernel(
+    head,
+    other,
+    grad_rows,
+    lines,
+    query_sum,
+    weight_sum,
+    query,
+    w_key,
+    w_value,
+    give,
+    parts,
+    total,
+    *scratch,
+):
+    del head
+    weights = jnp.concatenate([w_key[...], w_value[...]], axis=1)
+    total[...] = query_sum[...]
+    totals = weight_sum[...] + attend(
+        other,
+        grad_rows[...],
+        lines[0:1, :],
+        lines[1:2, :],
+        query[...],
+        weights,
+        give,
+        total,
+        *scratch,
+    )
+    turned = total[...].T
     halves = parts.shape[0] // 2
     for at in range(parts.shape[0]):
         start = at % halves * ROWS
@@ -293,26 +336,46 @@
 
     back = (chips, shard, width)
     part = (groups * windows, ROWS, width)
-    keep, give, parts = pl.pallas_call(
-        main_kernel,
-        out_shape=(shape(back), shape(back), shape(part)),
+    sums = ((HEAD, latents), (width, width))
+    many = (chips * shard, width)
+    held = [pltpu.VMEM(many, BF16)] * 2 + [pltpu.SemaphoreType.DMA((chips * shard // BLOCK,))]
+    work = pl.CostEstimate(
+        flops=11 * chips * shard * latents * HEAD,
+        bytes_accessed=4 * chips * shard * width,
+        transcendentals=chips * shard * latents,
+    )
+    operands = [
+        column((latents, HEAD), 0),
+        column((width, HEAD), 0),
+        column((width, HEAD), 0),
+    ]
+    rest = ((latents, HEAD), (ROWS, latents)) + sums
+    keep, grad_rows, lines, *totals = pl.pallas_call(
+        first_kernel,
+        out_shape=(pltpu.HBM(many, BF16), shape(rest[0])) + tuple(shape(dims, F32) for dims in rest[1:]),
         grid_spec=pltpu.PrefetchScalarGridSpec(
             num_scalar_prefetch=1,
             grid=(1,),
-            in_specs=[
-                full(got.shape),
-                full(other.shape),
-                full(grads.shape),
-                column((latents, HEAD), 0),
-                column((width, HEAD), 0),
-                column((width, HEAD), 0),
-            ],
-            out_specs=[full(back), full(back), full(part)],
-            scratch_shapes=[pltpu.VMEM((HEAD, latents), F32)]
-            + [pltpu.VMEM((2 * chips * shard, width), BF16)] * 2,
+            in_specs=[full(got.shape), full(grads.shape)] + operands,
+            out_specs=[HBM] + [full(dims) for dims in rest],
+            scratch_shapes=held,
         ),
-        compiler_params=params(40),
-    )(head, got, other, grads, queries, w_key, w_value)
+        compiler_params=params(30),
+        cost_estimate=work,
+    )(head, got, grads, queries, w_key, w_value)
+    give, parts = pl.pallas_call(
+        second_kernel,
+        out_shape=(pltpu.HBM(many, BF16), shape(part)),
+        grid_spec=pltpu.PrefetchScalarGridSpec(
+            num_scalar_prefetch=1,
+            grid=(1,),
+            in_specs=[full(other.shape)] + [full(dims) for dims in rest] + operands,
+            out_specs=[HBM, full(part)],
+            scratch_shapes=[pltpu.VMEM(sums[0], F32)] + held,
+        ),
+        compiler_params=params(30),
+        cost_estimate=work,
+    )(head, other, grad_rows, lines, *totals, queries, w_key, w_value)
 
     kept, given = pl.pallas_call(
         share_kernel,
@@ -320,7 +383,7 @@
         grid_spec=pltpu.PrefetchScalarGridSpec(
             num_scalar_prefetch=1,
             grid=(1,),
-            in_specs=[full(back)] * 2 + [column((width, HEAD), 0)] * 2,
+            in_specs=[full(many)] * 2 + [column((width, HEAD), 0)] * 2,
             out_specs=[full(back)] * 2,
         ),
         compiler_params=params(20),

time: 113 us -> 114 us (level)
  blocking collectives: 45.6 us -> 26.6 us
  waiting for transfers between devices: 22.9 us -> 31.3 us
  starting transfers between devices: 31.5 us -> 39 us
  local copies, waits for them, and re-layouts: 0.03 us -> 2.11 us
  Pallas kernels: 11.5 us -> 12.9 us
    all_to_all x3 -> x2, blocking collectives: 45.6 us -> 26.6 us  [swap(): return lax.all_to_all(array, axis, 0, 0, tiled=True)]
    all_to_all x2 -> x3, starting transfers between devices: 14.1 us -> 28.1 us  [swap(): return lax.all_to_all(array, axis, 0, 0, tiled=True)]
    all_to_all x2 -> x3, waiting for transfers between devices: 21.6 us -> 30 us  [swap(): return lax.all_to_all(array, axis, 0, 0, tiled=True)]
    ppermute x3, starting transfers between devices: 17.4 us -> 10.9 us  [sibling(): return lax.ppermute(array, 'c', ((0, 1), (1, 0)))]
    unnamed x10 -> x14, local copies, waits for them, and re-layouts: 0.03 us -> 2.11 us
    pallas_call x1 -> x2, Pallas kernels: 4.6 us -> 6.09 us  [the longest x1 3.42 us: body(): pl.pallas_call(second_kernel, out_shape=(pltpu.HBM(many, BF16), shape(par...]
  transfers between devices with their start and end apart: 5 -> 6, of which waited for: 3 -> 4; matrix products, arithmetic and copies ran while one was open for 0% -> 0% of each run, Pallas kernels for 3% -> 4%
where the time goes in v5:
time: 114 us; the launch traced here: 113 us
  starting transfers between devices  39 us (34%)
  waiting for transfers between devices  31.3 us (27%)
  blocking collectives  26.6 us (23%)
  Pallas kernels  12.9 us (11%)
  local copies, waits for them, and re-layouts  2.11 us (2%)
  between operations  1.45 us (1%)
    all_to_all x3, waiting for transfers between devices, swap(): return lax.all_to_all(array, axis, 0, 0, tiled=True)  30 us
    all_to_all x3, starting transfers between devices, swap(): return lax.all_to_all(array, axis, 0, 0, tiled=True)  28.1 us
    all_to_all x2, blocking collectives, swap(): return lax.all_to_all(array, axis, 0, 0, tiled=True)  26.6 us
    ppermute x3, starting transfers between devices, sibling(): return lax.ppermute(array, 'c', ((0, 1), (1, 0)))  10.9 us
    pallas_call x1, Pallas kernels, body(): pl.pallas_call(second_kernel, out_shape=(pltpu.HBM(many, BF16), shape(par...  3.42 us
    pallas_call x1, Pallas kernels, body(): pl.pallas_call(first_kernel, out_shape=(pltpu.HBM(many, BF16), shape(rest...  2.66 us
  transfers between devices with their start and end apart: 6, of which 4 were waited for; matrix products, arithmetic and copies ran while one was open for 0% of the time, Pallas kernels for 4%

profile of v5, /device:TPU:1, one launch (start us, length us, event | category | flops | bytes accessed | tf_op | source)
XLA Modules:
  0.0 113.3 jit_solution(10227540270113652131)
XLA Ops:
  1.3 2.0 %shard_map.120 = bf16[4,272,256]{2,1,0:T(8,128)(2,1)} custom-call(s32[1,1]{1,0:T(1,128)S(6)} %copy.13.refs_0_.counts, bf16[256,256]{1,0:T(8,128)(2,1)} %bitcast.8, s32[1,256]{1,0:T(1,128)} %occupancy.1, bf16[8,1024]{1,0:T(8,128)(2,1)} %bitcast.11, bf16[8,1024]{1,0:T(8,128)(2,1)} %bitcast.12, f32[8,8]{1,0:T(8,128)} %bitcast.13), custom_call_target="tpu_custom_call" | custom-call | tf_op jit(solution)/shard_map/pallas_call | solution.py:316
  3.3 0.0 copy-start
  3.3 0.0 copy-start.1
  3.4 0.0 copy-start.2
  3.4 12.1 %all_to_all.25.got.mine = bf16[4,272,256]{2,1,0:T(8,128)(2,1)S(1)} all-to-all(bf16[4,272,256]{2,1,0:T(8,128)(2,1)} %shard_map.120), channel_id=1, replica_groups=mesh['z'=8,'x'=4,'c'=2,'y'=8] {'x'}, dimensions={0} | all-to-all | bytes 1114112 | tf_op jit(solution)/shard_map/all_to_all | solution.py:287
  15.5 0.7 shard_map.121
  16.2 14.0 %all-to-all-start.1 = ((bf16[16,32,256]{2,1,0:T(8,128)(2,1)}), bf16[16,32,256]{2,1,0:T(8,128)(2,1)S(1)}, u32[]{:S(2)}, u32[]{:S(2)}) async-start(bf16[16,32,256]{2,1,0:T(8,128)(2,1)} %shard_map.121), calls=%async_computation.1 | async-start | bytes 524288 | tf_op jit(solution)/shard_map/all_to_all | solution.py:287
  30.2 2.0 %collective-permute-start = (bf16[4,272,256]{2,1,0:T(8,128)(2,1)S(1)}, bf16[4,272,256]{2,1,0:T(8,128)(2,1)S(1)}, u32[]{:S(2)}, u32[]{:S(2)}) collective-permute-start(bf16[4,272,256]{2,1,0:T(8,128)(2,1)S(1)} %all_to_all.25.got.mine), channel_id=1, source_target_pairs={{0,8},{8,0},{1,9},{9,1},{2,10},{10,2},{3,11},{11,3},{4,12},{12,4},... | collective-permute-start | bytes 1671176 | tf_op jit(solution)/shard_map/ppermute | solution.py:295
  32.2 9.7 %all-to-all-done.1.got = bf16[16,32,256]{2,1,0:T(8,128)(2,1)S(1)} async-done(((bf16[16,32,256]{2,1,0:T(8,128)(2,1)}), bf16[16,32,256]{2,1,0:T(8,128)(2,1)S(1)}, u32[]{:S(2)}, u32[]{:S(2)}) %all-to-all-start.1) | async-done | bytes 262176 | tf_op jit(solution)/shard_map/all_to_all | solution.py:287
  41.9 0.0 copy-done
  41.9 0.0 copy-done.1
  41.9 0.0 copy-done.2
  41.9 2.7 %shard_map.122 = (bf16[1024,256]{1,0:T(8,128)(2,1)}, bf16[512,128]{1,0:T(8,128)(2,1)S(1)}, f32[8,512]{1,0:T(8,128)S(1)}, f32[128,512]{1,0:T(8,128)S(1)}, f32[256,256]{1,0:T(8,128)S(1)}) custom-call(s32[1]{0:T(128)} %bitcast.1.head, bf16[4,272,256]{2,1,0:T(8,128)(2,1)S(1)} %all_to_all.25.got.mine, bf16[16,32,256]{2,1,0:T(8,128)(2,1)S(1)} %all-to-all-done.1.got, ...), custom_call_target="tpu_custom_call" | custom-call | flops 738197504 | bytes 1048576 | tf_op jit(solution)/shard_map/pallas_call | solution.py:353
  44.6 0.0 collective-permute-done.other
  44.6 3.4 %shard_map.123 = (bf16[1024,256]{1,0:T(8,128)(2,1)}, bf16[64,8,256]{2,1,0:T(8,128)(2,1)}) custom-call(s32[1]{0:T(128)} %bitcast.1.head, bf16[4,272,256]{2,1,0:T(8,128)(2,1)S(1)} %collective-permute-done.other, bf16[512,128]{1,0:T(8,128)(2,1)S(1)} %get-tuple-element.24.grad_rows, f32[8,512]{1,0:T(8,128)S(1)} %get-tuple-element.25.lines, ...), custom_call_target="tpu_custom_call" | custom-call | flops 738197504 | bytes 1048576 | tf_op jit(solution)/shard_map/pallas_call | solution.py:366
  48.0 8.5 %all-to-all-start.2 = ((bf16[64,8,256]{2,1,0:T(8,128)(2,1)}), bf16[64,8,256]{2,1,0:T(8,128)(2,1)S(1)}, u32[]{:S(2)}, u32[]{:S(2)}) async-start(bf16[64,8,256]{2,1,0:T(8,128)(2,1)} %get-tuple-element.31), calls=%async_computation.2 | async-start | bytes 524288 | tf_op jit(solution)/shard_map/all_to_all | solution.py:287
  56.5 0.0 copy-start.3
  56.5 1.0 copy-done.3
  57.6 0.0 copy-start.4
  57.6 1.0 copy-done.4
  58.6 0.5 shard_map.124
  59.1 2.6 %collective-permute-start.1 = (bf16[4,256,256]{2,1,0:T(8,128)(2,1)S(1)}, bf16[4,256,256]{2,1,0:T(8,128)(2,1)S(1)}, u32[]{:S(2)}, u32[]{:S(2)}) collective-permute-start(bf16[4,256,256]{2,1,0:T(8,128)(2,1)S(1)} %get-tuple-element.30), channel_id=1, source_target_pairs={{0,8},{8,0},{1,9},{9,1},{2,10},{10,2},{3,11},{11,3},{4,12},{12,4},... | collective-permute-start | bytes 1572872 | tf_op jit(solution)/shard_map/ppermute | solution.py:295
  61.7 7.8 %all-to-all-done.2.got = bf16[64,8,256]{2,1,0:T(8,128)(2,1)S(1)} async-done(((bf16[64,8,256]{2,1,0:T(8,128)(2,1)}), bf16[64,8,256]{2,1,0:T(8,128)(2,1)S(1)}, u32[]{:S(2)}, u32[]{:S(2)}) %all-to-all-start.2) | async-done | bytes 262176 | tf_op jit(solution)/shard_map/all_to_all | solution.py:287
  69.5 0.8 shard_map.125
  70.3 5.6 %all-to-all-start.3 = ((bf16[64,8,256]{2,1,0:T(8,128)(2,1)}), bf16[64,8,256]{2,1,0:T(8,128)(2,1)S(1)}, u32[]{:S(2)}, u32[]{:S(2)}) async-start(bf16[64,8,256]{2,1,0:T(8,128)(2,1)} %shard_map.125), calls=%async_computation.3 | async-start | bytes 524288 | tf_op jit(solution)/shard_map/all_to_all | solution.py:287
  75.9 0.0 collective-permute-done.1.theirs
  75.9 12.5 %all-to-all-done.3.got = bf16[64,8,256]{2,1,0:T(8,128)(2,1)S(1)} async-done(((bf16[64,8,256]{2,1,0:T(8,128)(2,1)}), bf16[64,8,256]{2,1,0:T(8,128)(2,1)S(1)}, u32[]{:S(2)}, u32[]{:S(2)}) %all-to-all-start.3) | async-done | bytes 262176 | tf_op jit(solution)/shard_map/all_to_all | solution.py:287
  88.4 0.1 shard_map.126
  88.5 0.0 copy-start.5
  88.5 0.0 copy-start.6
  88.6 14.5 %all_to_all.26.got = bf16[4,528,256]{2,1,0:T(8,128)(2,1)S(1)} all-to-all(bf16[4,528,256]{2,1,0:T(8,128)(2,1)S(1)} %shard_map.126), channel_id=1, replica_groups=mesh['z'=8,'x'=4,'c'=2,'y'=8] {'x'}, dimensions={0} | all-to-all | bytes 2162688 | tf_op jit(solution)/shard_map/all_to_all | solution.py:287
  103.1 6.3 %collective-permute-start.2 = (bf16[4,528,256]{2,1,0:T(8,128)(2,1)S(1)}, bf16[4,528,256]{2,1,0:T(8,128)(2,1)S(1)}, u32[]{:S(2)}, u32[]{:S(2)}) collective-permute-start(bf16[4,528,256]{2,1,0:T(8,128)(2,1)S(1)} %all_to_all.26.got), channel_id=1, source_target_pairs={{0,8},{8,0},{1,9},{9,1},{2,10},{10,2},{3,11},{11,3},{4,12},{12,4},... | collective-permute-start | bytes 3244040 | tf_op jit(solution)/shard_map/ppermute | solution.py:295
  109.4 0.0 copy-done.5
  109.4 0.0 copy-done.6
  109.4 1.0 shard_map.127
  110.4 1.3 %collective-permute-done.2.other = bf16[4,528,256]{2,1,0:T(8,128)(2,1)S(1)} collective-permute-done((bf16[4,528,256]{2,1,0:T(8,128)(2,1)S(1)}, bf16[4,528,256]{2,1,0:T(8,128)(2,1)S(1)}, u32[]{:S(2)}, u32[]{:S(2)}) %collective-permute-start.2) | collective-permute-done | bytes 1081376 | tf_op jit(solution)/shard_map/ppermute | solution.py:295
  111.7 1.6 %shard_map.128 = (f32[8,1024]{1,0:T(8,128)}, f32[256,1024]{1,0:T(8,128)}, f32[256,1024]{1,0:T(8,128)}) custom-call(s32[1]{0:T(128)} %bitcast.2.core, bf16[4,528,256]{2,1,0:T(8,128)(2,1)S(1)} %all_to_all.26.got, bf16[4,528,256]{2,1,0:T(8,128)(2,1)S(1)} %collective-permute-done.2.other), custom_call_target="tpu_custom_call" | custom-call | tf_op jit(solution)/shard_map/pallas_call | solution.py:420
Async XLA Ops:
  3.3 38.6 %copy-start = (bf16[256,1024]{1,0:T(8,128)(2,1)S(1)}, bf16[256,1024]{1,0:T(8,128)(2,1)}, u32[]{:S(2)}) copy-start(bf16[256,1024]{1,0:T(8,128)(2,1)} %w_key.5) | copy-start | bytes 1572868
  3.3 38.6 %copy-start.1 = (bf16[256,1024]{1,0:T(8,128)(2,1)S(1)}, bf16[256,1024]{1,0:T(8,128)(2,1)}, u32[]{:S(2)}) copy-start(bf16[256,1024]{1,0:T(8,128)(2,1)} %w_value.5) | copy-start | bytes 1572868
  3.4 38.5 %copy-start.2 = (bf16[512,1024]{1,0:T(8,128)(2,1)S(1)}, bf16[512,1024]{1,0:T(8,128)(2,1)}, u32[]{:S(2)}) copy-start(bf16[512,1024]{1,0:T(8,128)(2,1)} %query.3) | copy-start | bytes 3145732
  16.2 25.7 %all-to-all-start.1 = ((bf16[16,32,256]{2,1,0:T(8,128)(2,1)}), bf16[16,32,256]{2,1,0:T(8,128)(2,1)S(1)}, u32[]{:S(2)}, u32[]{:S(2)}) async-start(bf16[16,32,256]{2,1,0:T(8,128)(2,1)} %shard_map.121), calls=%async_computation.1 | async-start | bytes 524288 | tf_op jit(solution)/shard_map/all_to_all | solution.py:287
  30.2 14.4 %collective-permute-start = (bf16[4,272,256]{2,1,0:T(8,128)(2,1)S(1)}, bf16[4,272,256]{2,1,0:T(8,128)(2,1)S(1)}, u32[]{:S(2)}, u32[]{:S(2)}) collective-permute-start(bf16[4,272,256]{2,1,0:T(8,128)(2,1)S(1)} %all_to_all.25.got.mine), channel_id=1, source_target_pairs={{0,8},{8,0},{1,9},{9,1},{2,10},{10,2},{3,11},{11,3},{4,12},{12,4},... | collective-permute-start | bytes 1671176 | tf_op jit(solution)/shard_map/ppermute | solution.py:295
  48.0 21.5 %all-to-all-start.2 = ((bf16[64,8,256]{2,1,0:T(8,128)(2,1)}), bf16[64,8,256]{2,1,0:T(8,128)(2,1)S(1)}, u32[]{:S(2)}, u32[]{:S(2)}) async-start(bf16[64,8,256]{2,1,0:T(8,128)(2,1)} %get-tuple-element.31), calls=%async_computation.2 | async-start | bytes 524288 | tf_op jit(solution)/shard_map/all_to_all | solution.py:287
  56.5 1.0 copy-start.3
  57.6 1.0 copy-start.4
  59.1 16.8 %collective-permute-start.1 = (bf16[4,256,256]{2,1,0:T(8,128)(2,1)S(1)}, bf16[4,256,256]{2,1,0:T(8,128)(2,1)S(1)}, u32[]{:S(2)}, u32[]{:S(2)}) collective-permute-start(bf16[4,256,256]{2,1,0:T(8,128)(2,1)S(1)} %get-tuple-element.30), channel_id=1, source_target_pairs={{0,8},{8,0},{1,9},{9,1},{2,10},{10,2},{3,11},{11,3},{4,12},{12,4},... | collective-permute-start | bytes 1572872 | tf_op jit(solution)/shard_map/ppermute | solution.py:295
  70.3 18.1 %all-to-all-start.3 = ((bf16[64,8,256]{2,1,0:T(8,128)(2,1)}), bf16[64,8,256]{2,1,0:T(8,128)(2,1)S(1)}, u32[]{:S(2)}, u32[]{:S(2)}) async-start(bf16[64,8,256]{2,1,0:T(8,128)(2,1)} %shard_map.125), calls=%async_computation.3 | async-start | bytes 524288 | tf_op jit(solution)/shard_map/all_to_all | solution.py:287
  88.5 20.9 %copy-start.5 = (bf16[1,256,256]{2,1,0:T(8,128)(2,1)S(1)}, bf16[1,256,256]{2,1,0:T(8,128)(2,1)}, u32[]{:S(2)}) copy-start(bf16[1,256,256]{2,1,0:T(8,128)(2,1)} %param.9) | copy-start | bytes 393220
  88.5 20.9 %copy-start.6 = (s32[1,256]{1,0:T(1,128)S(1)}, s32[1,256]{1,0:T(1,128)}, u32[]{:S(2)}) copy-start(s32[1,256]{1,0:T(1,128)} %occupancy.1) | copy-start | bytes 3076
  103.1 8.6 %collective-permute-start.2 = (bf16[4,528,256]{2,1,0:T(8,128)(2,1)S(1)}, bf16[4,528,256]{2,1,0:T(8,128)(2,1)S(1)}, u32[]{:S(2)}, u32[]{:S(2)}) collective-permute-start(bf16[4,528,256]{2,1,0:T(8,128)(2,1)S(1)} %all_to_all.26.got), channel_id=1, source_target_pairs={{0,8},{8,0},{1,9},{9,1},{2,10},{10,2},{3,11},{11,3},{4,12},{12,4},... | collective-permute-start | bytes 3244040 | tf_op jit(solution)/shard_map/ppermute | solution.py:295

commit v6 on v4

--- a/solution.py
+++ b/solution.py
@@ -48,6 +48,10 @@
         parts.append(part)
         column = column - part
     return parts
+
+
+def columns_of(head):
+    return pl.ds(pl.multiple_of(head[0] * HEAD, HEAD), HEAD)
 
 
 def pack_kernel(*refs):
@@ -117,8 +121,8 @@
 
 
 def share_kernel(head, keep, give, w_key, w_value, kept, given):
-    del head
-    weights = jnp.concatenate([w_key[...], w_value[...]], axis=1)
+    cols = columns_of(head)
+    weights = jnp.concatenate([w_key[:, cols], w_value[:, cols]], axis=1)
     for chip in range(keep.shape[0]):
         kept[chip] = mm(keep[chip], weights, 1, 1)
         given[chip] = mm(give[chip], weights, 1, 1).astype(BF16)
@@ -127,7 +131,7 @@
 def main_kernel(
     head, mine, other, got, query, w_key, w_value, keep, give, parts, query_sum, normals, grads
 ):
-    del head
+    cols = columns_of(head)
     chips, shard = keep.shape[0], keep.shape[1]
     scale = 1.0 / math.sqrt(HEAD)
     rows = latent_order(got, chips)
@@ -135,8 +139,8 @@
     extra = rows[:, HEAD:].T
     lse = (extra[0:1] + extra[1:2] + extra[2:3]) * LOG2E
     delta = extra[3:4] + extra[4:5] + extra[5:6]
-    queries = query[...]
-    weights = jnp.concatenate([w_key[...], w_value[...]], axis=1)
+    queries = query[:, cols]
+    weights = jnp.concatenate([w_key[:, cols], w_value[:, cols]], axis=1)
     per = BLOCK // shard
     for block in range(2 * chips // per):
         first = block * per
@@ -184,8 +188,15 @@
         sent[at] = total
 
 
-def gather_kernel(group, kept, theirs, got, sent):
-    chips, shard = kept.shape[0], kept.shape[1]
+def combine_kernel(chip, kept, theirs, *shares):
+    chips = kept.shape[0]
+    for ahead in range(chips):
+        at = lax.rem(chip[0] + ahead, chips)
+        shares[ahead][...] = (kept[at] + theirs[at].astype(F32)).astype(BF16)
+
+
+def gather_kernel(group, got, sent):
+    chips = sent.shape[0]
     halves = got.shape[0] // 2
     depth = halves * ROWS
     pieces = [got[at].astype(F32)[:, :HEAD] for at in range(2 * halves)]
@@ -193,19 +204,19 @@
         [jnp.concatenate(pieces[:halves], axis=0), jnp.concatenate(pieces[halves:], axis=0)], axis=1
     ).astype(BF16)
     for chip in range(chips):
-        sent[chip, :shard, :] = (kept[chip] + theirs[chip].astype(F32)).astype(BF16)
-        sent[chip, shard : shard + depth, :] = weights
+        sent[chip, :depth, :] = weights
         first = group[0] * 2 * chips + 2 * chip
         rows = [got[first + core].astype(F32) for core in range(2)]
-        sent[chip, shard + depth :, :] = jnp.concatenate(rows, axis=0).astype(BF16)
-
-
-def tokens_kernel(counts, got, tokens, occupancy, grad_tokens):
-    chips, (shard, width) = got.shape[0], tokens.shape
+        sent[chip, depth:, :] = jnp.concatenate(rows, axis=0).astype(BF16)
+
+
+def tokens_kernel(counts, *refs):
+    shares, (tokens, occupancy, grad_tokens) = refs[:-3], refs[-3:]
+    width = tokens.shape[1]
     normal, inverse = layer_norm(tokens[...].astype(F32))
-    grad_normal = got[0, :shard, :].astype(F32)
-    for chip in range(1, chips):
-        grad_normal += got[chip, :shard, :].astype(F32)
+    grad_normal = shares[0][...].astype(F32)
+    for share in shares[1:]:
+        grad_normal += share[...].astype(F32)
     live = live_rows(occupancy[...], counts[0, 0], width)
     grad_normal = jnp.where(live > 0.0, grad_normal, 0.0)
     grad_input = inverse * (
@@ -218,16 +229,14 @@
 
 def finish_kernel(core, got, other, query_rows, key_total, value_total):
     chips, depth, rows = got.shape[0], key_total.shape[0], query_rows.shape[0]
-    shard = got.shape[1] - depth - 2 * rows
-
     def write(low, high):
         for chip in range(chips):
             for at, source in ((2 * chip, low), (2 * chip + 1, high)):
                 cols = slice(at * HEAD, (at + 1) * HEAD)
-                both = source[chip, shard : shard + depth, :].astype(F32)
+                both = source[chip, :depth, :].astype(F32)
                 key_total[:, cols] = both[:, :HEAD]
                 value_total[:, cols] = both[:, HEAD:]
-                piece = source[chip, shard + depth :, :].astype(F32)
+                piece = source[chip, depth:, :].astype(F32)
                 both_rows = piece[:, HEAD:]
                 query_rows[:, cols] = jnp.where(core[0] == 0, both_rows[:rows], both_rows[rows:])
 
@@ -250,14 +259,6 @@
 
 def sibling(array):
     return lax.ppermute(array, "c", ((0, 1), (1, 0)))
-
-
-def full(dims):
-    return pl.BlockSpec(dims, lambda *_: (0,) * len(dims))
-
-
-def column(dims, at):
-    return pl.BlockSpec(dims, lambda step, heads: (0, heads[at]))
 
 
 def body(tokens, occupancy, counts, queries, saved_lse, grad_out, attn_out, w_key, w_value):
@@ -266,10 +267,10 @@
     latents, rows = queries.shape[0], grad.shape[0]
     chips, groups, windows = lax.axis_size("x"), lax.axis_size("z"), lax.axis_size("y")
     heads = lse.shape[1]
-    core = lax.axis_index("c").astype(jnp.int32)
-    head = (2 * lax.axis_index("x").astype(jnp.int32) + core).reshape(1)
-    core, group = core.reshape(1), lax.axis_index("z").astype(jnp.int32).reshape(1)
-    tokens, head, core, group = lax.optimization_barrier((tokens, head, core, group))
+    core, chip, group = (lax.axis_index(at).astype(jnp.int32) for at in ("c", "x", "z"))
+    head = (2 * chip + core).reshape(1)
+    core, chip, group = core.reshape(1), chip.reshape(1), group.reshape(1)
+    tokens, head, core, chip, group = lax.optimization_barrier((tokens, head, core, chip, group))
     sent = pl.pallas_call(
         pack_kernel,
         out_shape=shape((chips, shard + 2 * rows, width)),
@@ -293,40 +294,34 @@
 
     back = (chips, shard, width)
     part = (groups * windows, ROWS, width)
+    many = (2 * chips * shard, width)
     keep, give, parts = pl.pallas_call(
         main_kernel,
         out_shape=(shape(back), shape(back), shape(part)),
-        grid_spec=pltpu.PrefetchScalarGridSpec(
-            num_scalar_prefetch=1,
-            grid=(1,),
-            in_specs=[
-                full(got.shape),
-                full(other.shape),
-                full(grads.shape),
-                column((latents, HEAD), 0),
-                column((width, HEAD), 0),
-                column((width, HEAD), 0),
-            ],
-            out_specs=[full(back), full(back), full(part)],
-            scratch_shapes=[pltpu.VMEM((HEAD, latents), F32)]
-            + [pltpu.VMEM((2 * chips * shard, width), BF16)] * 2,
-        ),
+        in_specs=[SMEM] + [VMEM] * 6,
+        out_specs=(VMEM,) * 3,
+        scratch_shapes=[pltpu.VMEM((HEAD, latents), F32)] + [pltpu.VMEM(many, BF16)] * 2,
         compiler_params=params(40),
     )(head, got, other, grads, queries, w_key, w_value)
-
     kept, given = pl.pallas_call(
         share_kernel,
         out_shape=(shape(back, F32), shape(back)),
-        grid_spec=pltpu.PrefetchScalarGridSpec(
-            num_scalar_prefetch=1,
-            grid=(1,),
-            in_specs=[full(back)] * 2 + [column((width, HEAD), 0)] * 2,
-            out_specs=[full(back)] * 2,
-        ),
-        compiler_params=params(20),
+        in_specs=[SMEM] + [VMEM] * 4,
+        out_specs=(VMEM,) * 2,
+        compiler_params=params(16),
         cost_estimate=pl.CostEstimate(flops=270000000, bytes_accessed=3000000, transcendentals=0),
     )(head, keep, give, w_key, w_value)
-    theirs = sibling(given)
+    shares = pl.pallas_call(
+        combine_kernel,
+        out_shape=(shape((shard, width)),) * chips,
+        in_specs=[SMEM] + [VMEM] * 2,
+        out_specs=(VMEM,) * chips,
+        compiler_params=params(16),
+    )(chip, kept, sibling(given))
+    shares = [shares[0]] + [
+        lax.ppermute(share, "x", [(at, (at + ahead) % chips) for at in range(chips)])
+        for ahead, share in enumerate(shares[1:], 1)
+    ]
     parts = swap(parts, ("z", "y"))
     parts = pl.pallas_call(
         spread_kernel,
@@ -336,24 +331,25 @@
         compiler_params=params(8),
     )(parts)
     parts = swap(parts, ("z", "y"))
-    last = (chips, shard + width + 2 * rows, width)
+    last = (chips, width + 2 * rows, width)
     sent = pl.pallas_call(
         gather_kernel,
         out_shape=shape(last),
-        in_specs=[SMEM] + [VMEM] * 3,
-        out_specs=VMEM,
-        compiler_params=params(16),
-    )(group, kept, theirs, parts)
+        in_specs=[SMEM, VMEM],
+        out_specs=VMEM,
+        compiler_params=params(16),
+    )(group, parts)
+    sent, *shares = lax.optimization_barrier((sent, *shares))
     got = swap(sent, "x")
     other = sibling(got)
     grad_tokens = pl.pallas_call(
         tokens_kernel,
         out_shape=shape((shard, width)),
-        in_specs=[SMEM] + [VMEM] * 3,
+        in_specs=[SMEM] + [VMEM] * (chips + 2),
         out_specs=VMEM,
         compiler_params=params(16),
         cost_estimate=pl.CostEstimate(flops=2000000, bytes_accessed=1000000, transcendentals=256),
-    )(counts, got, tokens, occupancy)
+    )(counts, *shares, tokens, occupancy)
     query_rows, key_total, value_total = pl.pallas_call(
         finish_kernel,
         out_shape=(

time: 113 us -> 109 us (0.965)
  waiting for transfers between devices: 22.9 us -> 14 us
  starting transfers between devices: 31.5 us -> 40.2 us
  blocking collectives: 45.6 us -> 41 us
    all_to_all x2, waiting for transfers between devices: 21.6 us -> 12.9 us  [swap(): return lax.all_to_all(array, axis, 0, 0, tiled=True)]
    ppermute x0 -> x3, starting transfers between devices: none -> 8.6 us  [body(): lax.ppermute(share, 'x', [(at, (at + ahead) % chips) for at in range(chip...]
    all_to_all x3, blocking collectives: 45.6 us -> 41 us  [swap(): return lax.all_to_all(array, axis, 0, 0, tiled=True)]
  transfers between devices with their start and end apart: 5 -> 8, of which waited for: 3 -> 4; matrix products, arithmetic and copies ran while one was open for 0% -> 0% of each run, Pallas kernels for 3% -> 3%
where the time goes in v6:
time: 109 us; the launch traced here: 108 us
  blocking collectives  41 us (38%)
  starting transfers between devices  40.2 us (37%)
  waiting for transfers between devices  14 us (13%)
  Pallas kernels  11.5 us (11%)
  between operations  1.45 us (1%)
    all_to_all x3, blocking collectives, swap(): return lax.all_to_all(array, axis, 0, 0, tiled=True)  41 us
    ppermute x3, starting transfers between devices, sibling(): return lax.ppermute(array, 'c', ((0, 1), (1, 0)))  17.5 us
    all_to_all x2, starting transfers between devices, swap(): return lax.all_to_all(array, axis, 0, 0, tiled=True)  14.1 us
    all_to_all x2, waiting for transfers between devices, swap(): return lax.all_to_all(array, axis, 0, 0, tiled=True)  12.9 us
    ppermute x3, starting transfers between devices, body(): lax.ppermute(share, 'x', [(at, (at + ahead) % chips) for at in range(chip...  8.6 us
    pallas_call x1, Pallas kernels, body(): pl.pallas_call(main_kernel, out_shape=(shape(back), shape(back), shape(pa...  4.59 us
  transfers between devices with their start and end apart: 8, of which 4 were waited for; matrix products, arithmetic and copies ran while one was open for 0% of the time, Pallas kernels for 3%

profile of v6, /device:TPU:1, one launch (start us, length us, event | category | flops | bytes accessed | tf_op | source)
XLA Modules:
  0.0 108.0 jit_solution(16854813554161999197)
XLA Ops:
  1.3 2.0 %shard_map.120 = bf16[4,272,256]{2,1,0:T(8,128)(2,1)} custom-call(s32[1,1]{1,0:T(1,128)S(6)} %copy.13.refs_0_.counts, bf16[256,256]{1,0:T(8,128)(2,1)} %bitcast.9, s32[1,256]{1,0:T(1,128)} %refs_5_.1, bf16[8,1024]{1,0:T(8,128)(2,1)} %bitcast.12, bf16[8,1024]{1,0:T(8,128)(2,1)} %bitcast.13, f32[8,8]{1,0:T(8,128)} %bitcast.14), custom_call_target="tpu_custom_call" | custom-call | tf_op jit(solution)/shard_map/pallas_call | solution.py:274
  3.3 0.0 copy-start.2
  3.3 12.1 %all_to_all.25.got.mine = bf16[4,272,256]{2,1,0:T(8,128)(2,1)S(1)} all-to-all(bf16[4,272,256]{2,1,0:T(8,128)(2,1)} %shard_map.120), channel_id=1, replica_groups=mesh['z'=8,'x'=4,'c'=2,'y'=8] {'x'}, dimensions={0} | all-to-all | bytes 1114112 | tf_op jit(solution)/shard_map/all_to_all | solution.py:253
  15.4 0.0 copy-start
  15.4 0.0 copy-start.1
  15.4 8.7 %collective-permute-start = (bf16[4,272,256]{2,1,0:T(8,128)(2,1)S(1)}, bf16[4,272,256]{2,1,0:T(8,128)(2,1)S(1)}, u32[]{:S(2)}, u32[]{:S(2)}) collective-permute-start(bf16[4,272,256]{2,1,0:T(8,128)(2,1)S(1)} %all_to_all.25.got.mine), channel_id=1, source_target_pairs={{0,8},{8,0},{1,9},{9,1},{2,10},{10,2},{3,11},{11,3},{4,12},{12,4},... | collective-permute-start | bytes 1671176 | tf_op jit(solution)/shard_map/ppermute | solution.py:261
  24.1 19.0 %all_to_all.26.got = bf16[16,32,256]{2,1,0:T(8,128)(2,1)S(1)} all-to-all(bf16[16,32,256]{2,1,0:T(8,128)(2,1)S(1)} %shard_map.121), channel_id=1, replica_groups=mesh['z'=8,'x'=4,'c'=2,'y'=8] {'z','c'}, dimensions={0} | all-to-all | bytes 524288 | tf_op jit(solution)/shard_map/all_to_all | solution.py:253
  43.1 0.0 collective-permute-done.other
  43.1 0.0 copy-done.2
  43.1 0.0 copy-done
  43.1 0.0 copy-done.1
  43.1 4.6 %shard_map.122 = (bf16[4,256,256]{2,1,0:T(8,128)(2,1)S(1)}, bf16[4,256,256]{2,1,0:T(8,128)(2,1)S(1)}, bf16[64,8,256]{2,1,0:T(8,128)(2,1)}) custom-call(s32[1]{0:T(128)} %bitcast.1.head, bf16[4,272,256]{2,1,0:T(8,128)(2,1)S(1)} %all_to_all.25.got.mine, bf16[4,272,256]{2,1,0:T(8,128)(2,1)S(1)} %collective-permute-done.other, ...), custom_call_target="tpu_custom_call" | custom-call | tf_op jit(solution)/shard_map/pallas_call | solution.py:298
  47.7 8.5 %all-to-all-start.2 = ((bf16[64,8,256]{2,1,0:T(8,128)(2,1)}), bf16[64,8,256]{2,1,0:T(8,128)(2,1)S(1)}, u32[]{:S(2)}, u32[]{:S(2)}) async-start(bf16[64,8,256]{2,1,0:T(8,128)(2,1)} %get-tuple-element.29), calls=%async_computation.2 | async-start | bytes 524288 | tf_op jit(solution)/shard_map/all_to_all | solution.py:253
  56.2 1.3 %shard_map.125 = (f32[4,256,256]{2,1,0:T(8,128)S(1)}, bf16[4,256,256]{2,1,0:T(8,128)(2,1)}) custom-call(s32[1]{0:T(128)} %bitcast.1.head, bf16[4,256,256]{2,1,0:T(8,128)(2,1)S(1)} %get-tuple-element.31.keep, bf16[4,256,256]{2,1,0:T(8,128)(2,1)S(1)} %get-tuple-element.32.give, bf16[256,1024]{1,0:T(8,128)(2,1)S(1)} %copy-done, bf16[256,1024]{1,0:T(8,128)(2,1)S(1)} %copy-done.1), custom_call_target="tpu_custom_call" | custom-call | flops 270000000 | bytes 3000000 | tf_op jit(solution)/shard_map/pallas_call | solution.py:306
  57.5 2.6 %collective-permute-start.1 = (bf16[4,256,256]{2,1,0:T(8,128)(2,1)}, bf16[4,256,256]{2,1,0:T(8,128)(2,1)S(1)}, u32[]{:S(2)}, u32[]{:S(2)}) collective-permute-start(bf16[4,256,256]{2,1,0:T(8,128)(2,1)} %get-tuple-element.34), channel_id=1, source_target_pairs={{0,8},{8,0},{1,9},{9,1},{2,10},{10,2},{3,11},{11,3},{4,12},{12,4},... | collective-permute-start | bytes 1572872 | tf_op jit(solution)/shard_map/ppermute | solution.py:261
  60.1 9.2 %all-to-all-done.2.got = bf16[64,8,256]{2,1,0:T(8,128)(2,1)S(1)} async-done(((bf16[64,8,256]{2,1,0:T(8,128)(2,1)}), bf16[64,8,256]{2,1,0:T(8,128)(2,1)S(1)}, u32[]{:S(2)}, u32[]{:S(2)}) %all-to-all-start.2) | async-done | bytes 262176 | tf_op jit(solution)/shard_map/all_to_all | solution.py:253
  69.2 0.8 shard_map.123
  70.0 5.6 %all-to-all-start.3 = ((bf16[64,8,256]{2,1,0:T(8,128)(2,1)}), bf16[64,8,256]{2,1,0:T(8,128)(2,1)S(1)}, u32[]{:S(2)}, u32[]{:S(2)}) async-start(bf16[64,8,256]{2,1,0:T(8,128)(2,1)} %shard_map.123), calls=%async_computation.3 | async-start | bytes 524288 | tf_op jit(solution)/shard_map/all_to_all | solution.py:253
  75.6 0.0 collective-permute-done.1.theirs
  75.6 0.1 shard_map.126
  75.7 2.2 %collective-permute-start.2 = (bf16[256,256]{1,0:T(8,128)(2,1)S(1)}, bf16[256,256]{1,0:T(8,128)(2,1)S(1)}, u32[]{:S(2)}, u32[]{:S(2)}) collective-permute-start(bf16[256,256]{1,0:T(8,128)(2,1)S(1)} %get-tuple-element.36), channel_id=1, source_target_pairs={{0,16},{16,32},{32,48},{48,0},{1,17},{17,33},{33,49},{49,1},{2,18}... | collective-permute-start | bytes 393224 | tf_op jit(solution)/shard_map/ppermute | solution.py:322
  77.9 3.7 %collective-permute-start.3 = (bf16[256,256]{1,0:T(8,128)(2,1)S(1)}, bf16[256,256]{1,0:T(8,128)(2,1)S(1)}, u32[]{:S(2)}, u32[]{:S(2)}) collective-permute-start(bf16[256,256]{1,0:T(8,128)(2,1)S(1)} %get-tuple-element.37), channel_id=1, source_target_pairs={{0,32},{16,48},{32,0},{48,16},{1,33},{17,49},{33,1},{49,17},{2,34}... | collective-permute-start | bytes 393224 | tf_op jit(solution)/shard_map/ppermute | solution.py:322
  81.6 2.7 %collective-permute-start.4 = (bf16[256,256]{1,0:T(8,128)(2,1)S(1)}, bf16[256,256]{1,0:T(8,128)(2,1)S(1)}, u32[]{:S(2)}, u32[]{:S(2)}) collective-permute-start(bf16[256,256]{1,0:T(8,128)(2,1)S(1)} %get-tuple-element.38), channel_id=1, source_target_pairs={{0,48},{16,0},{32,16},{48,32},{1,49},{17,1},{33,17},{49,33},{2,50}... | collective-permute-start | bytes 393224 | tf_op jit(solution)/shard_map/ppermute | solution.py:322
  84.4 3.8 %all-to-all-done.3.got = bf16[64,8,256]{2,1,0:T(8,128)(2,1)S(1)} async-done(((bf16[64,8,256]{2,1,0:T(8,128)(2,1)}), bf16[64,8,256]{2,1,0:T(8,128)(2,1)S(1)}, u32[]{:S(2)}, u32[]{:S(2)}) %all-to-all-start.3) | async-done | bytes 262176 | tf_op jit(solution)/shard_map/all_to_all | solution.py:253
  88.2 0.0 collective-permute-done.2.refs_1_
  88.2 0.0 collective-permute-done.3.refs_2_
  88.2 0.5 collective-permute-done.4.refs_3_
  88.7 0.0 copy-start.3
  88.7 0.0 copy-start.4
  88.7 9.9 %all_to_all.27.got = bf16[4,272,256]{2,1,0:T(8,128)(2,1)S(1)} all-to-all(bf16[4,272,256]{2,1,0:T(8,128)(2,1)S(1)} %shard_map.124), channel_id=1, replica_groups=mesh['z'=8,'x'=4,'c'=2,'y'=8] {'x'}, dimensions={0} | all-to-all | bytes 1114112 | tf_op jit(solution)/shard_map/all_to_all | solution.py:253
  98.6 6.3 %collective-permute-start.5 = (bf16[4,272,256]{2,1,0:T(8,128)(2,1)S(1)}, bf16[4,272,256]{2,1,0:T(8,128)(2,1)S(1)}, u32[]{:S(2)}, u32[]{:S(2)}) collective-permute-start(bf16[4,272,256]{2,1,0:T(8,128)(2,1)S(1)} %all_to_all.27.got), channel_id=1, source_target_pairs={{0,8},{8,0},{1,9},{9,1},{2,10},{10,2},{3,11},{11,3},{4,12},{12,4},... | collective-permute-start | bytes 1671176 | tf_op jit(solution)/shard_map/ppermute | solution.py:261
  104.9 0.0 copy-done.3
  104.9 0.0 copy-done.4
  104.9 1.0 shard_map.127
  105.9 0.5 collective-permute-done.5.other
  106.4 1.6 %shard_map.128 = (f32[8,1024]{1,0:T(8,128)}, f32[256,1024]{1,0:T(8,128)}, f32[256,1024]{1,0:T(8,128)}) custom-call(s32[1]{0:T(128)} %bitcast.2.core, bf16[4,272,256]{2,1,0:T(8,128)(2,1)S(1)} %all_to_all.27.got, bf16[4,272,256]{2,1,0:T(8,128)(2,1)S(1)} %collective-permute-done.5.other), custom_call_target="tpu_custom_call" | custom-call | tf_op jit(solution)/shard_map/pallas_call | solution.py:353
  (2 shorter events, 0.1 us)
Async XLA Ops:
  3.3 39.8 %copy-start.2 = (bf16[512,1024]{1,0:T(8,128)(2,1)S(1)}, bf16[512,1024]{1,0:T(8,128)(2,1)}, u32[]{:S(2)}) copy-start(bf16[512,1024]{1,0:T(8,128)(2,1)} %query.1) | copy-start | bytes 3145732
  15.4 27.7 %copy-start = (bf16[256,1024]{1,0:T(8,128)(2,1)S(1)}, bf16[256,1024]{1,0:T(8,128)(2,1)}, u32[]{:S(2)}) copy-start(bf16[256,1024]{1,0:T(8,128)(2,1)} %w_key.3) | copy-start | bytes 1572868
  15.4 27.7 %copy-start.1 = (bf16[256,1024]{1,0:T(8,128)(2,1)S(1)}, bf16[256,1024]{1,0:T(8,128)(2,1)}, u32[]{:S(2)}) copy-start(bf16[256,1024]{1,0:T(8,128)(2,1)} %w_value.3) | copy-start | bytes 1572868
  15.4 27.7 %collective-permute-start = (bf16[4,272,256]{2,1,0:T(8,128)(2,1)S(1)}, bf16[4,272,256]{2,1,0:T(8,128)(2,1)S(1)}, u32[]{:S(2)}, u32[]{:S(2)}) collective-permute-start(bf16[4,272,256]{2,1,0:T(8,128)(2,1)S(1)} %all_to_all.25.got.mine), channel_id=1, source_target_pairs={{0,8},{8,0},{1,9},{9,1},{2,10},{10,2},{3,11},{11,3},{4,12},{12,4},... | collective-permute-start | bytes 1671176 | tf_op jit(solution)/shard_map/ppermute | solution.py:261
  47.7 21.5 %all-to-all-start.2 = ((bf16[64,8,256]{2,1,0:T(8,128)(2,1)}), bf16[64,8,256]{2,1,0:T(8,128)(2,1)S(1)}, u32[]{:S(2)}, u32[]{:S(2)}) async-start(bf16[64,8,256]{2,1,0:T(8,128)(2,1)} %get-tuple-element.29), calls=%async_computation.2 | async-start | bytes 524288 | tf_op jit(solution)/shard_map/all_to_all | solution.py:253
  57.5 18.1 %collective-permute-start.1 = (bf16[4,256,256]{2,1,0:T(8,128)(2,1)}, bf16[4,256,256]{2,1,0:T(8,128)(2,1)S(1)}, u32[]{:S(2)}, u32[]{:S(2)}) collective-permute-start(bf16[4,256,256]{2,1,0:T(8,128)(2,1)} %get-tuple-element.34), channel_id=1, source_target_pairs={{0,8},{8,0},{1,9},{9,1},{2,10},{10,2},{3,11},{11,3},{4,12},{12,4},... | collective-permute-start | bytes 1572872 | tf_op jit(solution)/shard_map/ppermute | solution.py:261
  70.0 18.1 %all-to-all-start.3 = ((bf16[64,8,256]{2,1,0:T(8,128)(2,1)}), bf16[64,8,256]{2,1,0:T(8,128)(2,1)S(1)}, u32[]{:S(2)}, u32[]{:S(2)}) async-start(bf16[64,8,256]{2,1,0:T(8,128)(2,1)} %shard_map.123), calls=%async_computation.3 | async-start | bytes 524288 | tf_op jit(solution)/shard_map/all_to_all | solution.py:253
  75.7 12.4 %collective-permute-start.2 = (bf16[256,256]{1,0:T(8,128)(2,1)S(1)}, bf16[256,256]{1,0:T(8,128)(2,1)S(1)}, u32[]{:S(2)}, u32[]{:S(2)}) collective-permute-start(bf16[256,256]{1,0:T(8,128)(2,1)S(1)} %get-tuple-element.36), channel_id=1, source_target_pairs={{0,16},{16,32},{32,48},{48,0},{1,17},{17,33},{33,49},{49,1},{2,18}... | collective-permute-start | bytes 393224 | tf_op jit(solution)/shard_map/ppermute | solution.py:322
  77.9 10.2 %collective-permute-start.3 = (bf16[256,256]{1,0:T(8,128)(2,1)S(1)}, bf16[256,256]{1,0:T(8,128)(2,1)S(1)}, u32[]{:S(2)}, u32[]{:S(2)}) collective-permute-start(bf16[256,256]{1,0:T(8,128)(2,1)S(1)} %get-tuple-element.37), channel_id=1, source_target_pairs={{0,32},{16,48},{32,0},{48,16},{1,33},{17,49},{33,1},{49,17},{2,34}... | collective-permute-start | bytes 393224 | tf_op jit(solution)/shard_map/ppermute | solution.py:322
  81.6 7.0 %collective-permute-start.4 = (bf16[256,256]{1,0:T(8,128)(2,1)S(1)}, bf16[256,256]{1,0:T(8,128)(2,1)S(1)}, u32[]{:S(2)}, u32[]{:S(2)}) collective-permute-start(bf16[256,256]{1,0:T(8,128)(2,1)S(1)} %get-tuple-element.38), channel_id=1, source_target_pairs={{0,48},{16,0},{32,16},{48,32},{1,49},{17,1},{33,17},{49,33},{2,50}... | collective-permute-start | bytes 393224 | tf_op jit(solution)/shard_map/ppermute | solution.py:322
  88.7 16.2 %copy-start.3 = (bf16[1,256,256]{2,1,0:T(8,128)(2,1)S(1)}, bf16[1,256,256]{2,1,0:T(8,128)(2,1)}, u32[]{:S(2)}) copy-start(bf16[1,256,256]{2,1,0:T(8,128)(2,1)} %param.9) | copy-start | bytes 393220
  88.7 16.2 %copy-start.4 = (s32[1,256]{1,0:T(1,128)S(1)}, s32[1,256]{1,0:T(1,128)}, u32[]{:S(2)}) copy-start(s32[1,256]{1,0:T(1,128)} %refs_5_.1) | copy-start | bytes 3076
  98.6 7.8 %collective-permute-start.5 = (bf16[4,272,256]{2,1,0:T(8,128)(2,1)S(1)}, bf16[4,272,256]{2,1,0:T(8,128)(2,1)S(1)}, u32[]{:S(2)}, u32[]{:S(2)}) collective-permute-start(bf16[4,272,256]{2,1,0:T(8,128)(2,1)S(1)} %all_to_all.27.got), channel_id=1, source_target_pairs={{0,8},{8,0},{1,9},{9,1},{2,10},{10,2},{3,11},{11,3},{4,12},{12,4},... | collective-permute-start | bytes 1671176 | tf_op jit(solution)/shard_map/ppermute | solution.py:261

commit v7 on v6

--- a/solution.py
+++ b/solution.py
@@ -15,6 +15,7 @@
 LOG2E = math.log2(math.e)
 F32, BF16 = jnp.float32, jnp.bfloat16
 VMEM = pl.BlockSpec(memory_space=pltpu.VMEM)
+HBM = pl.BlockSpec(memory_space=pltpu.HBM)
 SMEM = pl.BlockSpec(memory_space=pltpu.SMEM)
 
 
@@ -55,118 +56,74 @@
 
 
 def pack_kernel(*refs):
-    sources, sent, (counts, tokens, occupancy, grad, out, lse), done = (
-        refs[:6],
-        refs[6],
-        refs[7:13],
-        refs[13],
-    )
+    sources, (masked, sent), held, done = refs[:6], refs[6:8], refs[8:14], refs[14]
     copies = [
         pltpu.make_async_copy(source, target, done.at[at])
-        for at, (source, target) in enumerate(zip(sources, refs[7:13]))
+        for at, (source, target) in enumerate(zip(sources, held))
     ]
     for copy in copies:
         copy.start()
     for copy in copies:
         copy.wait()
-    chips, (shard, width) = sent.shape[0], tokens.shape
-    live = live_rows(occupancy[...], counts[0, 0], width)
-    masked = jnp.where(live > 0.0, tokens[...].astype(F32), 0.0).astype(BF16)
-    rows = grad.shape[0]
+    counts, tokens, occupancy, grad, out, lse = held
+    live = live_rows(occupancy[...], counts[0, 0], tokens.shape[1])
+    masked[...] = jnp.where(live > 0.0, tokens[...].astype(F32), 0.0).astype(BF16)
+    rows, heads = grad.shape[0], lse.shape[1]
     lane = lax.broadcasted_iota(jnp.int32, (rows, HEAD), 1)
-    for chip in range(chips):
-        sent[chip, :shard, :] = masked
-        extras, grads = [], []
-        for head in (2 * chip, 2 * chip + 1):
-            cols = slice(head * HEAD, (head + 1) * HEAD)
-            grad_f32 = grad[:, cols].astype(F32)
-            delta = jnp.sum(grad_f32 * out[:, cols].astype(F32), axis=1, keepdims=True)
-            extra = jnp.zeros((rows, HEAD), F32)
-            for at, part in enumerate(three_parts(lse[:, head : head + 1]) + three_parts(delta)):
-                extra = jnp.where(lane == at, part, extra)
-            extras.append(extra)
-            grads.append(grad_f32)
-        both = jnp.concatenate(
-            [jnp.concatenate(grads, axis=1), jnp.concatenate(extras, axis=1)], axis=0
-        )
-        sent[chip, shard:, :] = both.astype(BF16)
-
-
-def turn_kernel(got, sent):
-    chips, width = got.shape[0], got.shape[2]
-    shard = got.shape[1] - sent.shape[1] // chips * 2
-    pieces = [got[chip, shard:, :].astype(F32) for chip in range(chips)]
-    rows = sent.shape[1] // chips
-    grads = jnp.concatenate([piece[:rows] for piece in pieces], axis=0)
-    extras = jnp.concatenate([piece[rows:] for piece in pieces], axis=0)
-    for core in range(2):
-        cols = slice(core * HEAD, (core + 1) * HEAD)
-        both = jnp.concatenate([grads[:, cols], extras[:, cols]], axis=1).astype(BF16)
-        for group in range(sent.shape[0] // 2):
-            sent[2 * group + core] = both
-
-
-def latent_order(got, chips):
-    rows = got.shape[1] // chips
-    blocks = [got[at].astype(F32) for at in range(got.shape[0])]
-    return jnp.concatenate(
-        [
-            blocks[2 * group + core][chip * rows : (chip + 1) * rows]
-            for group in range(got.shape[0] // 2)
-            for chip in range(chips)
-            for core in range(2)
-        ],
-        axis=0,
-    )
+    for head in range(heads):
+        cols = slice(head * HEAD, (head + 1) * HEAD)
+        grad_f32 = grad[:, cols].astype(F32)
+        delta = jnp.sum(grad_f32 * out[:, cols].astype(F32), axis=1, keepdims=True)
+        extra = jnp.zeros((rows, HEAD), F32)
+        for at, part in enumerate(three_parts(lse[:, head : head + 1]) + three_parts(delta)):
+            extra = jnp.where(lane == at, part, extra)
+        both = jnp.concatenate([grad_f32, extra], axis=1).astype(BF16)
+        for group in range(sent.shape[0] // heads):
+            sent[group * heads + head] = both
+
+
+def normal_kernel(*refs):
+    blocks, normals = refs[:-1], refs[-1]
+    shard = blocks[0].shape[0]
+    for at, block in enumerate(blocks):
+        normal = layer_norm(block[...].astype(F32))[0].astype(BF16)
+        normals[at * shard : (at + 1) * shard, :] = normal
 
 
 def share_kernel(head, keep, give, w_key, w_value, kept, given):
     cols = columns_of(head)
     weights = jnp.concatenate([w_key[:, cols], w_value[:, cols]], axis=1)
-    for chip in range(keep.shape[0]):
-        kept[chip] = mm(keep[chip], weights, 1, 1)
-        given[chip] = mm(give[chip], weights, 1, 1).astype(BF16)
-
-
-def main_kernel(
-    head, mine, other, got, query, w_key, w_value, keep, give, parts, query_sum, normals, grads
-):
+    kept[...] = mm(keep[...], weights, 1, 1)
+    given[...] = mm(give[...], weights, 1, 1).astype(BF16)
+
+
+def main_kernel(head, mine, other, got, query, w_key, w_value, keep, give, parts, query_sum):
     cols = columns_of(head)
-    chips, shard = keep.shape[0], keep.shape[1]
     scale = 1.0 / math.sqrt(HEAD)
-    rows = latent_order(got, chips)
-    grad = rows[:, :HEAD].astype(BF16)
-    extra = rows[:, HEAD:].T
+    grad = got[:, :HEAD]
+    extra = got[:, HEAD:].astype(F32).T
     lse = (extra[0:1] + extra[1:2] + extra[2:3]) * LOG2E
     delta = extra[3:4] + extra[4:5] + extra[5:6]
     queries = query[:, cols]
     weights = jnp.concatenate([w_key[:, cols], w_value[:, cols]], axis=1)
-    per = BLOCK // shard
-    for block in range(2 * chips // per):
-        first = block * per
-        source, target = (mine, keep) if first < chips else (other, give)
-        spots = [(first + at) % chips for at in range(per)]
-        tokens = jnp.concatenate([source[spot, :shard, :] for spot in spots], axis=0)
-        normal = layer_norm(tokens.astype(F32))[0].astype(BF16)
-        both = jnp.dot(normal, weights, preferred_element_type=F32).astype(BF16)
-        keys, values = both[:, :HEAD], both[:, HEAD:]
-        probs = jnp.exp2(mm(keys, queries, 1, 1) * (scale * LOG2E) - lse)
-        grad_values = jnp.dot(probs.astype(BF16), grad, preferred_element_type=F32)
-        grad_probs = mm(values, grad, 1, 1)
-        grad_scores = (scale * probs * (grad_probs - delta)).astype(BF16)
-        grad_keys = jnp.dot(grad_scores, queries, preferred_element_type=F32)
-        grad_both = jnp.concatenate([grad_keys, grad_values], axis=1).astype(BF16)
-        for at, spot in enumerate(spots):
-            target[spot] = grad_both[at * shard : (at + 1) * shard]
-        query_part = mm(keys, grad_scores, 0, 0)
-        if block == 0:
-            query_sum[...] = query_part
-        else:
-            query_sum[...] += query_part
-        normals[block * BLOCK : (block + 1) * BLOCK, :] = normal
-        grads[block * BLOCK : (block + 1) * BLOCK, :] = grad_both
+    for source, target in ((mine, keep), (other, give)):
+        for start in range(0, source.shape[0], BLOCK):
+            rows = slice(start, start + BLOCK)
+            both = jnp.dot(source[rows, :], weights, preferred_element_type=F32).astype(BF16)
+            keys, values = both[:, :HEAD], both[:, HEAD:]
+            probs = jnp.exp2(mm(keys, queries, 1, 1) * (scale * LOG2E) - lse)
+            grad_values = jnp.dot(probs.astype(BF16), grad, preferred_element_type=F32)
+            grad_probs = mm(values, grad, 1, 1)
+            grad_scores = (scale * probs * (grad_probs - delta)).astype(BF16)
+            grad_keys = jnp.dot(grad_scores, queries, preferred_element_type=F32)
+            target[rows, :] = jnp.concatenate([grad_keys, grad_values], axis=1).astype(BF16)
+            query_part = mm(keys, grad_scores, 0, 0)
+            if source is mine and start == 0:
+                query_sum[...] = query_part
+            else:
+                query_sum[...] += query_part
+    totals = mm(mine[...], keep[...], 0, 0) + mm(other[...], give[...], 0, 0)
     turned = query_sum[...].T
-    totals = mm(normals[...], grads[...], 0, 0)
     halves = parts.shape[0] // 2
     for at in range(parts.shape[0]):
         start = at % halves * ROWS
@@ -188,11 +145,12 @@
         sent[at] = total
 
 
-def combine_kernel(chip, kept, theirs, *shares):
-    chips = kept.shape[0]
+def combine_kernel(kept, theirs, *shares):
+    chips, shard = len(shares), shares[0].shape[0]
     for ahead in range(chips):
-        at = lax.rem(chip[0] + ahead, chips)
-        shares[ahead][...] = (kept[at] + theirs[at].astype(F32)).astype(BF16)
+        at = (chips - ahead) % chips * shard
+        rows = slice(at, at + shard)
+        shares[ahead][...] = (kept[rows, :] + theirs[rows, :].astype(F32)).astype(BF16)
 
 
 def gather_kernel(group, got, sent):
@@ -261,6 +219,10 @@
     return lax.ppermute(array, "c", ((0, 1), (1, 0)))
 
 
+def along_x(array, ahead, chips):
+    return lax.ppermute(array, "x", [(at, (at + ahead) % chips) for at in range(chips)])
+
+
 def body(tokens, occupancy, counts, queries, saved_lse, grad_out, attn_out, w_key, w_value):
     tokens, grad, out, lse = tokens[0], grad_out[0], attn_out[0], saved_lse[0]
     shard, width = tokens.shape
@@ -269,40 +231,44 @@
     heads = lse.shape[1]
     core, chip, group = (lax.axis_index(at).astype(jnp.int32) for at in ("c", "x", "z"))
     head = (2 * chip + core).reshape(1)
-    core, chip, group = core.reshape(1), chip.reshape(1), group.reshape(1)
-    tokens, head, core, chip, group = lax.optimization_barrier((tokens, head, core, chip, group))
-    sent = pl.pallas_call(
+    core, group = core.reshape(1), group.reshape(1)
+    tokens, head, core, group = lax.optimization_barrier((tokens, head, core, group))
+    masked, sent = pl.pallas_call(
         pack_kernel,
-        out_shape=shape((chips, shard + 2 * rows, width)),
-        in_specs=[pl.BlockSpec(memory_space=pltpu.HBM)] * 6,
-        out_specs=VMEM,
+        out_shape=(shape((shard, width)), shape((groups * heads, rows, width))),
+        in_specs=[HBM] * 6,
+        out_specs=(VMEM, VMEM),
         scratch_shapes=[pltpu.SMEM(counts.shape, counts.dtype)]
         + [pltpu.VMEM(ref.shape, ref.dtype) for ref in (tokens, occupancy, grad, out, lse)]
         + [pltpu.SemaphoreType.DMA((6,))],
         compiler_params=params(60),
     )(counts, tokens, occupancy, grad, out, lse)
-    got = swap(sent, "x")
-    other = sibling(got)
-    grads = pl.pallas_call(
-        turn_kernel,
-        out_shape=shape((2 * groups, rows * chips, width)),
-        in_specs=[VMEM],
+    grads, masked, *blocks = lax.optimization_barrier(
+        (
+            swap(sent, ("z", "x", "c")),
+            masked,
+            *[along_x(masked, ahead, chips) for ahead in range(1, chips)],
+        )
+    )
+    back = (chips * shard, width)
+    normals = pl.pallas_call(
+        normal_kernel,
+        out_shape=shape(back),
+        in_specs=[VMEM] * chips,
         out_specs=VMEM,
         compiler_params=params(8),
-    )(got)
-    grads = swap(grads, ("z", "c"))
-
-    back = (chips, shard, width)
+    )(masked, *blocks)
+    other = sibling(normals)
+
     part = (groups * windows, ROWS, width)
-    many = (2 * chips * shard, width)
     keep, give, parts = pl.pallas_call(
         main_kernel,
         out_shape=(shape(back), shape(back), shape(part)),
         in_specs=[SMEM] + [VMEM] * 6,
         out_specs=(VMEM,) * 3,
-        scratch_shapes=[pltpu.VMEM((HEAD, latents), F32)] + [pltpu.VMEM(many, BF16)] * 2,
+        scratch_shapes=[pltpu.VMEM((HEAD, latents), F32)],
         compiler_params=params(40),
-    )(head, got, other, grads, queries, w_key, w_value)
+    )(head, normals, other, grads.reshape(latents, width), queries, w_key, w_value)
     kept, given = pl.pallas_call(
         share_kernel,
         out_shape=(shape(back, F32), shape(back)),
@@ -314,13 +280,12 @@
     shares = pl.pallas_call(
         combine_kernel,
         out_shape=(shape((shard, width)),) * chips,
-        in_specs=[SMEM] + [VMEM] * 2,
+        in_specs=[VMEM] * 2,
         out_specs=(VMEM,) * chips,
         compiler_params=params(16),
-    )(chip, kept, sibling(given))
+    )(kept, sibling(given))
     shares = [shares[0]] + [
-        lax.ppermute(share, "x", [(at, (at + ahead) % chips) for at in range(chips)])
-        for ahead, share in enumerate(shares[1:], 1)
+        along_x(share, ahead, chips) for ahead, share in enumerate(shares[1:], 1)
     ]
     parts = swap(parts, ("z", "y"))
     parts = pl.pallas_call(

time: 109 us -> 110 us (level)
  blocking collectives: 41 us -> 9.98 us
  starting transfers between devices: 40.2 us -> 62.8 us
  waiting for transfers between devices: 14 us -> 21.8 us
  local copies, waits for them, and re-layouts: 0.02 us -> 1.26 us
    all_to_all x3 -> x1, blocking collectives: 41 us -> 9.98 us  [swap(): return lax.all_to_all(array, axis, 0, 0, tiled=True)]
    all_to_all x2 -> x3, starting transfers between devices: 14.1 us -> 33 us  [swap(): return lax.all_to_all(array, axis, 0, 0, tiled=True)]
    ppermute x3 -> x6, starting transfers between devices: 8.6 us -> 18 us  [along_x(): lax.ppermute(array, 'x', [(at, (at + ahead) % chips) for at in range(chip...]
    ppermute x3 -> x6, waiting for transfers between devices: 0.5 us -> 6.62 us  [along_x(): lax.ppermute(array, 'x', [(at, (at + ahead) % chips) for at in range(chip...]
    ppermute x3, starting transfers between devices: 17.5 us -> 11.8 us  [sibling(): return lax.ppermute(array, 'c', ((0, 1), (1, 0)))]
    ppermute x3, waiting for transfers between devices: 0.53 us -> 2.04 us  [sibling(): return lax.ppermute(array, 'c', ((0, 1), (1, 0)))]
    unnamed x10 -> x12, local copies, waits for them, and re-layouts: 0.02 us -> 1.26 us
    all_to_all x2 -> x3, waiting for transfers between devices: 12.9 us -> 13.2 us  [swap(): return lax.all_to_all(array, axis, 0, 0, tiled=True)]
  transfers between devices with their start and end apart: 8 -> 12, of which waited for: 4 -> 6; matrix products, arithmetic and copies ran while one was open for 0% -> 0% of each run, Pallas kernels for 3% -> 3%
where the time goes in v7:
time: 110 us; the launch traced here: 109 us
  starting transfers between devices  62.8 us (57%)
  waiting for transfers between devices  21.8 us (20%)
  Pallas kernels  11.7 us (11%)
  blocking collectives  9.98 us (9%)
  between operations  1.52 us (1%)
  local copies, waits for them, and re-layouts  1.26 us (1%)
    all_to_all x3, starting transfers between devices, swap(): return lax.all_to_all(array, axis, 0, 0, tiled=True)  33 us
    ppermute x6, starting transfers between devices, along_x(): lax.ppermute(array, 'x', [(at, (at + ahead) % chips) for at in range(chip...  18 us
    all_to_all x3, waiting for transfers between devices, swap(): return lax.all_to_all(array, axis, 0, 0, tiled=True)  13.2 us
    ppermute x3, starting transfers between devices, sibling(): return lax.ppermute(array, 'c', ((0, 1), (1, 0)))  11.8 us
    all_to_all x1, blocking collectives, swap(): return lax.all_to_all(array, axis, 0, 0, tiled=True)  9.98 us
    ppermute x6, waiting for transfers between devices, along_x(): lax.ppermute(array, 'x', [(at, (at + ahead) % chips) for at in range(chip...  6.62 us
    pallas_call x1, Pallas kernels, body(): pl.pallas_call(main_kernel, out_shape=(shape(back), shape(back), shape(pa...  4.41 us
  transfers between devices with their start and end apart: 12, of which 6 were waited for; matrix products, arithmetic and copies ran while one was open for 0% of the time, Pallas kernels for 3%

profile of v7, /device:TPU:1, one launch (start us, length us, event | category | flops | bytes accessed | tf_op | source)
XLA Modules:
  0.0 109.1 jit_solution(11913419547971853485)
XLA Ops:
  1.3 1.9 %shard_map.120 = (bf16[256,256]{1,0:T(8,128)(2,1)}, bf16[64,8,256]{2,1,0:T(8,128)(2,1)}) custom-call(s32[1,1]{1,0:T(1,128)S(6)} %copy.13.refs_0_.counts, bf16[256,256]{1,0:T(8,128)(2,1)} %bitcast.10, s32[1,256]{1,0:T(1,128)} %refs_5_.1, bf16[8,1024]{1,0:T(8,128)(2,1)} %bitcast.13, bf16[8,1024]{1,0:T(8,128)(2,1)} %bitcast.14, f32[8,8]{1,0:T(8,128)} %bitcast.15), custom_call_target="tpu_custom_call" | custom-call | tf_op jit(solution)/shard_map/pallas_call | solution.py:236
  3.2 0.0 copy-start.4
  3.2 15.0 %all-to-all-start = ((bf16[64,8,256]{2,1,0:T(8,128)(2,1)}), bf16[64,8,256]{2,1,0:T(8,128)(2,1)S(1)}, u32[]{:S(2)}, u32[]{:S(2)}) async-start(bf16[64,8,256]{2,1,0:T(8,128)(2,1)} %get-tuple-element.35), calls=%async_computation | async-start | bytes 524288 | tf_op jit(solution)/shard_map/all_to_all | solution.py:211
  18.2 0.0 copy-done.4
  18.2 0.0 copy-start
  18.3 0.0 copy-start.1
  18.3 4.6 %collective-permute-start.2 = (bf16[256,256]{1,0:T(8,128)(2,1)S(1)}, bf16[256,256]{1,0:T(8,128)(2,1)S(1)}, u32[]{:S(2)}, u32[]{:S(2)}) collective-permute-start(bf16[256,256]{1,0:T(8,128)(2,1)S(1)} %copy-done.4), channel_id=1, source_target_pairs={{0,48},{16,0},{32,16},{48,32},{1,49},{17,1},{33,17},{49,33},{2,50}... | collective-permute-start | bytes 393224 | tf_op jit(solution)/shard_map/ppermute | solution.py:223
  22.9 2.5 %collective-permute-start.1 = (bf16[256,256]{1,0:T(8,128)(2,1)S(1)}, bf16[256,256]{1,0:T(8,128)(2,1)S(1)}, u32[]{:S(2)}, u32[]{:S(2)}) collective-permute-start(bf16[256,256]{1,0:T(8,128)(2,1)S(1)} %copy-done.4), channel_id=1, source_target_pairs={{0,32},{16,48},{32,0},{48,16},{1,33},{17,49},{33,1},{49,17},{2,34}... | collective-permute-start | bytes 393224 | tf_op jit(solution)/shard_map/ppermute | solution.py:223
  25.4 2.5 %collective-permute-start = (bf16[256,256]{1,0:T(8,128)(2,1)S(1)}, bf16[256,256]{1,0:T(8,128)(2,1)S(1)}, u32[]{:S(2)}, u32[]{:S(2)}) collective-permute-start(bf16[256,256]{1,0:T(8,128)(2,1)S(1)} %copy-done.4), channel_id=1, source_target_pairs={{0,16},{16,32},{32,48},{48,0},{1,17},{17,33},{33,49},{49,1},{2,18}... | collective-permute-start | bytes 393224 | tf_op jit(solution)/shard_map/ppermute | solution.py:223
  27.9 0.0 collective-permute-done.2.refs_3_
  27.9 3.5 %collective-permute-done.1.refs_2_ = bf16[256,256]{1,0:T(8,128)(2,1)S(1)} collective-permute-done((bf16[256,256]{1,0:T(8,128)(2,1)S(1)}, bf16[256,256]{1,0:T(8,128)(2,1)S(1)}, u32[]{:S(2)}, u32[]{:S(2)}) %collective-permute-start.1) | collective-permute-done | bytes 131104 | tf_op jit(solution)/shard_map/ppermute | solution.py:223
  31.4 3.1 %collective-permute-done.refs_1_ = bf16[256,256]{1,0:T(8,128)(2,1)S(1)} collective-permute-done((bf16[256,256]{1,0:T(8,128)(2,1)S(1)}, bf16[256,256]{1,0:T(8,128)(2,1)S(1)}, u32[]{:S(2)}, u32[]{:S(2)}) %collective-permute-start) | collective-permute-done | bytes 131104 | tf_op jit(solution)/shard_map/ppermute | solution.py:223
  34.5 0.0 all-to-all-done
  34.5 0.5 shard_map.121.mine
  35.0 2.9 %collective-permute-start.3 = (bf16[1024,256]{1,0:T(8,128)(2,1)S(1)}, bf16[1024,256]{1,0:T(8,128)(2,1)S(1)}, u32[]{:S(2)}, u32[]{:S(2)}) collective-permute-start(bf16[1024,256]{1,0:T(8,128)(2,1)S(1)} %shard_map.121.mine), channel_id=1, source_target_pairs={{0,8},{8,0},{1,9},{9,1},{2,10},{10,2},{3,11},{11,3},{4,12},{12,4},... | collective-permute-start | bytes 1572872 | tf_op jit(solution)/shard_map/ppermute | solution.py:219
  38.0 1.5 %collective-permute-done.3.other = bf16[1024,256]{1,0:T(8,128)(2,1)S(1)} collective-permute-done((bf16[1024,256]{1,0:T(8,128)(2,1)S(1)}, bf16[1024,256]{1,0:T(8,128)(2,1)S(1)}, u32[]{:S(2)}, u32[]{:S(2)}) %collective-permute-start.3) | collective-permute-done | bytes 524320 | tf_op jit(solution)/shard_map/ppermute | solution.py:219
  39.5 0.0 copy-done
  39.5 0.0 copy-done.1
  39.5 0.0 copy-start.2
  39.5 1.2 %copy-done.2 = bf16[512,1024]{1,0:T(8,128)(2,1)S(1)} copy-done((bf16[512,1024]{1,0:T(8,128)(2,1)S(1)}, bf16[512,1024]{1,0:T(8,128)(2,1)}, u32[]{:S(2)}) %copy-start.2) | copy-done | bytes 1048600
  40.7 4.4 %shard_map.122 = (bf16[1024,256]{1,0:T(8,128)(2,1)S(1)}, bf16[1024,256]{1,0:T(8,128)(2,1)S(1)}, bf16[64,8,256]{2,1,0:T(8,128)(2,1)}) custom-call(s32[1]{0:T(128)} %bitcast.1.head, bf16[1024,256]{1,0:T(8,128)(2,1)S(1)} %shard_map.121.mine, bf16[1024,256]{1,0:T(8,128)(2,1)S(1)} %collective-permute-done.3.other, bf16[512,256]{1,0:T(8,128)(2,1)S(1)} %bitcast.9, ...), custom_call_target="tpu_custom_call" | custom-call | tf_op jit(solution)/shard_map/pallas_call | solution.py:264
  45.1 12.4 %all-to-all-start.1 = ((bf16[64,8,256]{2,1,0:T(8,128)(2,1)}), bf16[64,8,256]{2,1,0:T(8,128)(2,1)S(1)}, u32[]{:S(2)}, u32[]{:S(2)}) async-start(bf16[64,8,256]{2,1,0:T(8,128)(2,1)} %get-tuple-element.42), calls=%async_computation.1 | async-start | bytes 524288 | tf_op jit(solution)/shard_map/all_to_all | solution.py:211
  57.5 1.3 %shard_map.125 = (f32[1024,256]{1,0:T(8,128)S(1)}, bf16[1024,256]{1,0:T(8,128)(2,1)}) custom-call(s32[1]{0:T(128)} %bitcast.1.head, bf16[1024,256]{1,0:T(8,128)(2,1)S(1)} %get-tuple-element.43.keep, bf16[1024,256]{1,0:T(8,128)(2,1)S(1)} %get-tuple-element.44.give, bf16[256,1024]{1,0:T(8,128)(2,1)S(1)} %copy-done, bf16[256,1024]{1,0:T(8,128)(2,1)S(1)} %copy-done.1), custom_call_target="tpu_custom_call" | custom-call | flops 270000000 | bytes 3000000 | tf_op jit(solution)/shard_map/pallas_call | solution.py:272
  58.8 2.5 %collective-permute-start.4 = (bf16[1024,256]{1,0:T(8,128)(2,1)}, bf16[1024,256]{1,0:T(8,128)(2,1)S(1)}, u32[]{:S(2)}, u32[]{:S(2)}) collective-permute-start(bf16[1024,256]{1,0:T(8,128)(2,1)} %get-tuple-element.46), channel_id=1, source_target_pairs={{0,8},{8,0},{1,9},{9,1},{2,10},{10,2},{3,11},{11,3},{4,12},{12,4},... | collective-permute-start | bytes 1572872 | tf_op jit(solution)/shard_map/ppermute | solution.py:219
  61.4 9.2 %all-to-all-done.1.got = bf16[64,8,256]{2,1,0:T(8,128)(2,1)S(1)} async-done(((bf16[64,8,256]{2,1,0:T(8,128)(2,1)}), bf16[64,8,256]{2,1,0:T(8,128)(2,1)S(1)}, u32[]{:S(2)}, u32[]{:S(2)}) %all-to-all-start.1) | async-done | bytes 262176 | tf_op jit(solution)/shard_map/all_to_all | solution.py:211
  70.6 0.8 shard_map.123
  71.4 5.6 %all-to-all-start.2 = ((bf16[64,8,256]{2,1,0:T(8,128)(2,1)}), bf16[64,8,256]{2,1,0:T(8,128)(2,1)S(1)}, u32[]{:S(2)}, u32[]{:S(2)}) async-start(bf16[64,8,256]{2,1,0:T(8,128)(2,1)} %shard_map.123), calls=%async_computation.2 | async-start | bytes 524288 | tf_op jit(solution)/shard_map/all_to_all | solution.py:211
  76.9 0.0 collective-permute-done.4.theirs
  76.9 0.1 shard_map.126
  77.0 1.9 %collective-permute-start.5 = (bf16[256,256]{1,0:T(8,128)(2,1)S(1)}, bf16[256,256]{1,0:T(8,128)(2,1)S(1)}, u32[]{:S(2)}, u32[]{:S(2)}) collective-permute-start(bf16[256,256]{1,0:T(8,128)(2,1)S(1)} %get-tuple-element.48), channel_id=1, source_target_pairs={{0,16},{16,32},{32,48},{48,0},{1,17},{17,33},{33,49},{49,1},{2,18}... | collective-permute-start | bytes 393224 | tf_op jit(solution)/shard_map/ppermute | solution.py:223
  79.0 3.2 %collective-permute-start.6 = (bf16[256,256]{1,0:T(8,128)(2,1)S(1)}, bf16[256,256]{1,0:T(8,128)(2,1)S(1)}, u32[]{:S(2)}, u32[]{:S(2)}) collective-permute-start(bf16[256,256]{1,0:T(8,128)(2,1)S(1)} %get-tuple-element.49), channel_id=1, source_target_pairs={{0,32},{16,48},{32,0},{48,16},{1,33},{17,49},{33,1},{49,17},{2,34}... | collective-permute-start | bytes 393224 | tf_op jit(solution)/shard_map/ppermute | solution.py:223
  82.2 3.3 %collective-permute-start.7 = (bf16[256,256]{1,0:T(8,128)(2,1)S(1)}, bf16[256,256]{1,0:T(8,128)(2,1)S(1)}, u32[]{:S(2)}, u32[]{:S(2)}) collective-permute-start(bf16[256,256]{1,0:T(8,128)(2,1)S(1)} %get-tuple-element.50), channel_id=1, source_target_pairs={{0,48},{16,0},{32,16},{48,32},{1,49},{17,1},{33,17},{49,33},{2,50}... | collective-permute-start | bytes 393224 | tf_op jit(solution)/shard_map/ppermute | solution.py:223
  85.5 4.0 %all-to-all-done.2.got = bf16[64,8,256]{2,1,0:T(8,128)(2,1)S(1)} async-done(((bf16[64,8,256]{2,1,0:T(8,128)(2,1)}), bf16[64,8,256]{2,1,0:T(8,128)(2,1)S(1)}, u32[]{:S(2)}, u32[]{:S(2)}) %all-to-all-start.2) | async-done | bytes 262176 | tf_op jit(solution)/shard_map/all_to_all | solution.py:211
  89.5 0.0 collective-permute-done.5.refs_1_
  89.5 0.0 collective-permute-done.6.refs_2_
  89.5 0.0 collective-permute-done.7.refs_3_
  89.5 0.0 copy-start.3
  89.5 0.0 copy-start.5
  89.5 10.0 %all_to_all.20.got = bf16[4,272,256]{2,1,0:T(8,128)(2,1)S(1)} all-to-all(bf16[4,272,256]{2,1,0:T(8,128)(2,1)S(1)} %shard_map.124), channel_id=1, replica_groups=mesh['z'=8,'x'=4,'c'=2,'y'=8] {'x'}, dimensions={0} | all-to-all | bytes 1114112 | tf_op jit(solution)/shard_map/all_to_all | solution.py:211
  99.5 6.4 %collective-permute-start.8 = (bf16[4,272,256]{2,1,0:T(8,128)(2,1)S(1)}, bf16[4,272,256]{2,1,0:T(8,128)(2,1)S(1)}, u32[]{:S(2)}, u32[]{:S(2)}) collective-permute-start(bf16[4,272,256]{2,1,0:T(8,128)(2,1)S(1)} %all_to_all.20.got), channel_id=1, source_target_pairs={{0,8},{8,0},{1,9},{9,1},{2,10},{10,2},{3,11},{11,3},{4,12},{12,4},... | collective-permute-start | bytes 1671176 | tf_op jit(solution)/shard_map/ppermute | solution.py:219
  105.9 0.0 copy-done.3
  105.9 0.0 copy-done.5
  105.9 1.0 shard_map.127
  107.0 0.5 collective-permute-done.8.other
  107.5 1.6 %shard_map.128 = (f32[8,1024]{1,0:T(8,128)}, f32[256,1024]{1,0:T(8,128)}, f32[256,1024]{1,0:T(8,128)}) custom-call(s32[1]{0:T(128)} %bitcast.2.core, bf16[4,272,256]{2,1,0:T(8,128)(2,1)S(1)} %all_to_all.20.got, bf16[4,272,256]{2,1,0:T(8,128)(2,1)S(1)} %collective-permute-done.8.other), custom_call_target="tpu_custom_call" | custom-call | tf_op jit(solution)/shard_map/pallas_call | solution.py:318
  (1 shorter events, 0.0 us)
Async XLA Ops:
  3.2 15.0 %copy-start.4 = (bf16[256,256]{1,0:T(8,128)(2,1)S(1)}, bf16[256,256]{1,0:T(8,128)(2,1)}, u32[]{:S(2)}) copy-start(bf16[256,256]{1,0:T(8,128)(2,1)} %get-tuple-element.37.refs_0_) | copy-start | bytes 393220
  3.2 31.3 %all-to-all-start = ((bf16[64,8,256]{2,1,0:T(8,128)(2,1)}), bf16[64,8,256]{2,1,0:T(8,128)(2,1)S(1)}, u32[]{:S(2)}, u32[]{:S(2)}) async-start(bf16[64,8,256]{2,1,0:T(8,128)(2,1)} %get-tuple-element.35), calls=%async_computation | async-start | bytes 524288 | tf_op jit(solution)/shard_map/all_to_all | solution.py:211
  18.2 21.2 %copy-start = (bf16[256,1024]{1,0:T(8,128)(2,1)S(1)}, bf16[256,1024]{1,0:T(8,128)(2,1)}, u32[]{:S(2)}) copy-start(bf16[256,1024]{1,0:T(8,128)(2,1)} %w_key.3) | copy-start | bytes 1572868
  18.3 21.2 %copy-start.1 = (bf16[256,1024]{1,0:T(8,128)(2,1)S(1)}, bf16[256,1024]{1,0:T(8,128)(2,1)}, u32[]{:S(2)}) copy-start(bf16[256,1024]{1,0:T(8,128)(2,1)} %w_value.3) | copy-start | bytes 1572868
  18.3 9.6 %collective-permute-start.2 = (bf16[256,256]{1,0:T(8,128)(2,1)S(1)}, bf16[256,256]{1,0:T(8,128)(2,1)S(1)}, u32[]{:S(2)}, u32[]{:S(2)}) collective-permute-start(bf16[256,256]{1,0:T(8,128)(2,1)S(1)} %copy-done.4), channel_id=1, source_target_pairs={{0,48},{16,0},{32,16},{48,32},{1,49},{17,1},{33,17},{49,33},{2,50}... | collective-permute-start | bytes 393224 | tf_op jit(solution)/shard_map/ppermute | solution.py:223
  22.9 8.5 %collective-permute-start.1 = (bf16[256,256]{1,0:T(8,128)(2,1)S(1)}, bf16[256,256]{1,0:T(8,128)(2,1)S(1)}, u32[]{:S(2)}, u32[]{:S(2)}) collective-permute-start(bf16[256,256]{1,0:T(8,128)(2,1)S(1)} %copy-done.4), channel_id=1, source_target_pairs={{0,32},{16,48},{32,0},{48,16},{1,33},{17,49},{33,1},{49,17},{2,34}... | collective-permute-start | bytes 393224 | tf_op jit(solution)/shard_map/ppermute | solution.py:223
  25.4 9.1 %collective-permute-start = (bf16[256,256]{1,0:T(8,128)(2,1)S(1)}, bf16[256,256]{1,0:T(8,128)(2,1)S(1)}, u32[]{:S(2)}, u32[]{:S(2)}) collective-permute-start(bf16[256,256]{1,0:T(8,128)(2,1)S(1)} %copy-done.4), channel_id=1, source_target_pairs={{0,16},{16,32},{32,48},{48,0},{1,17},{17,33},{33,49},{49,1},{2,18}... | collective-permute-start | bytes 393224 | tf_op jit(solution)/shard_map/ppermute | solution.py:223
  35.0 4.4 %collective-permute-start.3 = (bf16[1024,256]{1,0:T(8,128)(2,1)S(1)}, bf16[1024,256]{1,0:T(8,128)(2,1)S(1)}, u32[]{:S(2)}, u32[]{:S(2)}) collective-permute-start(bf16[1024,256]{1,0:T(8,128)(2,1)S(1)} %shard_map.121.mine), channel_id=1, source_target_pairs={{0,8},{8,0},{1,9},{9,1},{2,10},{10,2},{3,11},{11,3},{4,12},{12,4},... | collective-permute-start | bytes 1572872 | tf_op jit(solution)/shard_map/ppermute | solution.py:219
  39.5 1.2 %copy-start.2 = (bf16[512,1024]{1,0:T(8,128)(2,1)S(1)}, bf16[512,1024]{1,0:T(8,128)(2,1)}, u32[]{:S(2)}) copy-start(bf16[512,1024]{1,0:T(8,128)(2,1)} %query.1) | copy-start | bytes 3145732
  45.1 25.5 %all-to-all-start.1 = ((bf16[64,8,256]{2,1,0:T(8,128)(2,1)}), bf16[64,8,256]{2,1,0:T(8,128)(2,1)S(1)}, u32[]{:S(2)}, u32[]{:S(2)}) async-start(bf16[64,8,256]{2,1,0:T(8,128)(2,1)} %get-tuple-element.42), calls=%async_computation.1 | async-start | bytes 524288 | tf_op jit(solution)/shard_map/all_to_all | solution.py:211
  58.8 18.1 %collective-permute-start.4 = (bf16[1024,256]{1,0:T(8,128)(2,1)}, bf16[1024,256]{1,0:T(8,128)(2,1)S(1)}, u32[]{:S(2)}, u32[]{:S(2)}) collective-permute-start(bf16[1024,256]{1,0:T(8,128)(2,1)} %get-tuple-element.46), channel_id=1, source_target_pairs={{0,8},{8,0},{1,9},{9,1},{2,10},{10,2},{3,11},{11,3},{4,12},{12,4},... | collective-permute-start | bytes 1572872 | tf_op jit(solution)/shard_map/ppermute | solution.py:219
  71.4 18.1 %all-to-all-start.2 = ((bf16[64,8,256]{2,1,0:T(8,128)(2,1)}), bf16[64,8,256]{2,1,0:T(8,128)(2,1)S(1)}, u32[]{:S(2)}, u32[]{:S(2)}) async-start(bf16[64,8,256]{2,1,0:T(8,128)(2,1)} %shard_map.123), calls=%async_computation.2 | async-start | bytes 524288 | tf_op jit(solution)/shard_map/all_to_all | solution.py:211
  77.0 12.4 %collective-permute-start.5 = (bf16[256,256]{1,0:T(8,128)(2,1)S(1)}, bf16[256,256]{1,0:T(8,128)(2,1)S(1)}, u32[]{:S(2)}, u32[]{:S(2)}) collective-permute-start(bf16[256,256]{1,0:T(8,128)(2,1)S(1)} %get-tuple-element.48), channel_id=1, source_target_pairs={{0,16},{16,32},{32,48},{48,0},{1,17},{17,33},{33,49},{49,1},{2,18}... | collective-permute-start | bytes 393224 | tf_op jit(solution)/shard_map/ppermute | solution.py:223
  79.0 10.5 %collective-permute-start.6 = (bf16[256,256]{1,0:T(8,128)(2,1)S(1)}, bf16[256,256]{1,0:T(8,128)(2,1)S(1)}, u32[]{:S(2)}, u32[]{:S(2)}) collective-permute-start(bf16[256,256]{1,0:T(8,128)(2,1)S(1)} %get-tuple-element.49), channel_id=1, source_target_pairs={{0,32},{16,48},{32,0},{48,16},{1,33},{17,49},{33,1},{49,17},{2,34}... | collective-permute-start | bytes 393224 | tf_op jit(solution)/shard_map/ppermute | solution.py:223
  82.2 7.3 %collective-permute-start.7 = (bf16[256,256]{1,0:T(8,128)(2,1)S(1)}, bf16[256,256]{1,0:T(8,128)(2,1)S(1)}, u32[]{:S(2)}, u32[]{:S(2)}) collective-permute-start(bf16[256,256]{1,0:T(8,128)(2,1)S(1)} %get-tuple-element.50), channel_id=1, source_target_pairs={{0,48},{16,0},{32,16},{48,32},{1,49},{17,1},{33,17},{49,33},{2,50}... | collective-permute-start | bytes 393224 | tf_op jit(solution)/shard_map/ppermute | solution.py:223
  89.5 16.4 %copy-start.3 = (bf16[1,256,256]{2,1,0:T(8,128)(2,1)S(1)}, bf16[1,256,256]{2,1,0:T(8,128)(2,1)}, u32[]{:S(2)}) copy-start(bf16[1,256,256]{2,1,0:T(8,128)(2,1)} %param.9) | copy-start | bytes 393220
  89.5 16.4 %copy-start.5 = (s32[1,256]{1,0:T(1,128)S(1)}, s32[1,256]{1,0:T(1,128)}, u32[]{:S(2)}) copy-start(s32[1,256]{1,0:T(1,128)} %refs_5_.1) | copy-start | bytes 3076
  99.5 8.0 %collective-permute-start.8 = (bf16[4,272,256]{2,1,0:T(8,128)(2,1)S(1)}, bf16[4,272,256]{2,1,0:T(8,128)(2,1)S(1)}, u32[]{:S(2)}, u32[]{:S(2)}) collective-permute-start(bf16[4,272,256]{2,1,0:T(8,128)(2,1)S(1)} %all_to_all.20.got), channel_id=1, source_target_pairs={{0,8},{8,0},{1,9},{9,1},{2,10},{10,2},{3,11},{11,3},{4,12},{12,4},... | collective-permute-start | bytes 1671176 | tf_op jit(solution)/shard_map/ppermute | solution.py:219

commit v8 on v6

--- a/solution.py
+++ b/solution.py
@@ -165,14 +165,16 @@
             query_sum[...] += query_part
         normals[block * BLOCK : (block + 1) * BLOCK, :] = normal
         grads[block * BLOCK : (block + 1) * BLOCK, :] = grad_both
-    turned = query_sum[...].T
-    totals = mm(normals[...], grads[...], 0, 0)
-    halves = parts.shape[0] // 2
-    for at in range(parts.shape[0]):
-        start = at % halves * ROWS
-        cols = slice(at // halves * HEAD, (at // halves + 1) * HEAD)
-        piece = [totals[start : start + ROWS, cols], turned[at * ROWS : (at + 1) * ROWS]]
-        parts[at] = jnp.concatenate(piece, axis=1).astype(BF16)
+    turned = query_sum[...].T.astype(BF16)
+    totals = mm(normals[...], grads[...], 0, 0).astype(BF16)
+    groups, part_rows = parts.shape[0], parts.shape[1]
+    each = totals.shape[0] // groups
+    half = part_rows - each
+    for group in range(groups):
+        parts[group, :each, :] = totals[group * each : (group + 1) * each, :]
+        start = group * 2 * half
+        parts[group, each:, :HEAD] = turned[start : start + half]
+        parts[group, each:, HEAD:] = turned[start + half : start + 2 * half]
 
 
 def add_up(got):
@@ -188,6 +190,16 @@
         sent[at] = total
 
 
+def total_kernel(got, sent, query_rows):
+    total = add_up(got)
+    each = sent.shape[1]
+    low = total[:each].astype(BF16)
+    for at in range(sent.shape[0]):
+        sent[at] = low
+    query_rows[: got.shape[1] - each, :] = total[each:, :HEAD]
+    query_rows[got.shape[1] - each :, :] = total[each:, HEAD:]
+
+
 def combine_kernel(chip, kept, theirs, *shares):
     chips = kept.shape[0]
     for ahead in range(chips):
@@ -195,19 +207,14 @@
         shares[ahead][...] = (kept[at] + theirs[at].astype(F32)).astype(BF16)
 
 
-def gather_kernel(group, got, sent):
-    chips = sent.shape[0]
-    halves = got.shape[0] // 2
-    depth = halves * ROWS
-    pieces = [got[at].astype(F32)[:, :HEAD] for at in range(2 * halves)]
-    weights = jnp.concatenate(
-        [jnp.concatenate(pieces[:halves], axis=0), jnp.concatenate(pieces[halves:], axis=0)], axis=1
-    ).astype(BF16)
+def gather_kernel(weights, query_rows, sent):
+    chips, depth = sent.shape[0], weights.shape[0]
+    rows = query_rows.shape[0] // chips
     for chip in range(chips):
-        sent[chip, :depth, :] = weights
-        first = group[0] * 2 * chips + 2 * chip
-        rows = [got[first + core].astype(F32) for core in range(2)]
-        sent[chip, depth:, :] = jnp.concatenate(rows, axis=0).astype(BF16)
+        sent[chip, :depth, :] = weights[...]
+        piece = query_rows[chip * rows : (chip + 1) * rows, :]
+        high = piece.astype(BF16).astype(F32)
+        sent[chip, depth:, :] = jnp.concatenate([high, piece - high], axis=1).astype(BF16)
 
 
 def tokens_kernel(counts, *refs):
@@ -237,7 +244,7 @@
                 key_total[:, cols] = both[:, :HEAD]
                 value_total[:, cols] = both[:, HEAD:]
                 piece = source[chip, depth:, :].astype(F32)
-                both_rows = piece[:, HEAD:]
+                both_rows = piece[:, :HEAD] + piece[:, HEAD:]
                 query_rows[:, cols] = jnp.where(core[0] == 0, both_rows[:rows], both_rows[rows:])
 
     @pl.when(core[0] == 0)
@@ -259,6 +266,10 @@
 
 def sibling(array):
     return lax.ppermute(array, "c", ((0, 1), (1, 0)))
+
+
+def along_x(array, ahead, chips):
+    return lax.ppermute(array, "x", [(at, (at + ahead) % chips) for at in range(chips)])
 
 
 def body(tokens, occupancy, counts, queries, saved_lse, grad_out, attn_out, w_key, w_value):
@@ -267,10 +278,10 @@
     latents, rows = queries.shape[0], grad.shape[0]
     chips, groups, windows = lax.axis_size("x"), lax.axis_size("z"), lax.axis_size("y")
     heads = lse.shape[1]
-    core, chip, group = (lax.axis_index(at).astype(jnp.int32) for at in ("c", "x", "z"))
+    core, chip = (lax.axis_index(at).astype(jnp.int32) for at in ("c", "x"))
     head = (2 * chip + core).reshape(1)
-    core, chip, group = core.reshape(1), chip.reshape(1), group.reshape(1)
-    tokens, head, core, chip, group = lax.optimization_barrier((tokens, head, core, chip, group))
+    core, chip = core.reshape(1), chip.reshape(1)
+    tokens, head, core, chip = lax.optimization_barrier((tokens, head, core, chip))
     sent = pl.pallas_call(
         pack_kernel,
         out_shape=shape((chips, shard + 2 * rows, width)),
@@ -293,7 +304,8 @@
     grads = swap(grads, ("z", "c"))
 
     back = (chips, shard, width)
-    part = (groups * windows, ROWS, width)
+    each, half = width // groups, rows * heads // 2
+    part = (groups, each + half, width)
     many = (2 * chips * shard, width)
     keep, give, parts = pl.pallas_call(
         main_kernel,
@@ -318,28 +330,37 @@
         out_specs=(VMEM,) * chips,
         compiler_params=params(16),
     )(chip, kept, sibling(given))
-    shares = [shares[0]] + [
-        lax.ppermute(share, "x", [(at, (at + ahead) % chips) for at in range(chips)])
-        for ahead, share in enumerate(shares[1:], 1)
-    ]
-    parts = swap(parts, ("z", "y"))
+    own, *ahead = shares
+    two = along_x(ahead[1], 2, chips)
+    one = along_x(ahead[0], 1, chips)
+    three = along_x(ahead[2], 3, chips)
+    parts = swap(parts, "z")
     parts = pl.pallas_call(
         spread_kernel,
-        out_shape=shape(part),
+        out_shape=shape((windows, each + half, width)),
         in_specs=[VMEM],
         out_specs=VMEM,
         compiler_params=params(8),
     )(parts)
-    parts = swap(parts, ("z", "y"))
+    parts = swap(parts, "y")
+    weights, query_part = pl.pallas_call(
+        total_kernel,
+        out_shape=(shape((groups, each, width)), shape((2 * half, HEAD), F32)),
+        in_specs=[VMEM],
+        out_specs=(VMEM, VMEM),
+        compiler_params=params(8),
+    )(parts)
+    weights, one, two = lax.optimization_barrier((weights, one, two))
+    weights = swap(weights, "z").reshape(width, width)
     last = (chips, width + 2 * rows, width)
     sent = pl.pallas_call(
         gather_kernel,
         out_shape=shape(last),
-        in_specs=[SMEM, VMEM],
-        out_specs=VMEM,
-        compiler_params=params(16),
-    )(group, parts)
-    sent, *shares = lax.optimization_barrier((sent, *shares))
+        in_specs=[VMEM] * 2,
+        out_specs=VMEM,
+        compiler_params=params(16),
+    )(weights, query_part)
+    sent, *shares = lax.optimization_barrier((sent, own, one, two, three))
     got = swap(sent, "x")
     other = sibling(got)
     grad_tokens = pl.pallas_call(

time: 109 us -> 114 us (1.046)
  waiting for transfers between devices: 14 us -> 19.7 us
  starting transfers between devices: 40.2 us -> 38.9 us
    all_to_all x2 -> x3, waiting for transfers between devices: 12.9 us -> 19.2 us  [swap(): return lax.all_to_all(array, axis, 0, 0, tiled=True)]
    all_to_all x2 -> x3, starting transfers between devices: 14.1 us -> 13.6 us  [swap(): return lax.all_to_all(array, axis, 0, 0, tiled=True)]
  transfers between devices with their start and end apart: 8 -> 9, of which waited for: 4 -> 4; matrix products, arithmetic and copies ran while one was open for 0% -> 0% of each run, Pallas kernels for 3% -> 3%
where the time goes in v8:
time: 114 us; the launch traced here: 113 us
  blocking collectives  40.7 us (36%)
  starting transfers between devices  38.9 us (34%)
  waiting for transfers between devices  19.7 us (17%)
  Pallas kernels  12.1 us (11%)
  between operations  1.45 us (1%)
    all_to_all x3, blocking collectives, swap(): return lax.all_to_all(array, axis, 0, 0, tiled=True)  40.7 us
    all_to_all x3, waiting for transfers between devices, swap(): return lax.all_to_all(array, axis, 0, 0, tiled=True)  19.2 us
    ppermute x3, starting transfers between devices, sibling(): return lax.ppermute(array, 'c', ((0, 1), (1, 0)))  16.6 us
    all_to_all x3, starting transfers between devices, swap(): return lax.all_to_all(array, axis, 0, 0, tiled=True)  13.6 us
    ppermute x3, starting transfers between devices, along_x(): lax.ppermute(array, 'x', [(at, (at + ahead) % chips) for at in range(chip...  8.68 us
    pallas_call x1, Pallas kernels, body(): pl.pallas_call(main_kernel, out_shape=(shape(back), shape(back), shape(pa...  4.59 us
  transfers between devices with their start and end apart: 9, of which 4 were waited for; matrix products, arithmetic and copies ran while one was open for 0% of the time, Pallas kernels for 3%

profile of v8, /device:TPU:1, one launch (start us, length us, event | category | flops | bytes accessed | tf_op | source)
XLA Modules:
  0.0 112.9 jit_solution(2904304363514140304)
XLA Ops:
  1.3 2.0 %shard_map.120 = bf16[4,272,256]{2,1,0:T(8,128)(2,1)} custom-call(s32[1,1]{1,0:T(1,128)S(6)} %copy.13.refs_0_.counts, bf16[256,256]{1,0:T(8,128)(2,1)} %bitcast.9, s32[1,256]{1,0:T(1,128)} %refs_5_.1, bf16[8,1024]{1,0:T(8,128)(2,1)} %bitcast.13, bf16[8,1024]{1,0:T(8,128)(2,1)} %bitcast.14, f32[8,8]{1,0:T(8,128)} %bitcast.15), custom_call_target="tpu_custom_call" | custom-call | tf_op jit(solution)/shard_map/pallas_call | solution.py:285
  3.3 0.0 copy-start.2
  3.3 12.1 %all_to_all.30.got.mine = bf16[4,272,256]{2,1,0:T(8,128)(2,1)S(1)} all-to-all(bf16[4,272,256]{2,1,0:T(8,128)(2,1)} %shard_map.120), channel_id=1, replica_groups=mesh['z'=8,'x'=4,'c'=2,'y'=8] {'x'}, dimensions={0} | all-to-all | bytes 1114112 | tf_op jit(solution)/shard_map/all_to_all | solution.py:260
  15.4 0.0 copy-start
  15.4 0.0 copy-start.1
  15.4 8.7 %collective-permute-start = (bf16[4,272,256]{2,1,0:T(8,128)(2,1)S(1)}, bf16[4,272,256]{2,1,0:T(8,128)(2,1)S(1)}, u32[]{:S(2)}, u32[]{:S(2)}) collective-permute-start(bf16[4,272,256]{2,1,0:T(8,128)(2,1)S(1)} %all_to_all.30.got.mine), channel_id=1, source_target_pairs={{0,8},{8,0},{1,9},{9,1},{2,10},{10,2},{3,11},{11,3},{4,12},{12,4},... | collective-permute-start | bytes 1671176 | tf_op jit(solution)/shard_map/ppermute | solution.py:268
  24.1 19.0 %all_to_all.31.got = bf16[16,32,256]{2,1,0:T(8,128)(2,1)S(1)} all-to-all(bf16[16,32,256]{2,1,0:T(8,128)(2,1)S(1)} %shard_map.121), channel_id=1, replica_groups=mesh['z'=8,'x'=4,'c'=2,'y'=8] {'z','c'}, dimensions={0} | all-to-all | bytes 524288 | tf_op jit(solution)/shard_map/all_to_all | solution.py:260
  43.1 0.0 collective-permute-done.other
  43.1 0.0 copy-done.2
  43.1 0.0 copy-done
  43.1 0.0 copy-done.1
  43.1 4.6 %shard_map.122 = (bf16[4,256,256]{2,1,0:T(8,128)(2,1)S(1)}, bf16[4,256,256]{2,1,0:T(8,128)(2,1)S(1)}, bf16[8,64,256]{2,1,0:T(8,128)(2,1)}) custom-call(s32[1]{0:T(128)} %bitcast.1.head, bf16[4,272,256]{2,1,0:T(8,128)(2,1)S(1)} %all_to_all.30.got.mine, bf16[4,272,256]{2,1,0:T(8,128)(2,1)S(1)} %collective-permute-done.other, ...), custom_call_target="tpu_custom_call" | custom-call | tf_op jit(solution)/shard_map/pallas_call | solution.py:310
  47.7 3.4 %all-to-all-start.2 = ((bf16[8,64,256]{2,1,0:T(8,128)(2,1)}), bf16[8,64,256]{2,1,0:T(8,128)(2,1)S(1)}, u32[]{:S(2)}, u32[]{:S(2)}) async-start(bf16[8,64,256]{2,1,0:T(8,128)(2,1)} %get-tuple-element.32), calls=%async_computation.2 | async-start | bytes 524288 | tf_op jit(solution)/shard_map/all_to_all | solution.py:260
  51.2 1.3 %shard_map.125 = (f32[4,256,256]{2,1,0:T(8,128)S(1)}, bf16[4,256,256]{2,1,0:T(8,128)(2,1)}) custom-call(s32[1]{0:T(128)} %bitcast.1.head, bf16[4,256,256]{2,1,0:T(8,128)(2,1)S(1)} %get-tuple-element.35.keep, bf16[4,256,256]{2,1,0:T(8,128)(2,1)S(1)} %get-tuple-element.36.give, bf16[256,1024]{1,0:T(8,128)(2,1)S(1)} %copy-done, bf16[256,1024]{1,0:T(8,128)(2,1)S(1)} %copy-done.1), custom_call_target="tpu_custom_call" | custom-call | flops 270000000 | bytes 3000000 | tf_op jit(solution)/shard_map/pallas_call | solution.py:318
  52.4 1.9 %collective-permute-start.1 = (bf16[4,256,256]{2,1,0:T(8,128)(2,1)}, bf16[4,256,256]{2,1,0:T(8,128)(2,1)S(1)}, u32[]{:S(2)}, u32[]{:S(2)}) collective-permute-start(bf16[4,256,256]{2,1,0:T(8,128)(2,1)} %get-tuple-element.38), channel_id=1, source_target_pairs={{0,8},{8,0},{1,9},{9,1},{2,10},{10,2},{3,11},{11,3},{4,12},{12,4},... | collective-permute-start | bytes 1572872 | tf_op jit(solution)/shard_map/ppermute | solution.py:268
  54.3 9.2 %all-to-all-done.2.got = bf16[8,64,256]{2,1,0:T(8,128)(2,1)S(1)} async-done(((bf16[8,64,256]{2,1,0:T(8,128)(2,1)}), bf16[8,64,256]{2,1,0:T(8,128)(2,1)S(1)}, u32[]{:S(2)}, u32[]{:S(2)}) %all-to-all-start.2) | async-done | bytes 262176 | tf_op jit(solution)/shard_map/all_to_all | solution.py:260
  63.5 0.7 shard_map.123
  64.2 6.8 %all-to-all-start.3 = ((bf16[8,64,256]{2,1,0:T(8,128)(2,1)}), bf16[8,64,256]{2,1,0:T(8,128)(2,1)S(1)}, u32[]{:S(2)}, u32[]{:S(2)}) async-start(bf16[8,64,256]{2,1,0:T(8,128)(2,1)} %shard_map.123), calls=%async_computation.3 | async-start | bytes 524288 | tf_op jit(solution)/shard_map/all_to_all | solution.py:260
  71.1 0.0 collective-permute-done.1.theirs
  71.1 0.1 shard_map.126
  71.2 2.2 %collective-permute-start.2 = (bf16[256,256]{1,0:T(8,128)(2,1)S(1)}, bf16[256,256]{1,0:T(8,128)(2,1)S(1)}, u32[]{:S(2)}, u32[]{:S(2)}) collective-permute-start(bf16[256,256]{1,0:T(8,128)(2,1)S(1)} %get-tuple-element.39), channel_id=1, source_target_pairs={{0,16},{16,32},{32,48},{48,0},{1,17},{17,33},{33,49},{49,1},{2,18}... | collective-permute-start | bytes 393224 | tf_op jit(solution)/shard_map/ppermute | solution.py:272
  73.4 3.7 %collective-permute-start.3 = (bf16[256,256]{1,0:T(8,128)(2,1)S(1)}, bf16[256,256]{1,0:T(8,128)(2,1)S(1)}, u32[]{:S(2)}, u32[]{:S(2)}) collective-permute-start(bf16[256,256]{1,0:T(8,128)(2,1)S(1)} %get-tuple-element.40), channel_id=1, source_target_pairs={{0,32},{16,48},{32,0},{48,16},{1,33},{17,49},{33,1},{49,17},{2,34}... | collective-permute-start | bytes 393224 | tf_op jit(solution)/shard_map/ppermute | solution.py:272
  77.1 5.0 %all-to-all-done.3.got = bf16[8,64,256]{2,1,0:T(8,128)(2,1)S(1)} async-done(((bf16[8,64,256]{2,1,0:T(8,128)(2,1)}), bf16[8,64,256]{2,1,0:T(8,128)(2,1)S(1)}, u32[]{:S(2)}, u32[]{:S(2)}) %all-to-all-start.3) | async-done | bytes 262176 | tf_op jit(solution)/shard_map/all_to_all | solution.py:260
  82.0 0.7 shard_map.124
  82.7 0.0 collective-permute-done.2.refs_1_
  82.7 0.0 collective-permute-done.3.refs_2_
  82.7 3.4 %all-to-all-start.4 = ((bf16[8,32,256]{2,1,0:T(8,128)(2,1)}), bf16[8,32,256]{2,1,0:T(8,128)(2,1)S(1)}, u32[]{:S(2)}, u32[]{:S(2)}) async-start(bf16[8,32,256]{2,1,0:T(8,128)(2,1)} %get-tuple-element.41), calls=%async_computation.4 | async-start | bytes 262144 | tf_op jit(solution)/shard_map/all_to_all | solution.py:260
  86.1 2.8 %collective-permute-start.4 = (bf16[256,256]{1,0:T(8,128)(2,1)S(1)}, bf16[256,256]{1,0:T(8,128)(2,1)S(1)}, u32[]{:S(2)}, u32[]{:S(2)}) collective-permute-start(bf16[256,256]{1,0:T(8,128)(2,1)S(1)} %get-tuple-element.46), channel_id=1, source_target_pairs={{0,48},{16,0},{32,16},{48,32},{1,49},{17,1},{33,17},{49,33},{2,50}... | collective-permute-start | bytes 393224 | tf_op jit(solution)/shard_map/ppermute | solution.py:272
  88.9 5.0 %all-to-all-done.4 = bf16[8,32,256]{2,1,0:T(8,128)(2,1)S(1)} async-done(((bf16[8,32,256]{2,1,0:T(8,128)(2,1)}), bf16[8,32,256]{2,1,0:T(8,128)(2,1)S(1)}, u32[]{:S(2)}, u32[]{:S(2)}) %all-to-all-start.4) | async-done | bytes 131104 | tf_op jit(solution)/shard_map/all_to_all | solution.py:260
  94.0 0.0 collective-permute-done.4.refs_3_
  94.0 0.0 copy-start.3
  94.0 0.0 copy-start.4
  94.0 9.6 %all_to_all.32.got = bf16[4,272,256]{2,1,0:T(8,128)(2,1)S(1)} all-to-all(bf16[4,272,256]{2,1,0:T(8,128)(2,1)S(1)} %shard_map.127), channel_id=1, replica_groups=mesh['z'=8,'x'=4,'c'=2,'y'=8] {'x'}, dimensions={0} | all-to-all | bytes 1114112 | tf_op jit(solution)/shard_map/all_to_all | solution.py:260
  103.7 6.0 %collective-permute-start.5 = (bf16[4,272,256]{2,1,0:T(8,128)(2,1)S(1)}, bf16[4,272,256]{2,1,0:T(8,128)(2,1)S(1)}, u32[]{:S(2)}, u32[]{:S(2)}) collective-permute-start(bf16[4,272,256]{2,1,0:T(8,128)(2,1)S(1)} %all_to_all.32.got), channel_id=1, source_target_pairs={{0,8},{8,0},{1,9},{9,1},{2,10},{10,2},{3,11},{11,3},{4,12},{12,4},... | collective-permute-start | bytes 1671176 | tf_op jit(solution)/shard_map/ppermute | solution.py:268
  109.7 0.0 copy-done.3
  109.7 0.0 copy-done.4
  109.7 1.0 shard_map.128
  110.7 0.5 collective-permute-done.5.other
  111.3 1.6 %shard_map.129 = (f32[8,1024]{1,0:T(8,128)}, f32[256,1024]{1,0:T(8,128)}, f32[256,1024]{1,0:T(8,128)}) custom-call(s32[1]{0:T(128)} %bitcast.2.core, bf16[4,272,256]{2,1,0:T(8,128)(2,1)S(1)} %all_to_all.32.got, bf16[4,272,256]{2,1,0:T(8,128)(2,1)S(1)} %collective-permute-done.5.other), custom_call_target="tpu_custom_call" | custom-call | tf_op jit(solution)/shard_map/pallas_call | solution.py:374
  (2 shorter events, 0.1 us)
Async XLA Ops:
  3.3 39.8 %copy-start.2 = (bf16[512,1024]{1,0:T(8,128)(2,1)S(1)}, bf16[512,1024]{1,0:T(8,128)(2,1)}, u32[]{:S(2)}) copy-start(bf16[512,1024]{1,0:T(8,128)(2,1)} %query.1) | copy-start | bytes 3145732
  15.4 27.7 %copy-start = (bf16[256,1024]{1,0:T(8,128)(2,1)S(1)}, bf16[256,1024]{1,0:T(8,128)(2,1)}, u32[]{:S(2)}) copy-start(bf16[256,1024]{1,0:T(8,128)(2,1)} %w_key.3) | copy-start | bytes 1572868
  15.4 27.7 %copy-start.1 = (bf16[256,1024]{1,0:T(8,128)(2,1)S(1)}, bf16[256,1024]{1,0:T(8,128)(2,1)}, u32[]{:S(2)}) copy-start(bf16[256,1024]{1,0:T(8,128)(2,1)} %w_value.3) | copy-start | bytes 1572868
  15.4 27.7 %collective-permute-start = (bf16[4,272,256]{2,1,0:T(8,128)(2,1)S(1)}, bf16[4,272,256]{2,1,0:T(8,128)(2,1)S(1)}, u32[]{:S(2)}, u32[]{:S(2)}) collective-permute-start(bf16[4,272,256]{2,1,0:T(8,128)(2,1)S(1)} %all_to_all.30.got.mine), channel_id=1, source_target_pairs={{0,8},{8,0},{1,9},{9,1},{2,10},{10,2},{3,11},{11,3},{4,12},{12,4},... | collective-permute-start | bytes 1671176 | tf_op jit(solution)/shard_map/ppermute | solution.py:268
  47.7 15.8 %all-to-all-start.2 = ((bf16[8,64,256]{2,1,0:T(8,128)(2,1)}), bf16[8,64,256]{2,1,0:T(8,128)(2,1)S(1)}, u32[]{:S(2)}, u32[]{:S(2)}) async-start(bf16[8,64,256]{2,1,0:T(8,128)(2,1)} %get-tuple-element.32), calls=%async_computation.2 | async-start | bytes 524288 | tf_op jit(solution)/shard_map/all_to_all | solution.py:260
  52.4 18.6 %collective-permute-start.1 = (bf16[4,256,256]{2,1,0:T(8,128)(2,1)}, bf16[4,256,256]{2,1,0:T(8,128)(2,1)S(1)}, u32[]{:S(2)}, u32[]{:S(2)}) collective-permute-start(bf16[4,256,256]{2,1,0:T(8,128)(2,1)} %get-tuple-element.38), channel_id=1, source_target_pairs={{0,8},{8,0},{1,9},{9,1},{2,10},{10,2},{3,11},{11,3},{4,12},{12,4},... | collective-permute-start | bytes 1572872 | tf_op jit(solution)/shard_map/ppermute | solution.py:268
  64.2 17.8 %all-to-all-start.3 = ((bf16[8,64,256]{2,1,0:T(8,128)(2,1)}), bf16[8,64,256]{2,1,0:T(8,128)(2,1)S(1)}, u32[]{:S(2)}, u32[]{:S(2)}) async-start(bf16[8,64,256]{2,1,0:T(8,128)(2,1)} %shard_map.123), calls=%async_computation.3 | async-start | bytes 524288 | tf_op jit(solution)/shard_map/all_to_all | solution.py:260
  71.2 11.6 %collective-permute-start.2 = (bf16[256,256]{1,0:T(8,128)(2,1)S(1)}, bf16[256,256]{1,0:T(8,128)(2,1)S(1)}, u32[]{:S(2)}, u32[]{:S(2)}) collective-permute-start(bf16[256,256]{1,0:T(8,128)(2,1)S(1)} %get-tuple-element.39), channel_id=1, source_target_pairs={{0,16},{16,32},{32,48},{48,0},{1,17},{17,33},{33,49},{49,1},{2,18}... | collective-permute-start | bytes 393224 | tf_op jit(solution)/shard_map/ppermute | solution.py:272
  73.4 9.4 %collective-permute-start.3 = (bf16[256,256]{1,0:T(8,128)(2,1)S(1)}, bf16[256,256]{1,0:T(8,128)(2,1)S(1)}, u32[]{:S(2)}, u32[]{:S(2)}) collective-permute-start(bf16[256,256]{1,0:T(8,128)(2,1)S(1)} %get-tuple-element.40), channel_id=1, source_target_pairs={{0,32},{16,48},{32,0},{48,16},{1,33},{17,49},{33,1},{49,17},{2,34}... | collective-permute-start | bytes 393224 | tf_op jit(solution)/shard_map/ppermute | solution.py:272
  82.7 11.2 %all-to-all-start.4 = ((bf16[8,32,256]{2,1,0:T(8,128)(2,1)}), bf16[8,32,256]{2,1,0:T(8,128)(2,1)S(1)}, u32[]{:S(2)}, u32[]{:S(2)}) async-start(bf16[8,32,256]{2,1,0:T(8,128)(2,1)} %get-tuple-element.41), calls=%async_computation.4 | async-start | bytes 262144 | tf_op jit(solution)/shard_map/all_to_all | solution.py:260
  86.1 7.9 %collective-permute-start.4 = (bf16[256,256]{1,0:T(8,128)(2,1)S(1)}, bf16[256,256]{1,0:T(8,128)(2,1)S(1)}, u32[]{:S(2)}, u32[]{:S(2)}) collective-permute-start(bf16[256,256]{1,0:T(8,128)(2,1)S(1)} %get-tuple-element.46), channel_id=1, source_target_pairs={{0,48},{16,0},{32,16},{48,32},{1,49},{17,1},{33,17},{49,33},{2,50}... | collective-permute-start | bytes 393224 | tf_op jit(solution)/shard_map/ppermute | solution.py:272
  94.0 15.7 %copy-start.3 = (bf16[1,256,256]{2,1,0:T(8,128)(2,1)S(1)}, bf16[1,256,256]{2,1,0:T(8,128)(2,1)}, u32[]{:S(2)}) copy-start(bf16[1,256,256]{2,1,0:T(8,128)(2,1)} %param.9) | copy-start | bytes 393220
  94.0 15.7 %copy-start.4 = (s32[1,256]{1,0:T(1,128)S(1)}, s32[1,256]{1,0:T(1,128)}, u32[]{:S(2)}) copy-start(s32[1,256]{1,0:T(1,128)} %refs_5_.1) | copy-start | bytes 3076
  103.7 7.6 %collective-permute-start.5 = (bf16[4,272,256]{2,1,0:T(8,128)(2,1)S(1)}, bf16[4,272,256]{2,1,0:T(8,128)(2,1)S(1)}, u32[]{:S(2)}, u32[]{:S(2)}) collective-permute-start(bf16[4,272,256]{2,1,0:T(8,128)(2,1)S(1)} %all_to_all.32.got), channel_id=1, source_target_pairs={{0,8},{8,0},{1,9},{9,1},{2,10},{10,2},{3,11},{11,3},{4,12},{12,4},... | collective-permute-start | bytes 1671176 | tf_op jit(solution)/shard_map/ppermute | solution.py:268

commit v9 on v6

--- a/solution.py
+++ b/solution.py
@@ -15,6 +15,7 @@
 LOG2E = math.log2(math.e)
 F32, BF16 = jnp.float32, jnp.bfloat16
 VMEM = pl.BlockSpec(memory_space=pltpu.VMEM)
+HBM = pl.BlockSpec(memory_space=pltpu.HBM)
 SMEM = pl.BlockSpec(memory_space=pltpu.SMEM)
 
 
@@ -55,27 +56,30 @@
 
 
 def pack_kernel(*refs):
-    sources, sent, (counts, tokens, occupancy, grad, out, lse), done = (
-        refs[:6],
-        refs[6],
-        refs[7:13],
-        refs[13],
-    )
+    sources, sent, held, (masked, extra_rows, taken, left) = refs[:6], refs[6], refs[7:13], refs[13:]
     copies = [
-        pltpu.make_async_copy(source, target, done.at[at])
-        for at, (source, target) in enumerate(zip(sources, refs[7:13]))
+        pltpu.make_async_copy(source, target, taken.at[at])
+        for at, (source, target) in enumerate(zip(sources, held))
     ]
     for copy in copies:
         copy.start()
-    for copy in copies:
+    counts, tokens, occupancy, grad, out, lse = held
+    chips, (shard, width) = sent.shape[0], tokens.shape
+    for copy in copies[:3]:
         copy.wait()
-    chips, (shard, width) = sent.shape[0], tokens.shape
     live = live_rows(occupancy[...], counts[0, 0], width)
-    masked = jnp.where(live > 0.0, tokens[...].astype(F32), 0.0).astype(BF16)
+    masked[...] = jnp.where(live > 0.0, tokens[...].astype(F32), 0.0).astype(BF16)
+    leaving = [
+        pltpu.make_async_copy(masked, sent.at[chip, pl.ds(0, shard)], left.at[0, chip])
+        for chip in range(chips)
+    ]
+    for copy in leaving:
+        copy.start()
+    for copy in copies[3:]:
+        copy.wait()
     rows = grad.shape[0]
     lane = lax.broadcasted_iota(jnp.int32, (rows, HEAD), 1)
     for chip in range(chips):
-        sent[chip, :shard, :] = masked
         extras, grads = [], []
         for head in (2 * chip, 2 * chip + 1):
             cols = slice(head * HEAD, (head + 1) * HEAD)
@@ -89,7 +93,14 @@
         both = jnp.concatenate(
             [jnp.concatenate(grads, axis=1), jnp.concatenate(extras, axis=1)], axis=0
         )
-        sent[chip, shard:, :] = both.astype(BF16)
+        extra_rows[chip] = both.astype(BF16)
+        copy = pltpu.make_async_copy(
+            extra_rows.at[chip], sent.at[chip, pl.ds(shard, 2 * rows)], left.at[1, chip]
+        )
+        copy.start()
+        leaving.append(copy)
+    for copy in leaving:
+        copy.wait()
 
 
 def turn_kernel(got, sent):
@@ -210,8 +221,28 @@
         sent[chip, depth:, :] = jnp.concatenate(rows, axis=0).astype(BF16)
 
 
-def tokens_kernel(counts, *refs):
-    shares, (tokens, occupancy, grad_tokens) = refs[:-3], refs[-3:]
+def place_totals(core, got, targets, staged, done):
+    copies = []
+    depth = staged.shape[2]
+    for chip in range(staged.shape[0]):
+        both = got[chip, :depth, :].astype(F32)
+        cols = pl.ds(pl.multiple_of((2 * chip + core) * HEAD, HEAD), HEAD)
+        for at, target in enumerate(targets):
+            staged[chip, at] = both[:, at * HEAD : (at + 1) * HEAD]
+            copy = pltpu.make_async_copy(
+                staged.at[chip, at], target.at[:, cols], done.at[chip, at]
+            )
+            copy.start()
+            copies.append(copy)
+    return copies
+
+
+def tokens_kernel(core, counts, got, *refs):
+    shares, (tokens, occupancy, grad_tokens, key_total, value_total, staged, done) = (
+        refs[:-7],
+        refs[-7:],
+    )
+    copies = place_totals(core[0], got, (key_total, value_total), staged, done)
     width = tokens.shape[1]
     normal, inverse = layer_norm(tokens[...].astype(F32))
     grad_normal = shares[0][...].astype(F32)
@@ -225,28 +256,26 @@
         - normal * jnp.mean(grad_normal * normal, axis=-1, keepdims=True)
     )
     grad_tokens[...] = grad_input.astype(BF16)
-
-
-def finish_kernel(core, got, other, query_rows, key_total, value_total):
-    chips, depth, rows = got.shape[0], key_total.shape[0], query_rows.shape[0]
-    def write(low, high):
-        for chip in range(chips):
-            for at, source in ((2 * chip, low), (2 * chip + 1, high)):
-                cols = slice(at * HEAD, (at + 1) * HEAD)
-                both = source[chip, :depth, :].astype(F32)
-                key_total[:, cols] = both[:, :HEAD]
-                value_total[:, cols] = both[:, HEAD:]
-                piece = source[chip, depth:, :].astype(F32)
-                both_rows = piece[:, HEAD:]
-                query_rows[:, cols] = jnp.where(core[0] == 0, both_rows[:rows], both_rows[rows:])
-
-    @pl.when(core[0] == 0)
-    def _():
-        write(got, other)
-
-    @pl.when(core[0] != 0)
-    def _():
-        write(other, got)
+    for copy in copies:
+        copy.wait()
+
+
+def finish_kernel(
+    core, got, other, key_half, value_half, query_rows, key_total, value_total, staged, done
+):
+    del key_half, value_half
+    copies = place_totals(1 - core[0], other, (key_total, value_total), staged, done)
+    rows, depth = query_rows.shape[0], staged.shape[2]
+    first = core[0] == 0
+    for chip in range(got.shape[0]):
+        mine, theirs = (ref[chip, depth:, HEAD:].astype(F32) for ref in (got, other))
+        mine = jnp.where(first, mine[:rows], mine[rows:])
+        theirs = jnp.where(first, theirs[:rows], theirs[rows:])
+        start = 2 * chip * HEAD
+        query_rows[:, start : start + HEAD] = jnp.where(first, mine, theirs)
+        query_rows[:, start + HEAD : start + 2 * HEAD] = jnp.where(first, theirs, mine)
+    for copy in copies:
+        copy.wait()
 
 
 def swap(array, axis):
@@ -273,12 +302,13 @@
     tokens, head, core, chip, group = lax.optimization_barrier((tokens, head, core, chip, group))
     sent = pl.pallas_call(
         pack_kernel,
-        out_shape=shape((chips, shard + 2 * rows, width)),
-        in_specs=[pl.BlockSpec(memory_space=pltpu.HBM)] * 6,
-        out_specs=VMEM,
+        out_shape=pltpu.HBM((chips, shard + 2 * rows, width), BF16),
+        in_specs=[HBM] * 6,
+        out_specs=HBM,
         scratch_shapes=[pltpu.SMEM(counts.shape, counts.dtype)]
         + [pltpu.VMEM(ref.shape, ref.dtype) for ref in (tokens, occupancy, grad, out, lse)]
-        + [pltpu.SemaphoreType.DMA((6,))],
+        + [pltpu.VMEM((shard, width), BF16), pltpu.VMEM((chips, 2 * rows, width), BF16)]
+        + [pltpu.SemaphoreType.DMA((6,)), pltpu.SemaphoreType.DMA((2, chips))],
         compiler_params=params(60),
     )(counts, tokens, occupancy, grad, out, lse)
     got = swap(sent, "x")
@@ -342,25 +372,29 @@
     sent, *shares = lax.optimization_barrier((sent, *shares))
     got = swap(sent, "x")
     other = sibling(got)
-    grad_tokens = pl.pallas_call(
+    total = pltpu.HBM((width, heads * HEAD), F32)
+    staging = [
+        pltpu.VMEM((chips, 2, width, HEAD), F32),
+        pltpu.SemaphoreType.DMA((chips, 2)),
+    ]
+    grad_tokens, key_total, value_total = pl.pallas_call(
         tokens_kernel,
-        out_shape=shape((shard, width)),
-        in_specs=[SMEM] + [VMEM] * (chips + 2),
-        out_specs=VMEM,
+        out_shape=(shape((shard, width)), total, total),
+        in_specs=[SMEM] * 2 + [VMEM] * (chips + 3),
+        out_specs=(VMEM, HBM, HBM),
+        scratch_shapes=staging,
         compiler_params=params(16),
-        cost_estimate=pl.CostEstimate(flops=2000000, bytes_accessed=1000000, transcendentals=256),
-    )(counts, *shares, tokens, occupancy)
+        cost_estimate=pl.CostEstimate(flops=2000000, bytes_accessed=3000000, transcendentals=256),
+    )(core, counts, got, *shares, tokens, occupancy)
     query_rows, key_total, value_total = pl.pallas_call(
         finish_kernel,
-        out_shape=(
-            shape((rows, heads * HEAD), F32),
-            shape((width, heads * HEAD), F32),
-            shape((width, heads * HEAD), F32),
-        ),
-        in_specs=[SMEM] + [VMEM] * 2,
-        out_specs=(VMEM,) * 3,
+        out_shape=(shape((rows, heads * HEAD), F32), total, total),
+        in_specs=[SMEM] + [VMEM] * 2 + [HBM] * 2,
+        out_specs=(VMEM, HBM, HBM),
+        input_output_aliases={3: 1, 4: 2},
+        scratch_shapes=staging,
         compiler_params=params(16),
-    )(core, got, other)
+    )(core, got, other, key_total, value_total)
     return grad_tokens[None], query_rows, key_total, value_total
 
 

time: 109 us -> 109 us (level)
  transfers between devices with their start and end apart: 8 -> 8, of which waited for: 4 -> 3; matrix products, arithmetic and copies ran while one was open for 0% -> 0% of each run, Pallas kernels for 3% -> 4%
where the time goes in v9:
time: 109 us; the launch traced here: 108 us
  blocking collectives  41 us (38%)
  starting transfers between devices  40.1 us (37%)
  waiting for transfers between devices  13.4 us (12%)
  Pallas kernels  12.4 us (11%)
  between operations  1.46 us (1%)
    all_to_all x3, blocking collectives, swap(): return lax.all_to_all(array, axis, 0, 0, tiled=True)  41 us
    ppermute x3, starting transfers between devices, sibling(): return lax.ppermute(array, 'c', ((0, 1), (1, 0)))  17.5 us
    all_to_all x2, starting transfers between devices, swap(): return lax.all_to_all(array, axis, 0, 0, tiled=True)  14.1 us
    all_to_all x2, waiting for transfers between devices, swap(): return lax.all_to_all(array, axis, 0, 0, tiled=True)  12.9 us
    ppermute x3, starting transfers between devices, body(): lax.ppermute(share, 'x', [(at, (at + ahead) % chips) for at in range(chip...  8.6 us
    pallas_call x1, Pallas kernels, body(): pl.pallas_call(main_kernel, out_shape=(shape(back), shape(back), shape(pa...  4.59 us
  transfers between devices with their start and end apart: 8, of which 3 were waited for; matrix products, arithmetic and copies ran while one was open for 0% of the time, Pallas kernels for 4%

profile of v9, /device:TPU:1, one launch (start us, length us, event | category | flops | bytes accessed | tf_op | source)
XLA Modules:
  0.0 108.5 jit_solution(3929588094765461305)
XLA Ops:
  1.3 2.0 %shard_map.120 = bf16[4,272,256]{2,1,0:T(8,128)(2,1)} custom-call(s32[1,1]{1,0:T(1,128)S(6)} %copy.17.refs_0_.counts, bf16[256,256]{1,0:T(8,128)(2,1)} %bitcast.9, s32[1,256]{1,0:T(1,128)} %refs_5_.1, bf16[8,1024]{1,0:T(8,128)(2,1)} %bitcast.11, bf16[8,1024]{1,0:T(8,128)(2,1)} %bitcast.12, f32[8,8]{1,0:T(8,128)} %bitcast.13), custom_call_target="tpu_custom_call" | custom-call | tf_op jit(solution)/shard_map/pallas_call | solution.py:303
  3.3 0.0 copy-start.2
  3.3 12.1 %all_to_all.25.got.mine = bf16[4,272,256]{2,1,0:T(8,128)(2,1)S(1)} all-to-all(bf16[4,272,256]{2,1,0:T(8,128)(2,1)} %shard_map.120), channel_id=1, replica_groups=mesh['z'=8,'x'=4,'c'=2,'y'=8] {'x'}, dimensions={0} | all-to-all | bytes 1114112 | tf_op jit(solution)/shard_map/all_to_all | solution.py:282
  15.4 0.0 copy-start
  15.4 0.0 copy-start.1
  15.4 8.7 %collective-permute-start = (bf16[4,272,256]{2,1,0:T(8,128)(2,1)S(1)}, bf16[4,272,256]{2,1,0:T(8,128)(2,1)S(1)}, u32[]{:S(2)}, u32[]{:S(2)}) collective-permute-start(bf16[4,272,256]{2,1,0:T(8,128)(2,1)S(1)} %all_to_all.25.got.mine), channel_id=1, source_target_pairs={{0,8},{8,0},{1,9},{9,1},{2,10},{10,2},{3,11},{11,3},{4,12},{12,4},... | collective-permute-start | bytes 1671176 | tf_op jit(solution)/shard_map/ppermute | solution.py:290
  24.1 19.0 %all_to_all.26.got = bf16[16,32,256]{2,1,0:T(8,128)(2,1)S(1)} all-to-all(bf16[16,32,256]{2,1,0:T(8,128)(2,1)S(1)} %shard_map.121), channel_id=1, replica_groups=mesh['z'=8,'x'=4,'c'=2,'y'=8] {'z','c'}, dimensions={0} | all-to-all | bytes 524288 | tf_op jit(solution)/shard_map/all_to_all | solution.py:282
  43.1 0.0 collective-permute-done.other
  43.1 0.0 copy-done.2
  43.1 0.0 copy-done
  43.1 0.0 copy-done.1
  43.1 4.6 %shard_map.122 = (bf16[4,256,256]{2,1,0:T(8,128)(2,1)S(1)}, bf16[4,256,256]{2,1,0:T(8,128)(2,1)S(1)}, bf16[64,8,256]{2,1,0:T(8,128)(2,1)}) custom-call(s32[1]{0:T(128)} %bitcast.1.head, bf16[4,272,256]{2,1,0:T(8,128)(2,1)S(1)} %all_to_all.25.got.mine, bf16[4,272,256]{2,1,0:T(8,128)(2,1)S(1)} %collective-permute-done.other, ...), custom_call_target="tpu_custom_call" | custom-call | tf_op jit(solution)/shard_map/pallas_call | solution.py:328
  47.7 8.5 %all-to-all-start.2 = ((bf16[64,8,256]{2,1,0:T(8,128)(2,1)}), bf16[64,8,256]{2,1,0:T(8,128)(2,1)S(1)}, u32[]{:S(2)}, u32[]{:S(2)}) async-start(bf16[64,8,256]{2,1,0:T(8,128)(2,1)} %get-tuple-element.33), calls=%async_computation.2 | async-start | bytes 524288 | tf_op jit(solution)/shard_map/all_to_all | solution.py:282
  56.2 1.3 %shard_map.125 = (f32[4,256,256]{2,1,0:T(8,128)S(1)}, bf16[4,256,256]{2,1,0:T(8,128)(2,1)}) custom-call(s32[1]{0:T(128)} %bitcast.1.head, bf16[4,256,256]{2,1,0:T(8,128)(2,1)S(1)} %get-tuple-element.35.keep, bf16[4,256,256]{2,1,0:T(8,128)(2,1)S(1)} %get-tuple-element.36.give, bf16[256,1024]{1,0:T(8,128)(2,1)S(1)} %copy-done, bf16[256,1024]{1,0:T(8,128)(2,1)S(1)} %copy-done.1), custom_call_target="tpu_custom_call" | custom-call | flops 270000000 | bytes 3000000 | tf_op jit(solution)/shard_map/pallas_call | solution.py:336
  57.4 2.6 %collective-permute-start.1 = (bf16[4,256,256]{2,1,0:T(8,128)(2,1)}, bf16[4,256,256]{2,1,0:T(8,128)(2,1)S(1)}, u32[]{:S(2)}, u32[]{:S(2)}) collective-permute-start(bf16[4,256,256]{2,1,0:T(8,128)(2,1)} %get-tuple-element.38), channel_id=1, source_target_pairs={{0,8},{8,0},{1,9},{9,1},{2,10},{10,2},{3,11},{11,3},{4,12},{12,4},... | collective-permute-start | bytes 1572872 | tf_op jit(solution)/shard_map/ppermute | solution.py:290
  60.0 9.2 %all-to-all-done.2.got = bf16[64,8,256]{2,1,0:T(8,128)(2,1)S(1)} async-done(((bf16[64,8,256]{2,1,0:T(8,128)(2,1)}), bf16[64,8,256]{2,1,0:T(8,128)(2,1)S(1)}, u32[]{:S(2)}, u32[]{:S(2)}) %all-to-all-start.2) | async-done | bytes 262176 | tf_op jit(solution)/shard_map/all_to_all | solution.py:282
  69.2 0.8 shard_map.123
  70.0 5.6 %all-to-all-start.3 = ((bf16[64,8,256]{2,1,0:T(8,128)(2,1)}), bf16[64,8,256]{2,1,0:T(8,128)(2,1)S(1)}, u32[]{:S(2)}, u32[]{:S(2)}) async-start(bf16[64,8,256]{2,1,0:T(8,128)(2,1)} %shard_map.123), calls=%async_computation.3 | async-start | bytes 524288 | tf_op jit(solution)/shard_map/all_to_all | solution.py:282
  75.6 0.0 collective-permute-done.1.theirs
  75.6 0.1 shard_map.126
  75.7 2.2 %collective-permute-start.2 = (bf16[256,256]{1,0:T(8,128)(2,1)S(1)}, bf16[256,256]{1,0:T(8,128)(2,1)S(1)}, u32[]{:S(2)}, u32[]{:S(2)}) collective-permute-start(bf16[256,256]{1,0:T(8,128)(2,1)S(1)} %get-tuple-element.40), channel_id=1, source_target_pairs={{0,16},{16,32},{32,48},{48,0},{1,17},{17,33},{33,49},{49,1},{2,18}... | collective-permute-start | bytes 393224 | tf_op jit(solution)/shard_map/ppermute | solution.py:352
  77.9 3.7 %collective-permute-start.3 = (bf16[256,256]{1,0:T(8,128)(2,1)S(1)}, bf16[256,256]{1,0:T(8,128)(2,1)S(1)}, u32[]{:S(2)}, u32[]{:S(2)}) collective-permute-start(bf16[256,256]{1,0:T(8,128)(2,1)S(1)} %get-tuple-element.41), channel_id=1, source_target_pairs={{0,32},{16,48},{32,0},{48,16},{1,33},{17,49},{33,1},{49,17},{2,34}... | collective-permute-start | bytes 393224 | tf_op jit(solution)/shard_map/ppermute | solution.py:352
  81.6 2.7 %collective-permute-start.4 = (bf16[256,256]{1,0:T(8,128)(2,1)S(1)}, bf16[256,256]{1,0:T(8,128)(2,1)S(1)}, u32[]{:S(2)}, u32[]{:S(2)}) collective-permute-start(bf16[256,256]{1,0:T(8,128)(2,1)S(1)} %get-tuple-element.42), channel_id=1, source_target_pairs={{0,48},{16,0},{32,16},{48,32},{1,49},{17,1},{33,17},{49,33},{2,50}... | collective-permute-start | bytes 393224 | tf_op jit(solution)/shard_map/ppermute | solution.py:352
  84.3 3.8 %all-to-all-done.3.got = bf16[64,8,256]{2,1,0:T(8,128)(2,1)S(1)} async-done(((bf16[64,8,256]{2,1,0:T(8,128)(2,1)}), bf16[64,8,256]{2,1,0:T(8,128)(2,1)S(1)}, u32[]{:S(2)}, u32[]{:S(2)}) %all-to-all-start.3) | async-done | bytes 262176 | tf_op jit(solution)/shard_map/all_to_all | solution.py:282
  88.1 0.0 collective-permute-done.2.refs_1_
  88.1 0.0 collective-permute-done.3.refs_2_
  88.1 0.5 collective-permute-done.4.refs_3_
  88.6 0.0 copy-start.3
  88.6 0.0 copy-start.4
  88.6 9.9 %all_to_all.27.got = bf16[4,272,256]{2,1,0:T(8,128)(2,1)S(1)} all-to-all(bf16[4,272,256]{2,1,0:T(8,128)(2,1)S(1)} %shard_map.124), channel_id=1, replica_groups=mesh['z'=8,'x'=4,'c'=2,'y'=8] {'x'}, dimensions={0} | all-to-all | bytes 1114112 | tf_op jit(solution)/shard_map/all_to_all | solution.py:282
  98.6 6.2 %collective-permute-start.5 = (bf16[4,272,256]{2,1,0:T(8,128)(2,1)S(1)}, bf16[4,272,256]{2,1,0:T(8,128)(2,1)S(1)}, u32[]{:S(2)}, u32[]{:S(2)}) collective-permute-start(bf16[4,272,256]{2,1,0:T(8,128)(2,1)S(1)} %all_to_all.27.got), channel_id=1, source_target_pairs={{0,8},{8,0},{1,9},{9,1},{2,10},{10,2},{3,11},{11,3},{4,12},{12,4},... | collective-permute-start | bytes 1671176 | tf_op jit(solution)/shard_map/ppermute | solution.py:290
  104.8 0.0 copy-done.3
  104.8 0.0 copy-done.4
  104.8 2.0 %shard_map.127 = (bf16[256,256]{1,0:T(8,128)(2,1)}, f32[256,1024]{1,0:T(8,128)}, f32[256,1024]{1,0:T(8,128)}) custom-call(s32[1]{0:T(128)} %bitcast.2.core, s32[1,1]{1,0:T(1,128)S(6)} %copy.17.refs_0_.counts, bf16[4,272,256]{2,1,0:T(8,128)(2,1)S(1)} %all_to_all.27.got, bf16[256,256]{1,0:T(8,128)(2,1)S(1)} %get-tuple-element.44.refs_0_, ...), custom_call_target="tpu_custom_call" | custom-call | flops 2000000 | bytes 3000000 | tf_op jit(solution)/shard_map/pallas_call | solution.py:380
  106.8 0.0 collective-permute-done.5.other
  106.8 1.7 %shard_map.128 = (f32[8,1024]{1,0:T(8,128)}, f32[256,1024]{1,0:T(8,128)}, f32[256,1024]{1,0:T(8,128)}) custom-call(s32[1]{0:T(128)} %bitcast.2.core, bf16[4,272,256]{2,1,0:T(8,128)(2,1)S(1)} %all_to_all.27.got, bf16[4,272,256]{2,1,0:T(8,128)(2,1)S(1)} %collective-permute-done.5.other, ...), custom_call_target="tpu_custom_call", output_to_operand_aliasing={{1}: (3, {}), {2}: (4, {})} | custom-call | tf_op jit(solution)/shard_map/pallas_call | solution.py:389
  (2 shorter events, 0.1 us)
Async XLA Ops:
  3.3 39.8 %copy-start.2 = (bf16[512,1024]{1,0:T(8,128)(2,1)S(1)}, bf16[512,1024]{1,0:T(8,128)(2,1)}, u32[]{:S(2)}) copy-start(bf16[512,1024]{1,0:T(8,128)(2,1)} %query.1) | copy-start | bytes 3145732
  15.4 27.7 %copy-start = (bf16[256,1024]{1,0:T(8,128)(2,1)S(1)}, bf16[256,1024]{1,0:T(8,128)(2,1)}, u32[]{:S(2)}) copy-start(bf16[256,1024]{1,0:T(8,128)(2,1)} %w_key.3) | copy-start | bytes 1572868
  15.4 27.7 %copy-start.1 = (bf16[256,1024]{1,0:T(8,128)(2,1)S(1)}, bf16[256,1024]{1,0:T(8,128)(2,1)}, u32[]{:S(2)}) copy-start(bf16[256,1024]{1,0:T(8,128)(2,1)} %w_value.3) | copy-start | bytes 1572868
  15.4 27.7 %collective-permute-start = (bf16[4,272,256]{2,1,0:T(8,128)(2,1)S(1)}, bf16[4,272,256]{2,1,0:T(8,128)(2,1)S(1)}, u32[]{:S(2)}, u32[]{:S(2)}) collective-permute-start(bf16[4,272,256]{2,1,0:T(8,128)(2,1)S(1)} %all_to_all.25.got.mine), channel_id=1, source_target_pairs={{0,8},{8,0},{1,9},{9,1},{2,10},{10,2},{3,11},{11,3},{4,12},{12,4},... | collective-permute-start | bytes 1671176 | tf_op jit(solution)/shard_map/ppermute | solution.py:290
  47.7 21.5 %all-to-all-start.2 = ((bf16[64,8,256]{2,1,0:T(8,128)(2,1)}), bf16[64,8,256]{2,1,0:T(8,128)(2,1)S(1)}, u32[]{:S(2)}, u32[]{:S(2)}) async-start(bf16[64,8,256]{2,1,0:T(8,128)(2,1)} %get-tuple-element.33), calls=%async_computation.2 | async-start | bytes 524288 | tf_op jit(solution)/shard_map/all_to_all | solution.py:282
  57.4 18.1 %collective-permute-start.1 = (bf16[4,256,256]{2,1,0:T(8,128)(2,1)}, bf16[4,256,256]{2,1,0:T(8,128)(2,1)S(1)}, u32[]{:S(2)}, u32[]{:S(2)}) collective-permute-start(bf16[4,256,256]{2,1,0:T(8,128)(2,1)} %get-tuple-element.38), channel_id=1, source_target_pairs={{0,8},{8,0},{1,9},{9,1},{2,10},{10,2},{3,11},{11,3},{4,12},{12,4},... | collective-permute-start | bytes 1572872 | tf_op jit(solution)/shard_map/ppermute | solution.py:290
  70.0 18.1 %all-to-all-start.3 = ((bf16[64,8,256]{2,1,0:T(8,128)(2,1)}), bf16[64,8,256]{2,1,0:T(8,128)(2,1)S(1)}, u32[]{:S(2)}, u32[]{:S(2)}) async-start(bf16[64,8,256]{2,1,0:T(8,128)(2,1)} %shard_map.123), calls=%async_computation.3 | async-start | bytes 524288 | tf_op jit(solution)/shard_map/all_to_all | solution.py:282
  75.7 12.4 %collective-permute-start.2 = (bf16[256,256]{1,0:T(8,128)(2,1)S(1)}, bf16[256,256]{1,0:T(8,128)(2,1)S(1)}, u32[]{:S(2)}, u32[]{:S(2)}) collective-permute-start(bf16[256,256]{1,0:T(8,128)(2,1)S(1)} %get-tuple-element.40), channel_id=1, source_target_pairs={{0,16},{16,32},{32,48},{48,0},{1,17},{17,33},{33,49},{49,1},{2,18}... | collective-permute-start | bytes 393224 | tf_op jit(solution)/shard_map/ppermute | solution.py:352
  77.9 10.2 %collective-permute-start.3 = (bf16[256,256]{1,0:T(8,128)(2,1)S(1)}, bf16[256,256]{1,0:T(8,128)(2,1)S(1)}, u32[]{:S(2)}, u32[]{:S(2)}) collective-permute-start(bf16[256,256]{1,0:T(8,128)(2,1)S(1)} %get-tuple-element.41), channel_id=1, source_target_pairs={{0,32},{16,48},{32,0},{48,16},{1,33},{17,49},{33,1},{49,17},{2,34}... | collective-permute-start | bytes 393224 | tf_op jit(solution)/shard_map/ppermute | solution.py:352
  81.6 7.0 %collective-permute-start.4 = (bf16[256,256]{1,0:T(8,128)(2,1)S(1)}, bf16[256,256]{1,0:T(8,128)(2,1)S(1)}, u32[]{:S(2)}, u32[]{:S(2)}) collective-permute-start(bf16[256,256]{1,0:T(8,128)(2,1)S(1)} %get-tuple-element.42), channel_id=1, source_target_pairs={{0,48},{16,0},{32,16},{48,32},{1,49},{17,1},{33,17},{49,33},{2,50}... | collective-permute-start | bytes 393224 | tf_op jit(solution)/shard_map/ppermute | solution.py:352
  88.6 16.2 %copy-start.3 = (bf16[1,256,256]{2,1,0:T(8,128)(2,1)S(1)}, bf16[1,256,256]{2,1,0:T(8,128)(2,1)}, u32[]{:S(2)}) copy-start(bf16[1,256,256]{2,1,0:T(8,128)(2,1)} %param.9) | copy-start | bytes 393220
  88.6 16.2 %copy-start.4 = (s32[1,256]{1,0:T(1,128)S(1)}, s32[1,256]{1,0:T(1,128)}, u32[]{:S(2)}) copy-start(s32[1,256]{1,0:T(1,128)} %refs_5_.1) | copy-start | bytes 3076
  98.6 8.3 %collective-permute-start.5 = (bf16[4,272,256]{2,1,0:T(8,128)(2,1)S(1)}, bf16[4,272,256]{2,1,0:T(8,128)(2,1)S(1)}, u32[]{:S(2)}, u32[]{:S(2)}) collective-permute-start(bf16[4,272,256]{2,1,0:T(8,128)(2,1)S(1)} %all_to_all.27.got), channel_id=1, source_target_pairs={{0,8},{8,0},{1,9},{9,1},{2,10},{10,2},{3,11},{11,3},{4,12},{12,4},... | collective-permute-start | bytes 1671176 | tf_op jit(solution)/shard_map/ppermute | solution.py:290

commit v10 on v9

--- a/solution.py
+++ b/solution.py
@@ -103,32 +103,48 @@
         copy.wait()
 
 
-def turn_kernel(got, sent):
-    chips, width = got.shape[0], got.shape[2]
-    shard = got.shape[1] - sent.shape[1] // chips * 2
+def turn_kernel(spot, got, sent):
+    chips = got.shape[0]
+    shard = got.shape[1] - 2 * ROWS
     pieces = [got[chip, shard:, :].astype(F32) for chip in range(chips)]
-    rows = sent.shape[1] // chips
-    grads = jnp.concatenate([piece[:rows] for piece in pieces], axis=0)
-    extras = jnp.concatenate([piece[rows:] for piece in pieces], axis=0)
+    blank = jnp.zeros((ROWS, HEAD), F32)
     for core in range(2):
         cols = slice(core * HEAD, (core + 1) * HEAD)
-        both = jnp.concatenate([grads[:, cols], extras[:, cols]], axis=1).astype(BF16)
+        early, late = [], []
+        for piece in pieces:
+            early += [piece[ROWS:, cols], blank]
+            late += [blank, piece[ROWS:, cols]]
+        early, late = jnp.concatenate(early, axis=0), jnp.concatenate(late, axis=0)
+        placed = jnp.where(spot[1] == 0, early, late)
+        empty = jnp.zeros_like(placed)
+        placed = jnp.concatenate(
+            [jnp.where(spot[0] == 0, placed, empty), jnp.where(spot[0] == 0, empty, placed)], axis=0
+        )
+        both = [piece[:ROWS, cols] for piece in pieces] + [placed.T[:ROWS]]
+        both = jnp.concatenate(both, axis=0).astype(BF16)
         for group in range(sent.shape[0] // 2):
             sent[2 * group + core] = both
 
 
 def latent_order(got, chips):
-    rows = got.shape[1] // chips
     blocks = [got[at].astype(F32) for at in range(got.shape[0])]
-    return jnp.concatenate(
+    rows = [
+        blocks[2 * group + core][chip * ROWS : (chip + 1) * ROWS]
+        for group in range(got.shape[0] // 2)
+        for chip in range(chips)
+        for core in range(2)
+    ]
+    tails = [block[chips * ROWS :] for block in blocks]
+    lines = jnp.concatenate(
         [
-            blocks[2 * group + core][chip * rows : (chip + 1) * rows]
-            for group in range(got.shape[0] // 2)
-            for chip in range(chips)
-            for core in range(2)
+            tails[at] + tails[at + 1] + tails[at + 2] + tails[at + 3]
+            for at in range(0, len(tails), 4)
         ],
-        axis=0,
-    )
+        axis=1,
+    )
+    lse = (lines[0:1] + lines[1:2] + lines[2:3]) * LOG2E
+    delta = lines[3:4] + lines[4:5] + lines[5:6]
+    return jnp.concatenate(rows, axis=0).astype(BF16), lse, delta
 
 
 def share_kernel(head, keep, give, w_key, w_value, kept, given):
@@ -145,11 +161,7 @@
     cols = columns_of(head)
     chips, shard = keep.shape[0], keep.shape[1]
     scale = 1.0 / math.sqrt(HEAD)
-    rows = latent_order(got, chips)
-    grad = rows[:, :HEAD].astype(BF16)
-    extra = rows[:, HEAD:].T
-    lse = (extra[0:1] + extra[1:2] + extra[2:3]) * LOG2E
-    delta = extra[3:4] + extra[4:5] + extra[5:6]
+    grad, lse, delta = latent_order(got, chips)
     queries = query[:, cols]
     weights = jnp.concatenate([w_key[:, cols], w_value[:, cols]], axis=1)
     per = BLOCK // shard
@@ -298,8 +310,11 @@
     heads = lse.shape[1]
     core, chip, group = (lax.axis_index(at).astype(jnp.int32) for at in ("c", "x", "z"))
     head = (2 * chip + core).reshape(1)
+    spot = jnp.stack([lax.rem(group, 2), core])
     core, chip, group = core.reshape(1), chip.reshape(1), group.reshape(1)
-    tokens, head, core, chip, group = lax.optimization_barrier((tokens, head, core, chip, group))
+    tokens, head, core, chip, group, spot = lax.optimization_barrier(
+        (tokens, head, core, chip, group, spot)
+    )
     sent = pl.pallas_call(
         pack_kernel,
         out_shape=pltpu.HBM((chips, shard + 2 * rows, width), BF16),
@@ -315,11 +330,11 @@
     other = sibling(got)
     grads = pl.pallas_call(
         turn_kernel,
-        out_shape=shape((2 * groups, rows * chips, width)),
-        in_specs=[VMEM],
+        out_shape=shape((2 * groups, (chips + 1) * rows, HEAD)),
+        in_specs=[SMEM, VMEM],
         out_specs=VMEM,
         compiler_params=params(8),
-    )(got)
+    )(spot, got)
     grads = swap(grads, ("z", "c"))
 
     back = (chips, shard, width)
@@ -349,8 +364,8 @@
         compiler_params=params(16),
     )(chip, kept, sibling(given))
     shares = [shares[0]] + [
-        lax.ppermute(share, "x", [(at, (at + ahead) % chips) for at in range(chips)])
-        for ahead, share in enumerate(shares[1:], 1)
+        lax.ppermute(shares[ahead], "x", [(at, (at + ahead) % chips) for at in range(chips)])
+        for ahead in (2, 1, 3)
     ]
     parts = swap(parts, ("z", "y"))
     parts = pl.pallas_call(

time: 109 us -> 108 us (level)
  blocking collectives: 41 us -> 39.4 us
  waiting for transfers between devices: 13.4 us -> 12.3 us
    all_to_all x3, blocking collectives: 41 us -> 39.4 us  [swap(): return lax.all_to_all(array, axis, 0, 0, tiled=True)]
  transfers between devices with their start and end apart: 8 -> 8, of which waited for: 3 -> 2; matrix products, arithmetic and copies ran while one was open for 0% -> 0% of each run, Pallas kernels for 4% -> 4%
where the time goes in v10:
time: 108 us; the launch traced here: 107 us
  starting transfers between devices  41.1 us (38%)
  blocking collectives  39.4 us (36%)
  Pallas kernels  13 us (12%)
  waiting for transfers between devices  12.3 us (11%)
  between operations  1.48 us (1%)
    all_to_all x3, blocking collectives, swap(): return lax.all_to_all(array, axis, 0, 0, tiled=True)  39.4 us
    ppermute x3, starting transfers between devices, sibling(): return lax.ppermute(array, 'c', ((0, 1), (1, 0)))  17.9 us
    all_to_all x2, starting transfers between devices, swap(): return lax.all_to_all(array, axis, 0, 0, tiled=True)  14 us
    all_to_all x2, waiting for transfers between devices, swap(): return lax.all_to_all(array, axis, 0, 0, tiled=True)  12.3 us
    ppermute x3, starting transfers between devices, body(): lax.ppermute(shares[ahead], 'x', [(at, (at + ahead) % chips) for at in ra...  9.2 us
    pallas_call x1, Pallas kernels, body(): pl.pallas_call(main_kernel, out_shape=(shape(back), shape(back), shape(pa...  4.58 us
  transfers between devices with their start and end apart: 8, of which 2 were waited for; matrix products, arithmetic and copies ran while one was open for 0% of the time, Pallas kernels for 4%

profile of v10, /device:TPU:1, one launch (start us, length us, event | category | flops | bytes accessed | tf_op | source)
XLA Modules:
  0.0 107.4 jit_solution(9288081729614029265)
XLA Ops:
  1.3 0.1 pad_add_fusion.spot
  1.4 2.0 %shard_map.120 = bf16[4,272,256]{2,1,0:T(8,128)(2,1)} custom-call(s32[1,1]{1,0:T(1,128)S(6)} %copy.17.refs_0_.counts, bf16[256,256]{1,0:T(8,128)(2,1)} %bitcast.10, s32[1,256]{1,0:T(1,128)} %refs_5_.1, bf16[8,1024]{1,0:T(8,128)(2,1)} %bitcast.12, bf16[8,1024]{1,0:T(8,128)(2,1)} %bitcast.13, f32[8,8]{1,0:T(8,128)} %bitcast.14), custom_call_target="tpu_custom_call" | custom-call | tf_op jit(solution)/shard_map/pallas_call | solution.py:318
  3.3 0.0 copy-start.2
  3.4 12.1 %all_to_all.25.got.mine = bf16[4,272,256]{2,1,0:T(8,128)(2,1)S(1)} all-to-all(bf16[4,272,256]{2,1,0:T(8,128)(2,1)} %shard_map.120), channel_id=1, replica_groups=mesh['z'=8,'x'=4,'c'=2,'y'=8] {'x'}, dimensions={0} | all-to-all | bytes 1114112 | tf_op jit(solution)/shard_map/all_to_all | solution.py:294
  15.4 0.0 copy-start
  15.4 0.0 copy-start.1
  15.5 8.7 %collective-permute-start = (bf16[4,272,256]{2,1,0:T(8,128)(2,1)S(1)}, bf16[4,272,256]{2,1,0:T(8,128)(2,1)S(1)}, u32[]{:S(2)}, u32[]{:S(2)}) collective-permute-start(bf16[4,272,256]{2,1,0:T(8,128)(2,1)S(1)} %all_to_all.25.got.mine), channel_id=1, source_target_pairs={{0,8},{8,0},{1,9},{9,1},{2,10},{10,2},{3,11},{11,3},{4,12},{12,4},... | collective-permute-start | bytes 1671176 | tf_op jit(solution)/shard_map/ppermute | solution.py:302
  24.1 0.6 shard_map.121
  24.7 16.9 %all_to_all.26.got = bf16[16,40,128]{2,1,0:T(8,128)(2,1)S(1)} all-to-all(bf16[16,40,128]{2,1,0:T(8,128)(2,1)S(1)} %shard_map.121), channel_id=1, replica_groups=mesh['z'=8,'x'=4,'c'=2,'y'=8] {'z','c'}, dimensions={0} | all-to-all | bytes 327680 | tf_op jit(solution)/shard_map/all_to_all | solution.py:294
  41.7 0.0 collective-permute-done.other
  41.7 0.0 copy-done.2
  41.7 0.0 copy-done
  41.7 0.0 copy-done.1
  41.7 4.6 %shard_map.122 = (bf16[4,256,256]{2,1,0:T(8,128)(2,1)S(1)}, bf16[4,256,256]{2,1,0:T(8,128)(2,1)S(1)}, bf16[64,8,256]{2,1,0:T(8,128)(2,1)}) custom-call(s32[1]{0:T(128)} %bitcast.1.head, bf16[4,272,256]{2,1,0:T(8,128)(2,1)S(1)} %all_to_all.25.got.mine, bf16[4,272,256]{2,1,0:T(8,128)(2,1)S(1)} %collective-permute-done.other, ...), custom_call_target="tpu_custom_call" | custom-call | tf_op jit(solution)/shard_map/pallas_call | solution.py:343
  46.3 8.4 %all-to-all-start.2 = ((bf16[64,8,256]{2,1,0:T(8,128)(2,1)}), bf16[64,8,256]{2,1,0:T(8,128)(2,1)S(1)}, u32[]{:S(2)}, u32[]{:S(2)}) async-start(bf16[64,8,256]{2,1,0:T(8,128)(2,1)} %get-tuple-element.35), calls=%async_computation.2 | async-start | bytes 524288 | tf_op jit(solution)/shard_map/all_to_all | solution.py:294
  54.7 1.3 %shard_map.125 = (f32[4,256,256]{2,1,0:T(8,128)S(1)}, bf16[4,256,256]{2,1,0:T(8,128)(2,1)}) custom-call(s32[1]{0:T(128)} %bitcast.1.head, bf16[4,256,256]{2,1,0:T(8,128)(2,1)S(1)} %get-tuple-element.37.keep, bf16[4,256,256]{2,1,0:T(8,128)(2,1)S(1)} %get-tuple-element.38.give, bf16[256,1024]{1,0:T(8,128)(2,1)S(1)} %copy-done, bf16[256,1024]{1,0:T(8,128)(2,1)S(1)} %copy-done.1), custom_call_target="tpu_custom_call" | custom-call | flops 270000000 | bytes 3000000 | tf_op jit(solution)/shard_map/pallas_call | solution.py:351
  56.0 2.6 %collective-permute-start.1 = (bf16[4,256,256]{2,1,0:T(8,128)(2,1)}, bf16[4,256,256]{2,1,0:T(8,128)(2,1)S(1)}, u32[]{:S(2)}, u32[]{:S(2)}) collective-permute-start(bf16[4,256,256]{2,1,0:T(8,128)(2,1)} %get-tuple-element.40), channel_id=1, source_target_pairs={{0,8},{8,0},{1,9},{9,1},{2,10},{10,2},{3,11},{11,3},{4,12},{12,4},... | collective-permute-start | bytes 1572872 | tf_op jit(solution)/shard_map/ppermute | solution.py:302
  58.6 9.1 %all-to-all-done.2.got = bf16[64,8,256]{2,1,0:T(8,128)(2,1)S(1)} async-done(((bf16[64,8,256]{2,1,0:T(8,128)(2,1)}), bf16[64,8,256]{2,1,0:T(8,128)(2,1)S(1)}, u32[]{:S(2)}, u32[]{:S(2)}) %all-to-all-start.2) | async-done | bytes 262176 | tf_op jit(solution)/shard_map/all_to_all | solution.py:294
  67.7 0.8 shard_map.123
  68.5 5.6 %all-to-all-start.3 = ((bf16[64,8,256]{2,1,0:T(8,128)(2,1)}), bf16[64,8,256]{2,1,0:T(8,128)(2,1)S(1)}, u32[]{:S(2)}, u32[]{:S(2)}) async-start(bf16[64,8,256]{2,1,0:T(8,128)(2,1)} %shard_map.123), calls=%async_computation.3 | async-start | bytes 524288 | tf_op jit(solution)/shard_map/all_to_all | solution.py:294
  74.1 0.0 collective-permute-done.1.theirs
  74.1 0.1 shard_map.126
  74.2 2.7 %collective-permute-start.2 = (bf16[256,256]{1,0:T(8,128)(2,1)S(1)}, bf16[256,256]{1,0:T(8,128)(2,1)S(1)}, u32[]{:S(2)}, u32[]{:S(2)}) collective-permute-start(bf16[256,256]{1,0:T(8,128)(2,1)S(1)} %get-tuple-element.42), channel_id=1, source_target_pairs={{0,32},{16,48},{32,0},{48,16},{1,33},{17,49},{33,1},{49,17},{2,34}... | collective-permute-start | bytes 393224 | tf_op jit(solution)/shard_map/ppermute | solution.py:367
  76.9 2.6 %collective-permute-start.3 = (bf16[256,256]{1,0:T(8,128)(2,1)S(1)}, bf16[256,256]{1,0:T(8,128)(2,1)S(1)}, u32[]{:S(2)}, u32[]{:S(2)}) collective-permute-start(bf16[256,256]{1,0:T(8,128)(2,1)S(1)} %get-tuple-element.43), channel_id=1, source_target_pairs={{0,16},{16,32},{32,48},{48,0},{1,17},{17,33},{33,49},{49,1},{2,18}... | collective-permute-start | bytes 393224 | tf_op jit(solution)/shard_map/ppermute | solution.py:367
  79.5 3.9 %collective-permute-start.4 = (bf16[256,256]{1,0:T(8,128)(2,1)S(1)}, bf16[256,256]{1,0:T(8,128)(2,1)S(1)}, u32[]{:S(2)}, u32[]{:S(2)}) collective-permute-start(bf16[256,256]{1,0:T(8,128)(2,1)S(1)} %get-tuple-element.44), channel_id=1, source_target_pairs={{0,48},{16,0},{32,16},{48,32},{1,49},{17,1},{33,17},{49,33},{2,50}... | collective-permute-start | bytes 393224 | tf_op jit(solution)/shard_map/ppermute | solution.py:367
  83.4 3.2 %all-to-all-done.3.got = bf16[64,8,256]{2,1,0:T(8,128)(2,1)S(1)} async-done(((bf16[64,8,256]{2,1,0:T(8,128)(2,1)}), bf16[64,8,256]{2,1,0:T(8,128)(2,1)S(1)}, u32[]{:S(2)}, u32[]{:S(2)}) %all-to-all-start.3) | async-done | bytes 262176 | tf_op jit(solution)/shard_map/all_to_all | solution.py:294
  86.6 0.0 collective-permute-done.2.refs_1_
  86.6 0.0 collective-permute-done.3.refs_2_
  86.7 0.0 collective-permute-done.4.refs_3_
  86.7 0.0 copy-start.3
  86.7 0.0 copy-start.4
  86.7 10.3 %all_to_all.27.got = bf16[4,272,256]{2,1,0:T(8,128)(2,1)S(1)} all-to-all(bf16[4,272,256]{2,1,0:T(8,128)(2,1)S(1)} %shard_map.124), channel_id=1, replica_groups=mesh['z'=8,'x'=4,'c'=2,'y'=8] {'x'}, dimensions={0} | all-to-all | bytes 1114112 | tf_op jit(solution)/shard_map/all_to_all | solution.py:294
  97.0 6.6 %collective-permute-start.5 = (bf16[4,272,256]{2,1,0:T(8,128)(2,1)S(1)}, bf16[4,272,256]{2,1,0:T(8,128)(2,1)S(1)}, u32[]{:S(2)}, u32[]{:S(2)}) collective-permute-start(bf16[4,272,256]{2,1,0:T(8,128)(2,1)S(1)} %all_to_all.27.got), channel_id=1, source_target_pairs={{0,8},{8,0},{1,9},{9,1},{2,10},{10,2},{3,11},{11,3},{4,12},{12,4},... | collective-permute-start | bytes 1671176 | tf_op jit(solution)/shard_map/ppermute | solution.py:302
  103.7 0.0 copy-done.3
  103.7 0.0 copy-done.4
  103.7 2.0 %shard_map.127 = (bf16[256,256]{1,0:T(8,128)(2,1)}, f32[256,1024]{1,0:T(8,128)}, f32[256,1024]{1,0:T(8,128)}) custom-call(s32[1]{0:T(128)} %bitcast.2.core, s32[1,1]{1,0:T(1,128)S(6)} %copy.17.refs_0_.counts, bf16[4,272,256]{2,1,0:T(8,128)(2,1)S(1)} %all_to_all.27.got, bf16[256,256]{1,0:T(8,128)(2,1)S(1)} %get-tuple-element.46.refs_0_, ...), custom_call_target="tpu_custom_call" | custom-call | flops 2000000 | bytes 3000000 | tf_op jit(solution)/shard_map/pallas_call | solution.py:395
  105.7 0.0 collective-permute-done.5.other
  105.7 1.7 %shard_map.128 = (f32[8,1024]{1,0:T(8,128)}, f32[256,1024]{1,0:T(8,128)}, f32[256,1024]{1,0:T(8,128)}) custom-call(s32[1]{0:T(128)} %bitcast.2.core, bf16[4,272,256]{2,1,0:T(8,128)(2,1)S(1)} %all_to_all.27.got, bf16[4,272,256]{2,1,0:T(8,128)(2,1)S(1)} %collective-permute-done.5.other, ...), custom_call_target="tpu_custom_call", output_to_operand_aliasing={{1}: (3, {}), {2}: (4, {})} | custom-call | tf_op jit(solution)/shard_map/pallas_call | solution.py:404
  (1 shorter events, 0.0 us)
Async XLA Ops:
  3.3 38.3 %copy-start.2 = (bf16[512,1024]{1,0:T(8,128)(2,1)S(1)}, bf16[512,1024]{1,0:T(8,128)(2,1)}, u32[]{:S(2)}) copy-start(bf16[512,1024]{1,0:T(8,128)(2,1)} %query.1) | copy-start | bytes 3145732
  15.4 26.2 %copy-start = (bf16[256,1024]{1,0:T(8,128)(2,1)S(1)}, bf16[256,1024]{1,0:T(8,128)(2,1)}, u32[]{:S(2)}) copy-start(bf16[256,1024]{1,0:T(8,128)(2,1)} %w_key.3) | copy-start | bytes 1572868
  15.4 26.2 %copy-start.1 = (bf16[256,1024]{1,0:T(8,128)(2,1)S(1)}, bf16[256,1024]{1,0:T(8,128)(2,1)}, u32[]{:S(2)}) copy-start(bf16[256,1024]{1,0:T(8,128)(2,1)} %w_value.3) | copy-start | bytes 1572868
  15.5 26.2 %collective-permute-start = (bf16[4,272,256]{2,1,0:T(8,128)(2,1)S(1)}, bf16[4,272,256]{2,1,0:T(8,128)(2,1)S(1)}, u32[]{:S(2)}, u32[]{:S(2)}) collective-permute-start(bf16[4,272,256]{2,1,0:T(8,128)(2,1)S(1)} %all_to_all.25.got.mine), channel_id=1, source_target_pairs={{0,8},{8,0},{1,9},{9,1},{2,10},{10,2},{3,11},{11,3},{4,12},{12,4},... | collective-permute-start | bytes 1671176 | tf_op jit(solution)/shard_map/ppermute | solution.py:302
  46.3 21.4 %all-to-all-start.2 = ((bf16[64,8,256]{2,1,0:T(8,128)(2,1)}), bf16[64,8,256]{2,1,0:T(8,128)(2,1)S(1)}, u32[]{:S(2)}, u32[]{:S(2)}) async-start(bf16[64,8,256]{2,1,0:T(8,128)(2,1)} %get-tuple-element.35), calls=%async_computation.2 | async-start | bytes 524288 | tf_op jit(solution)/shard_map/all_to_all | solution.py:294
  56.0 18.1 %collective-permute-start.1 = (bf16[4,256,256]{2,1,0:T(8,128)(2,1)}, bf16[4,256,256]{2,1,0:T(8,128)(2,1)S(1)}, u32[]{:S(2)}, u32[]{:S(2)}) collective-permute-start(bf16[4,256,256]{2,1,0:T(8,128)(2,1)} %get-tuple-element.40), channel_id=1, source_target_pairs={{0,8},{8,0},{1,9},{9,1},{2,10},{10,2},{3,11},{11,3},{4,12},{12,4},... | collective-permute-start | bytes 1572872 | tf_op jit(solution)/shard_map/ppermute | solution.py:302
  68.5 18.1 %all-to-all-start.3 = ((bf16[64,8,256]{2,1,0:T(8,128)(2,1)}), bf16[64,8,256]{2,1,0:T(8,128)(2,1)S(1)}, u32[]{:S(2)}, u32[]{:S(2)}) async-start(bf16[64,8,256]{2,1,0:T(8,128)(2,1)} %shard_map.123), calls=%async_computation.3 | async-start | bytes 524288 | tf_op jit(solution)/shard_map/all_to_all | solution.py:294
  74.2 12.4 %collective-permute-start.2 = (bf16[256,256]{1,0:T(8,128)(2,1)S(1)}, bf16[256,256]{1,0:T(8,128)(2,1)S(1)}, u32[]{:S(2)}, u32[]{:S(2)}) collective-permute-start(bf16[256,256]{1,0:T(8,128)(2,1)S(1)} %get-tuple-element.42), channel_id=1, source_target_pairs={{0,32},{16,48},{32,0},{48,16},{1,33},{17,49},{33,1},{49,17},{2,34}... | collective-permute-start | bytes 393224 | tf_op jit(solution)/shard_map/ppermute | solution.py:367
  76.9 9.7 %collective-permute-start.3 = (bf16[256,256]{1,0:T(8,128)(2,1)S(1)}, bf16[256,256]{1,0:T(8,128)(2,1)S(1)}, u32[]{:S(2)}, u32[]{:S(2)}) collective-permute-start(bf16[256,256]{1,0:T(8,128)(2,1)S(1)} %get-tuple-element.43), channel_id=1, source_target_pairs={{0,16},{16,32},{32,48},{48,0},{1,17},{17,33},{33,49},{49,1},{2,18}... | collective-permute-start | bytes 393224 | tf_op jit(solution)/shard_map/ppermute | solution.py:367
  79.5 7.2 %collective-permute-start.4 = (bf16[256,256]{1,0:T(8,128)(2,1)S(1)}, bf16[256,256]{1,0:T(8,128)(2,1)S(1)}, u32[]{:S(2)}, u32[]{:S(2)}) collective-permute-start(bf16[256,256]{1,0:T(8,128)(2,1)S(1)} %get-tuple-element.44), channel_id=1, source_target_pairs={{0,48},{16,0},{32,16},{48,32},{1,49},{17,1},{33,17},{49,33},{2,50}... | collective-permute-start | bytes 393224 | tf_op jit(solution)/shard_map/ppermute | solution.py:367
  86.7 17.0 %copy-start.3 = (bf16[1,256,256]{2,1,0:T(8,128)(2,1)S(1)}, bf16[1,256,256]{2,1,0:T(8,128)(2,1)}, u32[]{:S(2)}) copy-start(bf16[1,256,256]{2,1,0:T(8,128)(2,1)} %param.9) | copy-start | bytes 393220
  86.7 17.0 %copy-start.4 = (s32[1,256]{1,0:T(1,128)S(1)}, s32[1,256]{1,0:T(1,128)}, u32[]{:S(2)}) copy-start(s32[1,256]{1,0:T(1,128)} %refs_5_.1) | copy-start | bytes 3076
  97.0 8.7 %collective-permute-start.5 = (bf16[4,272,256]{2,1,0:T(8,128)(2,1)S(1)}, bf16[4,272,256]{2,1,0:T(8,128)(2,1)S(1)}, u32[]{:S(2)}, u32[]{:S(2)}) collective-permute-start(bf16[4,272,256]{2,1,0:T(8,128)(2,1)S(1)} %all_to_all.27.got), channel_id=1, source_target_pairs={{0,8},{8,0},{1,9},{9,1},{2,10},{10,2},{3,11},{11,3},{4,12},{12,4},... | collective-permute-start | bytes 1671176 | tf_op jit(solution)/shard_map/ppermute | solution.py:302

commit v11 on v10

--- a/solution.py
+++ b/solution.py
@@ -87,7 +87,7 @@
             delta = jnp.sum(grad_f32 * out[:, cols].astype(F32), axis=1, keepdims=True)
             extra = jnp.zeros((rows, HEAD), F32)
             for at, part in enumerate(three_parts(lse[:, head : head + 1]) + three_parts(delta)):
-                extra = jnp.where(lane == at, part, extra)
+                extra = jnp.where(lane == at + head % 2 * ROWS, part, extra)
             extras.append(extra)
             grads.append(grad_f32)
         both = jnp.concatenate(
@@ -108,20 +108,21 @@
     shard = got.shape[1] - 2 * ROWS
     pieces = [got[chip, shard:, :].astype(F32) for chip in range(chips)]
     blank = jnp.zeros((ROWS, HEAD), F32)
+    early, late = [], []
+    for piece in pieces:
+        tail = piece[ROWS:, :HEAD] + piece[ROWS:, HEAD:]
+        early += [tail, blank]
+        late += [blank, tail]
+    early, late = jnp.concatenate(early, axis=0), jnp.concatenate(late, axis=0)
+    placed = jnp.where(spot[1] == 0, early, late)
+    empty = jnp.zeros_like(placed)
+    lines = jnp.concatenate(
+        [jnp.where(spot[0] == 0, placed, empty), jnp.where(spot[0] == 0, empty, placed)], axis=0
+    ).T
     for core in range(2):
         cols = slice(core * HEAD, (core + 1) * HEAD)
-        early, late = [], []
-        for piece in pieces:
-            early += [piece[ROWS:, cols], blank]
-            late += [blank, piece[ROWS:, cols]]
-        early, late = jnp.concatenate(early, axis=0), jnp.concatenate(late, axis=0)
-        placed = jnp.where(spot[1] == 0, early, late)
-        empty = jnp.zeros_like(placed)
-        placed = jnp.concatenate(
-            [jnp.where(spot[0] == 0, placed, empty), jnp.where(spot[0] == 0, empty, placed)], axis=0
-        )
-        both = [piece[:ROWS, cols] for piece in pieces] + [placed.T[:ROWS]]
-        both = jnp.concatenate(both, axis=0).astype(BF16)
+        both = [piece[:ROWS, cols] for piece in pieces]
+        both = jnp.concatenate(both + [lines[core * ROWS : (core + 1) * ROWS]], axis=0).astype(BF16)
         for group in range(sent.shape[0] // 2):
             sent[2 * group + core] = both
 
@@ -194,7 +195,8 @@
     for at in range(parts.shape[0]):
         start = at % halves * ROWS
         cols = slice(at // halves * HEAD, (at // halves + 1) * HEAD)
-        piece = [totals[start : start + ROWS, cols], turned[at * ROWS : (at + 1) * ROWS]]
+        query_at = (at % 8 * 8 + at // 8) * ROWS
+        piece = [totals[start : start + ROWS, cols], turned[query_at : query_at + ROWS]]
         parts[at] = jnp.concatenate(piece, axis=1).astype(BF16)
 
 
@@ -228,8 +230,9 @@
     ).astype(BF16)
     for chip in range(chips):
         sent[chip, :depth, :] = weights
-        first = group[0] * 2 * chips + 2 * chip
-        rows = [got[first + core].astype(F32) for core in range(2)]
+        rows = [
+            got[(2 * chip + core) * 2 * chips + group[0]].astype(F32) for core in range(2)
+        ]
         sent[chip, depth:, :] = jnp.concatenate(rows, axis=0).astype(BF16)
 
 
@@ -367,7 +370,7 @@
         lax.ppermute(shares[ahead], "x", [(at, (at + ahead) % chips) for at in range(chips)])
         for ahead in (2, 1, 3)
     ]
-    parts = swap(parts, ("z", "y"))
+    parts = swap(parts, ("y", "z"))
     parts = pl.pallas_call(
         spread_kernel,
         out_shape=shape(part),
@@ -375,7 +378,7 @@
         out_specs=VMEM,
         compiler_params=params(8),
     )(parts)
-    parts = swap(parts, ("z", "y"))
+    parts = swap(parts, ("y", "z"))
     last = (chips, width + 2 * rows, width)
     sent = pl.pallas_call(
         gather_kernel,

time: 108 us -> 108 us (level)
  no operation moved by 1% of the time
where the time goes in v11:
time: 108 us; the launch traced here: 107 us
  starting transfers between devices  41.1 us (38%)
  blocking collectives  39.4 us (36%)
  Pallas kernels  13 us (12%)
  waiting for transfers between devices  12.3 us (11%)
  between operations  1.48 us (1%)
    all_to_all x3, blocking collectives, swap(): return lax.all_to_all(array, axis, 0, 0, tiled=True)  39.4 us
    ppermute x3, starting transfers between devices, sibling(): return lax.ppermute(array, 'c', ((0, 1), (1, 0)))  17.9 us
    all_to_all x2, starting transfers between devices, swap(): return lax.all_to_all(array, axis, 0, 0, tiled=True)  14 us
    all_to_all x2, waiting for transfers between devices, swap(): return lax.all_to_all(array, axis, 0, 0, tiled=True)  12.3 us
    ppermute x3, starting transfers between devices, body(): lax.ppermute(shares[ahead], 'x', [(at, (at + ahead) % chips) for at in ra...  9.2 us
    pallas_call x1, Pallas kernels, body(): pl.pallas_call(main_kernel, out_shape=(shape(back), shape(back), shape(pa...  4.58 us
  transfers between devices with their start and end apart: 8, of which 2 were waited for; matrix products, arithmetic and copies ran while one was open for 0% of the time, Pallas kernels for 4%

profile of v11, /device:TPU:1, one launch (start us, length us, event | category | flops | bytes accessed | tf_op | source)
XLA Modules:
  0.0 107.4 jit_solution(17050050130272919129)
XLA Ops:
  1.3 0.1 pad_add_fusion.spot
  1.4 2.0 %shard_map.120 = bf16[4,272,256]{2,1,0:T(8,128)(2,1)} custom-call(s32[1,1]{1,0:T(1,128)S(6)} %copy.17.refs_0_.counts, bf16[256,256]{1,0:T(8,128)(2,1)} %bitcast.10, s32[1,256]{1,0:T(1,128)} %refs_5_.1, bf16[8,1024]{1,0:T(8,128)(2,1)} %bitcast.12, bf16[8,1024]{1,0:T(8,128)(2,1)} %bitcast.13, f32[8,8]{1,0:T(8,128)} %bitcast.14), custom_call_target="tpu_custom_call" | custom-call | tf_op jit(solution)/shard_map/pallas_call | solution.py:321
  3.3 0.0 copy-start.2
  3.4 12.1 %all_to_all.25.got.mine = bf16[4,272,256]{2,1,0:T(8,128)(2,1)S(1)} all-to-all(bf16[4,272,256]{2,1,0:T(8,128)(2,1)} %shard_map.120), channel_id=1, replica_groups=mesh['z'=8,'x'=4,'c'=2,'y'=8] {'x'}, dimensions={0} | all-to-all | bytes 1114112 | tf_op jit(solution)/shard_map/all_to_all | solution.py:297
  15.4 0.0 copy-start
  15.4 0.0 copy-start.1
  15.5 8.7 %collective-permute-start = (bf16[4,272,256]{2,1,0:T(8,128)(2,1)S(1)}, bf16[4,272,256]{2,1,0:T(8,128)(2,1)S(1)}, u32[]{:S(2)}, u32[]{:S(2)}) collective-permute-start(bf16[4,272,256]{2,1,0:T(8,128)(2,1)S(1)} %all_to_all.25.got.mine), channel_id=1, source_target_pairs={{0,8},{8,0},{1,9},{9,1},{2,10},{10,2},{3,11},{11,3},{4,12},{12,4},... | collective-permute-start | bytes 1671176 | tf_op jit(solution)/shard_map/ppermute | solution.py:305
  24.1 0.6 shard_map.121
  24.7 16.9 %all_to_all.26.got = bf16[16,40,128]{2,1,0:T(8,128)(2,1)S(1)} all-to-all(bf16[16,40,128]{2,1,0:T(8,128)(2,1)S(1)} %shard_map.121), channel_id=1, replica_groups=mesh['z'=8,'x'=4,'c'=2,'y'=8] {'z','c'}, dimensions={0} | all-to-all | bytes 327680 | tf_op jit(solution)/shard_map/all_to_all | solution.py:297
  41.7 0.0 collective-permute-done.other
  41.7 0.0 copy-done.2
  41.7 0.0 copy-done
  41.7 0.0 copy-done.1
  41.7 4.6 %shard_map.122 = (bf16[4,256,256]{2,1,0:T(8,128)(2,1)S(1)}, bf16[4,256,256]{2,1,0:T(8,128)(2,1)S(1)}, bf16[64,8,256]{2,1,0:T(8,128)(2,1)}) custom-call(s32[1]{0:T(128)} %bitcast.1.head, bf16[4,272,256]{2,1,0:T(8,128)(2,1)S(1)} %all_to_all.25.got.mine, bf16[4,272,256]{2,1,0:T(8,128)(2,1)S(1)} %collective-permute-done.other, ...), custom_call_target="tpu_custom_call" | custom-call | tf_op jit(solution)/shard_map/pallas_call | solution.py:346
  46.3 8.4 %all-to-all-start.2 = ((bf16[64,8,256]{2,1,0:T(8,128)(2,1)}), bf16[64,8,256]{2,1,0:T(8,128)(2,1)S(1)}, u32[]{:S(2)}, u32[]{:S(2)}) async-start(bf16[64,8,256]{2,1,0:T(8,128)(2,1)} %get-tuple-element.35), calls=%async_computation.2 | async-start | bytes 524288 | tf_op jit(solution)/shard_map/all_to_all | solution.py:297
  54.7 1.3 %shard_map.125 = (f32[4,256,256]{2,1,0:T(8,128)S(1)}, bf16[4,256,256]{2,1,0:T(8,128)(2,1)}) custom-call(s32[1]{0:T(128)} %bitcast.1.head, bf16[4,256,256]{2,1,0:T(8,128)(2,1)S(1)} %get-tuple-element.37.keep, bf16[4,256,256]{2,1,0:T(8,128)(2,1)S(1)} %get-tuple-element.38.give, bf16[256,1024]{1,0:T(8,128)(2,1)S(1)} %copy-done, bf16[256,1024]{1,0:T(8,128)(2,1)S(1)} %copy-done.1), custom_call_target="tpu_custom_call" | custom-call | flops 270000000 | bytes 3000000 | tf_op jit(solution)/shard_map/pallas_call | solution.py:354
  56.0 2.6 %collective-permute-start.1 = (bf16[4,256,256]{2,1,0:T(8,128)(2,1)}, bf16[4,256,256]{2,1,0:T(8,128)(2,1)S(1)}, u32[]{:S(2)}, u32[]{:S(2)}) collective-permute-start(bf16[4,256,256]{2,1,0:T(8,128)(2,1)} %get-tuple-element.40), channel_id=1, source_target_pairs={{0,8},{8,0},{1,9},{9,1},{2,10},{10,2},{3,11},{11,3},{4,12},{12,4},... | collective-permute-start | bytes 1572872 | tf_op jit(solution)/shard_map/ppermute | solution.py:305
  58.6 9.2 %all-to-all-done.2.got = bf16[64,8,256]{2,1,0:T(8,128)(2,1)S(1)} async-done(((bf16[64,8,256]{2,1,0:T(8,128)(2,1)}), bf16[64,8,256]{2,1,0:T(8,128)(2,1)S(1)}, u32[]{:S(2)}, u32[]{:S(2)}) %all-to-all-start.2) | async-done | bytes 262176 | tf_op jit(solution)/shard_map/all_to_all | solution.py:297
  67.7 0.8 shard_map.123
  68.5 5.6 %all-to-all-start.3 = ((bf16[64,8,256]{2,1,0:T(8,128)(2,1)}), bf16[64,8,256]{2,1,0:T(8,128)(2,1)S(1)}, u32[]{:S(2)}, u32[]{:S(2)}) async-start(bf16[64,8,256]{2,1,0:T(8,128)(2,1)} %shard_map.123), calls=%async_computation.3 | async-start | bytes 524288 | tf_op jit(solution)/shard_map/all_to_all | solution.py:297
  74.1 0.0 collective-permute-done.1.theirs
  74.1 0.1 shard_map.126
  74.2 2.7 %collective-permute-start.2 = (bf16[256,256]{1,0:T(8,128)(2,1)S(1)}, bf16[256,256]{1,0:T(8,128)(2,1)S(1)}, u32[]{:S(2)}, u32[]{:S(2)}) collective-permute-start(bf16[256,256]{1,0:T(8,128)(2,1)S(1)} %get-tuple-element.42), channel_id=1, source_target_pairs={{0,32},{16,48},{32,0},{48,16},{1,33},{17,49},{33,1},{49,17},{2,34}... | collective-permute-start | bytes 393224 | tf_op jit(solution)/shard_map/ppermute | solution.py:370
  76.9 2.6 %collective-permute-start.3 = (bf16[256,256]{1,0:T(8,128)(2,1)S(1)}, bf16[256,256]{1,0:T(8,128)(2,1)S(1)}, u32[]{:S(2)}, u32[]{:S(2)}) collective-permute-start(bf16[256,256]{1,0:T(8,128)(2,1)S(1)} %get-tuple-element.43), channel_id=1, source_target_pairs={{0,16},{16,32},{32,48},{48,0},{1,17},{17,33},{33,49},{49,1},{2,18}... | collective-permute-start | bytes 393224 | tf_op jit(solution)/shard_map/ppermute | solution.py:370
  79.5 3.9 %collective-permute-start.4 = (bf16[256,256]{1,0:T(8,128)(2,1)S(1)}, bf16[256,256]{1,0:T(8,128)(2,1)S(1)}, u32[]{:S(2)}, u32[]{:S(2)}) collective-permute-start(bf16[256,256]{1,0:T(8,128)(2,1)S(1)} %get-tuple-element.44), channel_id=1, source_target_pairs={{0,48},{16,0},{32,16},{48,32},{1,49},{17,1},{33,17},{49,33},{2,50}... | collective-permute-start | bytes 393224 | tf_op jit(solution)/shard_map/ppermute | solution.py:370
  83.4 3.1 %all-to-all-done.3.got = bf16[64,8,256]{2,1,0:T(8,128)(2,1)S(1)} async-done(((bf16[64,8,256]{2,1,0:T(8,128)(2,1)}), bf16[64,8,256]{2,1,0:T(8,128)(2,1)S(1)}, u32[]{:S(2)}, u32[]{:S(2)}) %all-to-all-start.3) | async-done | bytes 262176 | tf_op jit(solution)/shard_map/all_to_all | solution.py:297
  86.6 0.0 collective-permute-done.2.refs_1_
  86.6 0.0 collective-permute-done.3.refs_2_
  86.6 0.0 collective-permute-done.4.refs_3_
  86.6 0.0 copy-start.3
  86.7 0.0 copy-start.4
  86.7 10.4 %all_to_all.27.got = bf16[4,272,256]{2,1,0:T(8,128)(2,1)S(1)} all-to-all(bf16[4,272,256]{2,1,0:T(8,128)(2,1)S(1)} %shard_map.124), channel_id=1, replica_groups=mesh['z'=8,'x'=4,'c'=2,'y'=8] {'x'}, dimensions={0} | all-to-all | bytes 1114112 | tf_op jit(solution)/shard_map/all_to_all | solution.py:297
  97.0 6.7 %collective-permute-start.5 = (bf16[4,272,256]{2,1,0:T(8,128)(2,1)S(1)}, bf16[4,272,256]{2,1,0:T(8,128)(2,1)S(1)}, u32[]{:S(2)}, u32[]{:S(2)}) collective-permute-start(bf16[4,272,256]{2,1,0:T(8,128)(2,1)S(1)} %all_to_all.27.got), channel_id=1, source_target_pairs={{0,8},{8,0},{1,9},{9,1},{2,10},{10,2},{3,11},{11,3},{4,12},{12,4},... | collective-permute-start | bytes 1671176 | tf_op jit(solution)/shard_map/ppermute | solution.py:305
  103.7 0.0 copy-done.3
  103.8 0.0 copy-done.4
  103.8 2.0 %shard_map.127 = (bf16[256,256]{1,0:T(8,128)(2,1)}, f32[256,1024]{1,0:T(8,128)}, f32[256,1024]{1,0:T(8,128)}) custom-call(s32[1]{0:T(128)} %bitcast.2.core, s32[1,1]{1,0:T(1,128)S(6)} %copy.17.refs_0_.counts, bf16[4,272,256]{2,1,0:T(8,128)(2,1)S(1)} %all_to_all.27.got, bf16[256,256]{1,0:T(8,128)(2,1)S(1)} %get-tuple-element.46.refs_0_, ...), custom_call_target="tpu_custom_call" | custom-call | flops 2000000 | bytes 3000000 | tf_op jit(solution)/shard_map/pallas_call | solution.py:398
  105.8 0.0 collective-permute-done.5.other
  105.8 1.7 %shard_map.128 = (f32[8,1024]{1,0:T(8,128)}, f32[256,1024]{1,0:T(8,128)}, f32[256,1024]{1,0:T(8,128)}) custom-call(s32[1]{0:T(128)} %bitcast.2.core, bf16[4,272,256]{2,1,0:T(8,128)(2,1)S(1)} %all_to_all.27.got, bf16[4,272,256]{2,1,0:T(8,128)(2,1)S(1)} %collective-permute-done.5.other, ...), custom_call_target="tpu_custom_call", output_to_operand_aliasing={{1}: (3, {}), {2}: (4, {})} | custom-call | tf_op jit(solution)/shard_map/pallas_call | solution.py:407
  (1 shorter events, 0.0 us)
Async XLA Ops:
  3.3 38.3 %copy-start.2 = (bf16[512,1024]{1,0:T(8,128)(2,1)S(1)}, bf16[512,1024]{1,0:T(8,128)(2,1)}, u32[]{:S(2)}) copy-start(bf16[512,1024]{1,0:T(8,128)(2,1)} %query.1) | copy-start | bytes 3145732
  15.4 26.2 %copy-start = (bf16[256,1024]{1,0:T(8,128)(2,1)S(1)}, bf16[256,1024]{1,0:T(8,128)(2,1)}, u32[]{:S(2)}) copy-start(bf16[256,1024]{1,0:T(8,128)(2,1)} %w_key.3) | copy-start | bytes 1572868
  15.4 26.2 %copy-start.1 = (bf16[256,1024]{1,0:T(8,128)(2,1)S(1)}, bf16[256,1024]{1,0:T(8,128)(2,1)}, u32[]{:S(2)}) copy-start(bf16[256,1024]{1,0:T(8,128)(2,1)} %w_value.3) | copy-start | bytes 1572868
  15.5 26.2 %collective-permute-start = (bf16[4,272,256]{2,1,0:T(8,128)(2,1)S(1)}, bf16[4,272,256]{2,1,0:T(8,128)(2,1)S(1)}, u32[]{:S(2)}, u32[]{:S(2)}) collective-permute-start(bf16[4,272,256]{2,1,0:T(8,128)(2,1)S(1)} %all_to_all.25.got.mine), channel_id=1, source_target_pairs={{0,8},{8,0},{1,9},{9,1},{2,10},{10,2},{3,11},{11,3},{4,12},{12,4},... | collective-permute-start | bytes 1671176 | tf_op jit(solution)/shard_map/ppermute | solution.py:305
  46.3 21.5 %all-to-all-start.2 = ((bf16[64,8,256]{2,1,0:T(8,128)(2,1)}), bf16[64,8,256]{2,1,0:T(8,128)(2,1)S(1)}, u32[]{:S(2)}, u32[]{:S(2)}) async-start(bf16[64,8,256]{2,1,0:T(8,128)(2,1)} %get-tuple-element.35), calls=%async_computation.2 | async-start | bytes 524288 | tf_op jit(solution)/shard_map/all_to_all | solution.py:297
  56.0 18.1 %collective-permute-start.1 = (bf16[4,256,256]{2,1,0:T(8,128)(2,1)}, bf16[4,256,256]{2,1,0:T(8,128)(2,1)S(1)}, u32[]{:S(2)}, u32[]{:S(2)}) collective-permute-start(bf16[4,256,256]{2,1,0:T(8,128)(2,1)} %get-tuple-element.40), channel_id=1, source_target_pairs={{0,8},{8,0},{1,9},{9,1},{2,10},{10,2},{3,11},{11,3},{4,12},{12,4},... | collective-permute-start | bytes 1572872 | tf_op jit(solution)/shard_map/ppermute | solution.py:305
  68.5 18.0 %all-to-all-start.3 = ((bf16[64,8,256]{2,1,0:T(8,128)(2,1)}), bf16[64,8,256]{2,1,0:T(8,128)(2,1)S(1)}, u32[]{:S(2)}, u32[]{:S(2)}) async-start(bf16[64,8,256]{2,1,0:T(8,128)(2,1)} %shard_map.123), calls=%async_computation.3 | async-start | bytes 524288 | tf_op jit(solution)/shard_map/all_to_all | solution.py:297
  74.2 12.4 %collective-permute-start.2 = (bf16[256,256]{1,0:T(8,128)(2,1)S(1)}, bf16[256,256]{1,0:T(8,128)(2,1)S(1)}, u32[]{:S(2)}, u32[]{:S(2)}) collective-permute-start(bf16[256,256]{1,0:T(8,128)(2,1)S(1)} %get-tuple-element.42), channel_id=1, source_target_pairs={{0,32},{16,48},{32,0},{48,16},{1,33},{17,49},{33,1},{49,17},{2,34}... | collective-permute-start | bytes 393224 | tf_op jit(solution)/shard_map/ppermute | solution.py:370
  76.9 9.7 %collective-permute-start.3 = (bf16[256,256]{1,0:T(8,128)(2,1)S(1)}, bf16[256,256]{1,0:T(8,128)(2,1)S(1)}, u32[]{:S(2)}, u32[]{:S(2)}) collective-permute-start(bf16[256,256]{1,0:T(8,128)(2,1)S(1)} %get-tuple-element.43), channel_id=1, source_target_pairs={{0,16},{16,32},{32,48},{48,0},{1,17},{17,33},{33,49},{49,1},{2,18}... | collective-permute-start | bytes 393224 | tf_op jit(solution)/shard_map/ppermute | solution.py:370
  79.5 7.1 %collective-permute-start.4 = (bf16[256,256]{1,0:T(8,128)(2,1)S(1)}, bf16[256,256]{1,0:T(8,128)(2,1)S(1)}, u32[]{:S(2)}, u32[]{:S(2)}) collective-permute-start(bf16[256,256]{1,0:T(8,128)(2,1)S(1)} %get-tuple-element.44), channel_id=1, source_target_pairs={{0,48},{16,0},{32,16},{48,32},{1,49},{17,1},{33,17},{49,33},{2,50}... | collective-permute-start | bytes 393224 | tf_op jit(solution)/shard_map/ppermute | solution.py:370
  86.6 17.1 %copy-start.3 = (bf16[1,256,256]{2,1,0:T(8,128)(2,1)S(1)}, bf16[1,256,256]{2,1,0:T(8,128)(2,1)}, u32[]{:S(2)}) copy-start(bf16[1,256,256]{2,1,0:T(8,128)(2,1)} %param.9) | copy-start | bytes 393220
  86.7 17.1 %copy-start.4 = (s32[1,256]{1,0:T(1,128)S(1)}, s32[1,256]{1,0:T(1,128)}, u32[]{:S(2)}) copy-start(s32[1,256]{1,0:T(1,128)} %refs_5_.1) | copy-start | bytes 3076
  97.0 8.7 %collective-permute-start.5 = (bf16[4,272,256]{2,1,0:T(8,128)(2,1)S(1)}, bf16[4,272,256]{2,1,0:T(8,128)(2,1)S(1)}, u32[]{:S(2)}, u32[]{:S(2)}) collective-permute-start(bf16[4,272,256]{2,1,0:T(8,128)(2,1)S(1)} %all_to_all.27.got), channel_id=1, source_target_pairs={{0,8},{8,0},{1,9},{9,1},{2,10},{10,2},{3,11},{11,3},{4,12},{12,4},... | collective-permute-start | bytes 1671176 | tf_op jit(solution)/shard_map/ppermute | solution.py:305
